TPU v7x, 32 devices: a whole 2x2x4 slice. The times are simulated.
32 devices in a mesh: groups: 2 (over y), tensor: 4 (over z), store: 4 (over x, core).
Axes of the slice: x: 2, y: 2, z: 4, core: 2. Of those that a mesh axis runs over, the one named last changes fastest.
Arguments:
- tokens: bfloat16 [4096, 8192], P(('groups', 'store', 'tensor')), parts along dimension 0, may hold values from -32 to 32
- query_weight: bfloat16 [8192, 8192], P(None, 'tensor'), may hold values from -0.0625 to 0.0625
- key_value_weight: bfloat16 [8192, 2048], P(None, 'tensor'), may hold values from -0.0625 to 0.0625
- adapter_down_maps: bfloat16 [32, 128, 8192], P('store', None, 'tensor'), may hold values from -0.0625 to 0.0625
- adapter_up_query: bfloat16 [32, 64, 8192], P('store', None, 'tensor'), may hold values from -0.375 to 0.375
- adapter_up_key_value: bfloat16 [32, 64, 2048], P('store', None, 'tensor'), may hold values from -0.375 to 0.375
- adapter_row_table: int32 [64], P('groups'), parts along dimension 0, may hold values from 0 to 31, as said below
- request_adapter_ids: int32 [8, 4], P('groups'), parts along dimension 0, may hold values from 0 to 31, as said below
- token_request_ids: int32 [8, 512], P(('groups', 'store')), parts along dimension 0, may hold values from 0 to 3, never falling along the last dimension, each value on 1 to 256 neighbouring positions
Outputs:
- attention: bfloat16 [4096, 8192], P(('groups', 'store'), 'tensor'), parts along dimension 0
There are 2 independent parts, one for each index of `groups`. A program takes and returns all parts, laid end to end along the dimension named above; an argument that names none is the same for every part. Nothing has to cross between parts.
Inputs may be any that keep to these rules, and one draw needn't show every extreme that they name: A permutation: adapter a lies in row adapter_row_table[a] of the adapter arrays, on store index adapter_row_table[a] // 8. `request_adapter_ids`: the 4 requests of one store batch use adapters held on 4 different store indices. `token_request_ids`: requests are contiguous runs of a store batch, each of 1 to 256 tokens.
All inputs are finite; a program needn't handle non-finite values.
Results may differ from a plain program's by a relative error of at most 0.012.
The roundings to bfloat16 on the way count: a program that leaves them out, or rounds other values in their place, can miss the bound.
Values may be sent and summed in bfloat16 or wider, within the bound.
No kernel may reach another device: no remote copies, remote signals or barrier semaphores. Data moves between devices by JAX's collectives and lax.ppermute only.
A program may use at most 128 MiB of HBM per device.

v0:
```python
import math

import jax
import jax.numpy as jnp
from jax import lax
from jax.sharding import PartitionSpec as P

MODEL_WIDTH = 8192
QUERY_HEADS = 64
KEY_VALUE_HEADS = 8
HEAD_SIZE = 128
ADAPTER_RANK = 64
STORE_REQUESTS = 4
TOK_ST = 512


adapter_scale = 2.0
rope_theta = 500000.0


def from_partner(shard, axis, bit):
    return lax.ppermute(shard, axis, [(i, i ^ 1 << bit) for i in range(lax.axis_size(axis))])


def token_positions(segment_row):
    members = segment_row[:, None] == jnp.arange(STORE_REQUESTS, dtype=jnp.int32)[None, :]
    counts = jnp.sum(members.astype(jnp.int32), axis=0)
    starts = jnp.cumsum(counts) - counts
    first_index = jnp.sum(jnp.where(members, starts[None, :], 0), axis=1)
    return jnp.arange(segment_row.shape[0], dtype=jnp.int32) - first_index


def rotary(heads_values, positions):
    half_size = heads_values.shape[-1] // 2
    exponent = jnp.arange(half_size, dtype=jnp.float32) * (2.0 / heads_values.shape[-1])
    frequency = jnp.exp(-exponent * math.log(rope_theta))
    angles = positions.astype(jnp.float32)[:, None] * frequency[None, :]
    cosine = jnp.cos(angles)[:, None, :]
    sine = jnp.sin(angles)[:, None, :]
    lower = heads_values[..., :half_size]
    upper = heads_values[..., half_size:]
    return jnp.concatenate([lower * cosine - upper * sine, upper * cosine + lower * sine], axis=-1)


def select_rows(selector, stack):
    flat = stack.reshape(stack.shape[0], -1)
    picked = jnp.dot(selector, flat, preferred_element_type=jnp.float32)
    return picked.reshape(selector.shape[:-1] + stack.shape[1:])


def on_device(
    tokens,
    query_weight,
    key_value_weight,
    adapter_down_maps,
    adapter_up_query,
    adapter_up_key_value,
    adapter_row_table,
    request_adapter_ids,
    token_request_ids,
):
    tensor_rank = lax.axis_index("tensor")
    store_rank = lax.axis_index("store")
    tensor_count = lax.axis_size("tensor")
    store_count = lax.axis_size("store")
    position_count = adapter_down_maps.shape[0]
    adapter_total = adapter_row_table.shape[0]
    lookup = (
        request_adapter_ids[:, :, None] == jnp.arange(adapter_total, dtype=jnp.int32)[None, None, :]
    ).astype(jnp.int32)
    slot_table = jnp.sum(lookup * adapter_row_table[None, None, :], axis=2)
    my_slots = lax.dynamic_index_in_dim(slot_table, store_rank, 0, keepdims=False)
    local_slots = store_rank * position_count + jnp.arange(position_count, dtype=jnp.int32)
    serving = jnp.sum(
        (slot_table[:, :, None] == local_slots[None, None, :]).astype(jnp.int32), axis=1
    ).astype(jnp.bfloat16)
    out_down = select_rows(serving, adapter_down_maps).astype(jnp.bfloat16)
    out_query = select_rows(serving, adapter_up_query).astype(jnp.bfloat16)
    out_keyval = select_rows(serving, adapter_up_key_value).astype(jnp.bfloat16)
    got_down, got_query, got_keyval = (
        lax.all_to_all(out_down, "store", split_axis=0, concat_axis=0, tiled=True),
        lax.all_to_all(out_query, "store", split_axis=0, concat_axis=0, tiled=True),
        lax.all_to_all(out_keyval, "store", split_axis=0, concat_axis=0, tiled=True),
    )
    holder_pick = (
        (my_slots // position_count)[:, None] == jnp.arange(store_count, dtype=jnp.int32)[None, :]
    ).astype(jnp.bfloat16)
    down_blocks = select_rows(holder_pick, got_down).astype(jnp.bfloat16)
    up_query_blocks = select_rows(holder_pick, got_query).astype(jnp.bfloat16)
    up_keyval_blocks = select_rows(holder_pick, got_keyval).astype(jnp.bfloat16)
    segment_row = token_request_ids[0]
    members = segment_row[:, None] == jnp.arange(STORE_REQUESTS, dtype=jnp.int32)[None, :]
    member_float = members.astype(jnp.float32)
    member_half = members.astype(jnp.bfloat16)
    width_share = MODEL_WIDTH // tensor_count
    column_first = tensor_rank * width_share
    down_matrix = down_blocks.reshape(STORE_REQUESTS * 2 * ADAPTER_RANK, width_share)
    query_width = query_weight.shape[1]
    keyval_width = key_value_weight.shape[1]
    rows_piece = lax.all_gather(tokens, "tensor", axis=0, tiled=True)
    count = rows_piece.shape[0]
    plain_query = jnp.dot(rows_piece, query_weight, preferred_element_type=jnp.float32)
    plain_key_value = jnp.dot(rows_piece, key_value_weight, preferred_element_type=jnp.float32)
    features = lax.dynamic_slice_in_dim(rows_piece, column_first, width_share, 1)
    partial_low = lax.dot_general(
        features, down_matrix, (((1,), (1,)), ((), ())), preferred_element_type=jnp.float32
    )
    partial_low = jnp.sum(
        partial_low.reshape(count, STORE_REQUESTS, 2 * ADAPTER_RANK) * member_float[:, :, None],
        axis=1,
    )
    joined = jnp.concatenate([plain_query, plain_key_value, partial_low], axis=1)
    plain_query = joined[:, :query_width]
    plain_key_value = joined[:, query_width : query_width + keyval_width]
    low = lax.psum(joined[:, query_width + keyval_width :], "tensor").astype(jnp.bfloat16)
    token_query_update = (low[:, None, :ADAPTER_RANK] * member_half[:, :, None]).reshape(
        TOK_ST, STORE_REQUESTS * ADAPTER_RANK
    )
    token_key_value_update = (low[:, None, ADAPTER_RANK:] * member_half[:, :, None]).reshape(
        TOK_ST, STORE_REQUESTS * ADAPTER_RANK
    )
    query_update = jnp.dot(
        token_query_update,
        up_query_blocks.reshape(STORE_REQUESTS * ADAPTER_RANK, query_width),
        preferred_element_type=jnp.float32,
    )
    key_value_update = jnp.dot(
        token_key_value_update,
        up_keyval_blocks.reshape(STORE_REQUESTS * ADAPTER_RANK, keyval_width),
        preferred_element_type=jnp.float32,
    )
    query_unrotated = plain_query + adapter_scale * query_update
    key_value_unrotated = plain_key_value + adapter_scale * key_value_update
    positions = token_positions(segment_row)
    head_local = query_width // HEAD_SIZE
    query = rotary(query_unrotated.reshape(TOK_ST, head_local, HEAD_SIZE), positions).astype(
        jnp.bfloat16
    )
    pair_heads = keyval_width // HEAD_SIZE
    keyval_heads = key_value_unrotated.reshape(TOK_ST, pair_heads, HEAD_SIZE)
    holds_keys = tensor_rank % 2 == 0
    own_part = jnp.where(holds_keys, rotary(keyval_heads, positions), keyval_heads).astype(
        jnp.bfloat16
    )
    other_part = from_partner(own_part, "tensor", 0)
    keys = jnp.where(holds_keys, own_part, other_part)
    values = jnp.where(holds_keys, other_part, own_part)
    group_size = QUERY_HEADS // KEY_VALUE_HEADS
    kv_used = max(head_local // group_size, 1)
    per_kv = head_local // kv_used
    kv_first = tensor_rank * head_local // group_size - tensor_rank // 2 * pair_heads
    keys_used = lax.dynamic_slice_in_dim(keys, kv_first, kv_used, 1)
    values_used = lax.dynamic_slice_in_dim(values, kv_first, kv_used, 1)
    grouped = query.reshape(TOK_ST, kv_used, per_kv, HEAD_SIZE)
    scores = jnp.einsum(
        "tkgd,skd->kgts", grouped, keys_used, preferred_element_type=jnp.float32
    ) / math.sqrt(HEAD_SIZE)
    token_index = jnp.arange(TOK_ST, dtype=jnp.int32)
    allowed = (segment_row[:, None] == segment_row[None, :]) & (
        token_index[:, None] >= token_index[None, :]
    )
    scores = jnp.where(allowed, scores, -1e30)
    scores = scores - jnp.max(scores, axis=-1, keepdims=True)
    weights = jnp.exp(scores)
    weights = (weights / jnp.sum(weights, axis=-1, keepdims=True)).astype(jnp.bfloat16)
    mixed = jnp.einsum("kgts,skd->tkgd", weights, values_used, preferred_element_type=jnp.float32)
    return mixed.reshape(TOK_ST, query_width).astype(jnp.bfloat16)


def solution(mesh):
    return jax.shard_map(
        on_device,
        mesh=mesh,
        in_specs=(
            P(("groups", "store", "tensor"), None),
            P(None, "tensor"),
            P(None, "tensor"),
            P("store", None, "tensor"),
            P("store", None, "tensor"),
            P("store", None, "tensor"),
            P("groups"),
            P("groups", None),
            P(("groups", "store"), None),
        ),
        out_specs=P(("groups", "store"), "tensor"),
        check_vma=False,
    )
```

profile of v0, /device:TPU:0, one launch (start us, length us, event | category | flops | bytes accessed | tf_op | source)
XLA Modules:
  0.0 270.5 jit_solution(15919129932199313101)
XLA Ops:
  6.5 0.0 copy-start
  6.5 0.0 all-gather.2.cloned.1.call-start
  6.5 0.7 all-gather.2.cloned.1.call-update
  7.3 0.9 select_reduce_fusion.1
  8.2 0.1 convert_reduce_fusion.1
  8.3 1.4 convolution_convert_fusion.4
  9.7 0.0 copy-start.4
  9.7 0.7 copy.34
  10.5 4.2 %all-to-all-start.1 = ((bf16[4,64,512]{2,1,0:T(8,128)(2,1)}), bf16[4,64,512]{2,1,0:T(8,128)(2,1)S(1)}, u32[]{:S(2)}, u32[]{:S(2)}) async-start(bf16[4,64,512]{2,1,0:T(8,128)(2,1)} %copy.34), calls=%async_computation.1 | async-start | bytes 524288 | tf_op jit(solution)/shard_map/all_to_all | solution.py:83
  14.7 0.0 copy-done
  14.7 1.6 convolution_convert_fusion.3
  16.3 1.6 copy.40
  18.0 2.8 %all-to-all-done.1 = bf16[4,64,512]{2,1,0:T(8,128)(2,1)S(1)} async-done(((bf16[4,64,512]{2,1,0:T(8,128)(2,1)}), bf16[4,64,512]{2,1,0:T(8,128)(2,1)S(1)}, u32[]{:S(2)}, u32[]{:S(2)}) %all-to-all-start.1) | async-done | bytes 262176 | tf_op jit(solution)/shard_map/all_to_all | solution.py:83
  20.7 3.5 %all-to-all-start.2 = ((bf16[4,64,2048]{2,1,0:T(8,128)(2,1)}), bf16[4,64,2048]{2,1,0:T(8,128)(2,1)S(1)}, u32[]{:S(2)}, u32[]{:S(2)}) async-start(bf16[4,64,2048]{2,1,0:T(8,128)(2,1)} %copy.40), calls=%async_computation.2 | async-start | bytes 2097152 | tf_op jit(solution)/shard_map/all_to_all | solution.py:82
  24.3 0.0 copy-done.4
  24.3 0.1 convert_reduce_fusion
  24.4 0.2 reduce-window.8
  24.6 5.4 %convolution_convert_fusion = bf16[4,128,2048]{2,0,1:T(4,128)(2,1)S(1)} fusion(s32[4,8]{1,0:T(4,128)S(1)} %convert_reduce_fusion.1, bf16[1,8,128,2048]{3,2,1,0:T(8,128)(2,1)} %bitcast.125), kind=kOutput, calls=%fused_computation.14 | convolution fusion | flops 17825824 | bytes 6291584 | tf_op jit(solution)/shard_map/dot_general | solution.py:47
  30.0 2.5 copy.31
  32.5 6.3 %all-to-all-done.2 = bf16[4,64,2048]{2,1,0:T(8,128)(2,1)S(1)} async-done(((bf16[4,64,2048]{2,1,0:T(8,128)(2,1)}), bf16[4,64,2048]{2,1,0:T(8,128)(2,1)S(1)}, u32[]{:S(2)}, u32[]{:S(2)}) %all-to-all-start.2) | async-done | bytes 1048608 | tf_op jit(solution)/shard_map/all_to_all | solution.py:82
  38.7 0.0 copy-start.2
  38.7 1.0 copy-done.2
  39.7 3.8 %all-to-all-start = ((bf16[4,128,2048]{2,1,0:T(8,128)(2,1)}), bf16[4,128,2048]{2,1,0:T(8,128)(2,1)S(1)}, u32[]{:S(2)}, u32[]{:S(2)}) async-start(bf16[4,128,2048]{2,1,0:T(8,128)(2,1)} %copy.31), calls=%async_computation | async-start | bytes 4194304 | tf_op jit(solution)/shard_map/all_to_all | solution.py:81
  43.6 0.1 select_reduce_fusion
  43.7 0.2 fusion.31
  43.9 1.0 multiply_cosine_fusion
  44.9 0.4 convolution_convert_fusion.5
  45.2 3.3 %convolution_convert_fusion.2 = bf16[4,64,2048]{2,0,1:T(4,128)(2,1)} fusion(s32[4]{0:T(128)S(1)} %and_select_fusion, bf16[1,4,64,2048]{3,2,1,0:T(8,128)(2,1)} %bitcast.129), kind=kOutput, calls=%fused_computation.16 | convolution fusion | flops 4718608 | bytes 2097168 | tf_op jit(solution)/shard_map/dot_general | solution.py:47
  48.5 20.5 %all-to-all-done = bf16[4,128,2048]{2,1,0:T(8,128)(2,1)S(1)} async-done(((bf16[4,128,2048]{2,1,0:T(8,128)(2,1)}), bf16[4,128,2048]{2,1,0:T(8,128)(2,1)S(1)}, u32[]{:S(2)}, u32[]{:S(2)}) %all-to-all-start) | async-done | bytes 2097184 | tf_op jit(solution)/shard_map/all_to_all | solution.py:81
  69.0 3.1 %convolution_convert_fusion.1 = bf16[4,128,2048]{2,0,1:T(4,128)(2,1)} fusion(s32[4]{0:T(128)S(1)} %and_select_fusion, bf16[1,4,128,2048]{3,2,1,0:T(8,128)(2,1)S(1)} %bitcast.127), kind=kOutput, calls=%fused_computation.15 | convolution fusion | flops 9437200 | bytes 4194320 | tf_op jit(solution)/shard_map/dot_general | solution.py:47
  72.1 89.2 %all-gather.2.cloned.1.call-done = bf16[512,8192]{1,0:T(8,128)(2,1)} async-done(((bf16[128,8192]{1,0:T(8,128)(2,1)}), bf16[512,8192]{1,0:T(8,128)(2,1)}) %all-gather.2.cloned.1.call-update) | async-done | bytes 8388624 | tf_op jit(solution)/shard_map/all_gather | solution.py:100
  161.3 4.9 %fusion.24 = f32[512,128]{1,0:T(8,128)S(1)} fusion(bf16[4,128,2048]{2,0,1:T(4,128)(2,1)} %convolution_convert_fusion.1, bf16[512,8192]{1,0:T(8,128)(2,1)} %all-gather.2.cloned.1.call-done, s32[]{:T(128)S(6)} %select_n.62, f32[512,4]{0,1:T(4,128)S(1)} %get-tuple-element.14), kind=kOutput, calls=%fused_computation.31 | convolution fusion | flops 1074200576 | bytes 4464644 | tf_op jit(solution)/shard_map/dot_general | solution.py:105
  166.2 21.5 %all-reduce.1 = bf16[512,128]{1,0:T(8,128)(2,1)S(1)} all-reduce(f32[512,128]{1,0:T(8,128)S(1)} %fusion.24), channel_id=1, replica_groups=mesh['groups'=2,'tensor'=4,'store'=4] {'tensor'}, use_global_device_ids=true, to_apply=%region_3.4 | all-reduce | flops 65536 | bytes 393216 | tf_op jit(solution)/shard_map/psum | solution.py:115
  187.7 0.1 fusion.68
  187.8 0.1 copy.33
  187.9 9.5 %fusion.82 = f32[512,512]{0,1:T(8,128)S(1)} fusion(bf16[512,8192]{1,0:T(8,128)(2,1)} %all-gather.2.cloned.1.call-done, bf16[8192,512]{1,0:T(8,128)(2,1)} %param.11), kind=kOutput, calls=%fused_computation.106 | convolution fusion | flops 4294967296 | bytes 17825792 | tf_op jit(solution)/shard_map/dot_general | solution.py:103
  197.4 0.3 fusion.23
  197.7 0.3 copy.36
  198.1 0.1 copy.39
  198.2 0.4 multiply_subtract_fusion
  198.6 0.3 fusion.29
  199.0 0.0 copy-start.1
  199.0 0.1 collective-permute-start
  199.0 23.8 %fusion.83 = f32[512,2048]{1,0:T(8,128)S(1)} fusion(bf16[512,8192]{1,0:T(8,128)(2,1)} %all-gather.2.cloned.1.call-done, bf16[8192,2048]{1,0:T(8,128)(2,1)} %param.10), kind=kOutput, calls=%fused_computation.107 | convolution fusion | flops 17179869184 | bytes 46137344 | tf_op jit(solution)/shard_map/dot_general | solution.py:102
  222.9 0.0 copy-done.1
  222.9 1.7 fusion.7
  224.7 0.9 copy.58
  225.6 1.8 subtract_convert_fusion
  227.4 0.5 copy.42
  228.0 0.5 copy.43
  228.5 0.0 collective-permute-done
  228.5 0.0 copy-start.3
  228.6 8.2 %fusion.8 = f32[2,512,512,8]{2,1,3,0:T(8,128)} fusion(bf16[512,2,8,64]{3,0,2,1:T(8,128)(2,1)S(1)} %bitcast.123, bf16[512,2,8,64]{3,0,2,1:T(8,128)(2,1)S(1)} %bitcast.122, pred[]{:T(512)S(6)} %eq.43, bf16[512,4,128]{2,0,1:T(8,128)(2,1)S(1)} %fusion.29, s32[]{:T(128)S(6)} %select_n.70, bf16[512,4,128]{2,0,1:T(8,128)(2,1)S(1)} %collective-permute-done), kind=kOutput, calls=%fused_computation.18 | convolution fusion | flops 1078067200 | bytes 21495812 | tf_op jit(solution)/shard_map/tkgd,skd->kgts/dot_general | solution.py:155
  236.7 0.0 copy-done.3
  236.7 17.2 %fusion.69 = (f32[2,8,512]{2,1,0:T(8,128)S(1)}, f32[2,8,512,512]{2,3,1,0:T(8,128)}) fusion(f32[2,512,512,8]{2,1,3,0:T(8,128)} %fusion.8, pred[512,512]{0,1:T(8,128)(4,1)S(1)} %fusion.31), kind=kOutput, calls=%fused_computation.93 | output fusion | flops 25166336 | bytes 33849344 | tf_op jit(solution)/shard_map/sub | solution.py:163
  253.9 7.3 %fusion.16 = bf16[2,128,8,512]{3,1,2,0:T(8,128)(2,1)S(1)} fusion(f32[2,8,512,512]{2,3,1,0:T(8,128)} %get-tuple-element.16, f32[2,8,512]{2,1,0:T(8,128)S(1)} %get-tuple-element.15, pred[]{:T(512)S(6)} %eq.43, bf16[512,4,128]{2,0,1:T(8,128)(2,1)S(1)} %fusion.29, s32[]{:T(128)S(6)} %select_n.70, bf16[512,4,128]{2,0,1:T(8,128)(2,1)} %copy-done.3), kind=kOutput, calls=%fused_computation.26 | convolution fusion | flops 1083310080 | bytes 19431428 | tf_op jit(solution)/shard_map/kgts,skd->tkgd/dot_general | solution.py:166
  261.3 2.4 copy.46
  (6 shorter events, 0.0 us)
Async XLA Ops:
  6.5 8.2 %copy-start = (bf16[8,64,2048]{2,1,0:T(8,128)(2,1)S(1)}, bf16[8,64,2048]{2,1,0:T(8,128)(2,1)}, u32[]{:S(2)}) copy-start(bf16[8,64,2048]{2,1,0:T(8,128)(2,1)} %param.13) | copy-start | bytes 6291460
  6.5 154.8 %all-gather.2.cloned.1.call-start = ((), (), s32[]{:S(2)}) async-start(), calls=%async_computation.3 | async-start | bytes 10485760 | tf_op jit(solution)/shard_map/all_gather | solution.py:100
  9.7 14.6 %copy-start.4 = (s32[1,512]{1,0:T(1,128)S(1)}, s32[1,512]{1,0:T(1,128)}, u32[]{:S(2)}) copy-start(s32[1,512]{1,0:T(1,128)} %param.17) | copy-start | bytes 6148
  10.5 10.2 %all-to-all-start.1 = ((bf16[4,64,512]{2,1,0:T(8,128)(2,1)}), bf16[4,64,512]{2,1,0:T(8,128)(2,1)S(1)}, u32[]{:S(2)}, u32[]{:S(2)}) async-start(bf16[4,64,512]{2,1,0:T(8,128)(2,1)} %copy.34), calls=%async_computation.1 | async-start | bytes 524288 | tf_op jit(solution)/shard_map/all_to_all | solution.py:83
  20.7 18.0 %all-to-all-start.2 = ((bf16[4,64,2048]{2,1,0:T(8,128)(2,1)}), bf16[4,64,2048]{2,1,0:T(8,128)(2,1)S(1)}, u32[]{:S(2)}, u32[]{:S(2)}) async-start(bf16[4,64,2048]{2,1,0:T(8,128)(2,1)} %copy.40), calls=%async_computation.2 | async-start | bytes 2097152 | tf_op jit(solution)/shard_map/all_to_all | solution.py:82
  38.7 1.0 copy-start.2
  39.7 29.3 %all-to-all-start = ((bf16[4,128,2048]{2,1,0:T(8,128)(2,1)}), bf16[4,128,2048]{2,1,0:T(8,128)(2,1)S(1)}, u32[]{:S(2)}, u32[]{:S(2)}) async-start(bf16[4,128,2048]{2,1,0:T(8,128)(2,1)} %copy.31), calls=%async_computation | async-start | bytes 4194304 | tf_op jit(solution)/shard_map/all_to_all | solution.py:81
  199.0 23.9 %copy-start.1 = (bf16[4,64,2048]{2,0,1:T(4,128)(2,1)S(1)}, bf16[4,64,2048]{2,0,1:T(4,128)(2,1)}, u32[]{:S(2)}) copy-start(bf16[4,64,2048]{2,0,1:T(4,128)(2,1)} %convolution_convert_fusion.2) | copy-start | bytes 3145732
  199.0 29.6 %collective-permute-start = (bf16[512,4,128]{2,0,1:T(8,128)(2,1)S(1)}, bf16[512,4,128]{2,0,1:T(8,128)(2,1)S(1)}, u32[]{:S(2)}, u32[]{:S(2)}) collective-permute-start(bf16[512,4,128]{2,0,1:T(8,128)(2,1)S(1)} %fusion.29), channel_id=1, source_target_pairs={{0,4},{4,0},{8,12},{12,8},{1,5},{5,1},{9,13},{13,9},{2,6},{6,2},{1... | collective-permute-start | bytes 1572872 | tf_op jit(solution)/shard_map/ppermute | solution.py:22
  228.5 8.2 %copy-start.3 = (bf16[512,4,128]{2,0,1:T(8,128)(2,1)}, bf16[512,4,128]{2,0,1:T(8,128)(2,1)S(1)}, u32[]{:S(2)}) copy-start(bf16[512,4,128]{2,0,1:T(8,128)(2,1)S(1)} %collective-permute-done) | copy-start | bytes 1572868
Sparse Core Ops, SparseCore 0:
  8.9 152.3 all-gather.1
where the time goes:
time: 271 us
  waiting for transfers between devices  119 us (44%)
  matrix products  70.9 us (26%)
  other arithmetic  22.4 us (8%)
  blocking collectives  21.5 us (8%)
  between operations  13.7 us (5%)
  starting transfers between devices  11.6 us (4%)
  local copies, waits for them, and re-layouts  10.9 us (4%)
    all_gather x1, waiting for transfers between devices, on_device(): rows_piece = lax.all_gather(tokens, 'tensor', axis=0, tiled=True)  89.2 us
    dot_general x1, matrix products, on_device(): jnp.dot(rows_piece, query_weight, preferred_element_type=jnp.float32)  23.8 us
    psum x1, blocking collectives, on_device(): lax.psum(joined[:, query_width + keyval_width:], 'tensor')  21.5 us
    all_to_all x1, waiting for transfers between devices, on_device(): lax.all_to_all(out_down, 'store', split_axis=0, concat_axis=0, tiled=True)  20.5 us
    sub x1, other arithmetic, on_device(): scores = scores - jnp.max(scores, axis=-1, keepdims=True)  17.2 us
    dot_general x6, matrix products, select_rows(): picked = jnp.dot(selector, flat, preferred_element_type=jnp.float32)  15.1 us
    dot_general x1, matrix products, on_device(): jnp.dot(rows_piece, key_value_weight, preferred_element_type=jnp.float32)  9.46 us
    dot_general x1, matrix products, on_device(): jnp.einsum('tkgd,skd->kgts', grouped, keys_used, preferred_element_type=j...  8.15 us
  transfers between devices with their start and end apart: 5, of which 4 were waited for; matrix products, arithmetic and copies ran while one was open for 19% of the time, Pallas kernels for 0%

commit v1 on v0

v1 whole, which is shorter than its diff:
```python
import functools
import math

import jax
import jax.numpy as jnp
from jax import lax
from jax.experimental import pallas as pl
from jax.experimental.pallas import tpu as pltpu
from jax.sharding import PartitionSpec as P

QUERY_HEADS = 64
KEY_VALUE_HEADS = 8
HEAD_SIZE = 128
ADAPTER_RANK = 64
STORE_REQUESTS = 4
LONGEST_REQUEST = 256

adapter_scale = 2.0
rope_theta = 500000.0

CHUNKS = 4
TILE = 128
VMEM_LIMIT = 40 * 2**20
F32 = jnp.float32
BF16 = jnp.bfloat16
ANY = pl.BlockSpec(memory_space=pl.ANY)


def params():
    return pltpu.CompilerParams(vmem_limit_bytes=VMEM_LIMIT)


def whole(shape):
    return pl.BlockSpec(shape, lambda *_: (0,) * len(shape))


def start_picked(candidates, pick, target, semaphore, columns=None):
    def start(source):
        view = source if columns is None else source.at[:, columns]
        pltpu.make_async_copy(view, target, semaphore).start()

    if len(candidates) == 1:
        start(candidates[0])
        return
    for index, source in enumerate(candidates):
        pl.when(pick == index)(functools.partial(start, source))


def project(candidates, picks, chunk_ids, weights, starts=None):
    steps, groups = len(candidates), len(candidates[0])
    rows, chunk = candidates[0][0][0].shape
    block = min(1024, chunk)
    sub = chunk // block
    flat = [x for at_chunk in candidates for group in at_chunk for x in group]
    widths = [w.shape[1] for w in weights]
    count = len(weights)

    def kernel(info, *refs):
        tokens_in = iter(refs[: len(flat)])
        sources = [[[next(tokens_in) for _ in group] for group in at_chunk] for at_chunk in candidates]
        rest = refs[len(flat) :]
        weight_refs, rest = rest[:count], rest[count:]
        start_refs = ()
        if starts is not None:
            start_refs, rest = rest[:count], rest[count:]
        out_refs, (held, sems) = rest[:count], rest[count:]
        step = pl.program_id(0)
        at = step // sub

        @pl.when(step == 0)
        def _():
            for a in range(steps):
                for r in range(groups):
                    start_picked(
                        sources[a][r], info[r], held.at[a, pl.ds(r * rows, rows), :], sems.at[a, r]
                    )

        @pl.when(step % sub == 0)
        def _():
            for r in range(groups):
                pltpu.make_async_copy(
                    sources[0][r][0], held.at[at, pl.ds(r * rows, rows), :], sems.at[at, r]
                ).wait()

        part = held[at, :, pl.ds(pl.multiple_of((step % sub) * block, block), block)]
        for i in range(count):
            product = jnp.dot(part, weight_refs[i][...], preferred_element_type=F32)

            @pl.when(step == 0)
            def _(i=i, product=product):
                out_refs[i][...] = product if starts is None else start_refs[i][...] + product

            @pl.when(step > 0)
            def _(i=i, product=product):
                out_refs[i][...] += product

    height = groups * rows
    info = jnp.concatenate([jnp.asarray(picks, jnp.int32), jnp.asarray(chunk_ids, jnp.int32)])
    results = pl.pallas_call(
        kernel,
        grid_spec=pltpu.PrefetchScalarGridSpec(
            num_scalar_prefetch=1,
            grid=(steps * sub,),
            in_specs=[ANY] * len(flat)
            + [
                pl.BlockSpec(
                    (block, w), lambda g, info: (info[groups + g // sub] * sub + g % sub, 0)
                )
                for w in widths
            ]
            + ([whole((height, w)) for w in widths] if starts is not None else []),
            out_specs=[whole((height, w)) for w in widths],
            scratch_shapes=[
                pltpu.VMEM((steps, height, chunk), BF16),
                pltpu.SemaphoreType.DMA((steps, groups)),
            ],
        ),
        out_shape=[jax.ShapeDtypeStruct((height, w), F32) for w in widths],
        compiler_params=params(),
        cost_estimate=pl.CostEstimate(
            flops=2 * height * steps * chunk * sum(widths),
            bytes_accessed=2 * steps * chunk * (sum(widths) + height),
            transcendentals=0,
        ),
    )(info, *flat, *weights, *(starts or []))
    return results


def low_parts(candidates, pick, offset, width, downs, member_groups):
    groups = len(candidates)
    rows = candidates[0][0].shape[0]
    flat = [x for group in candidates for x in group]
    holders = len(downs)
    rank = downs[0].shape[0]
    members = jnp.concatenate(member_groups, axis=0)

    def kernel(info, *refs):
        tokens_in = iter(refs[: len(flat)])
        sources = [[next(tokens_in) for _ in group] for group in candidates]
        down_refs = refs[len(flat) : len(flat) + holders]
        member_ref, out_ref, held, sems = refs[len(flat) + holders :]
        columns = pl.ds(pl.multiple_of(info[1], 128), width)
        for r in range(groups):
            start_picked(sources[r], info[0], held.at[pl.ds(r * rows, rows), :], sems.at[r], columns)
        for r in range(groups):
            pltpu.make_async_copy(
                sources[r][0].at[:, columns], held.at[pl.ds(r * rows, rows), :], sems.at[r]
            ).wait()
        total = None
        for d in range(holders):
            product = lax.dot_general(
                held[...], down_refs[d][...], (((1,), (1,)), ((), ())), preferred_element_type=F32
            )
            term = product * member_ref[:, d : d + 1]
            total = term if total is None else total + term
        out_ref[...] = total

    return pl.pallas_call(
        kernel,
        grid_spec=pltpu.PrefetchScalarGridSpec(
            num_scalar_prefetch=1,
            grid=(1,),
            in_specs=[ANY] * len(flat)
            + [whole(d.shape) for d in downs]
            + [whole(members.shape)],
            out_specs=whole((groups * rows, rank)),
            scratch_shapes=[
                pltpu.VMEM((groups * rows, width), BF16),
                pltpu.SemaphoreType.DMA((groups,)),
            ],
        ),
        out_shape=jax.ShapeDtypeStruct((groups * rows, rank), F32),
        compiler_params=params(),
        cost_estimate=pl.CostEstimate(
            flops=2 * groups * rows * width * rank * holders,
            bytes_accessed=2 * width * (groups * rows + rank * holders),
            transcendentals=0,
        ),
    )(jnp.stack([pick, offset]).astype(jnp.int32), *flat, *downs, members)


def spread(low, member):
    return jnp.concatenate([low * member[:, d : d + 1] for d in range(member.shape[1])], axis=1)


def rotate(block, cosine, sine):
    return block * cosine + pltpu.roll(block, HEAD_SIZE // 2, 1) * sine


def finish(sources, rank_index, low, members, up_query, up_keyval, tables, firsts, blocks):
    rows = low.shape[0] // blocks
    query_width = up_query.shape[1]
    keyval_width = up_keyval.shape[1]
    used = firsts[2] * HEAD_SIZE
    rank = ADAPTER_RANK
    count = len(sources)

    def kernel(info, *refs):
        sums = refs[: 2 * count]
        (low_ref, member_ref, upq_ref, upkv_ref, cos_ref, sin_ref, kcos_ref, ksin_ref) = refs[
            2 * count : 2 * count + 8
        ]
        query_ref, mine_ref, send_ref, held_q, held_kv, sems = refs[2 * count + 8 :]
        block = pl.program_id(0)
        z = info[0]
        for i, (_, _, first, test) in enumerate(sources):

            @pl.when(test(block, z))
            def _(i=i, first=first):
                a = pltpu.make_async_copy(sums[2 * i].at[pl.ds(first, rows), :], held_q, sems.at[0])
                b = pltpu.make_async_copy(
                    sums[2 * i + 1].at[pl.ds(first, rows), :], held_kv, sems.at[1]
                )
                a.start()
                b.start()
                a.wait()
                b.wait()

        member = member_ref[...].astype(BF16)
        low_block = low_ref[...]
        update = jnp.dot(
            spread(low_block[:, :rank], member), upq_ref[...], preferred_element_type=F32
        )
        for h in range(query_width // HEAD_SIZE):
            at = slice(h * HEAD_SIZE, (h + 1) * HEAD_SIZE)
            query_ref[:, at] = rotate(
                held_q[:, at] + adapter_scale * update[:, at], cos_ref[...], sin_ref[...]
            ).astype(BF16)
        update = jnp.dot(
            spread(low_block[:, rank:], member), upkv_ref[...], preferred_element_type=F32
        )
        for h in range(keyval_width // HEAD_SIZE):
            at = slice(h * HEAD_SIZE, (h + 1) * HEAD_SIZE)
            held_kv[:, at] = rotate(
                held_kv[:, at] + adapter_scale * update[:, at], kcos_ref[...], ksin_ref[...]
            )
        mine_ref[...] = held_kv[:, pl.ds(pl.multiple_of(info[1], HEAD_SIZE), used)].astype(BF16)
        send_ref[...] = held_kv[:, pl.ds(pl.multiple_of(info[2], HEAD_SIZE), used)].astype(BF16)

    def by_block(width):
        return pl.BlockSpec((rows, width), lambda b, info: (b, 0))

    flat = [x for q, kv, _, _ in sources for x in (q, kv)]
    total = rows * blocks
    info = jnp.stack([rank_index, firsts[0] * HEAD_SIZE, firsts[1] * HEAD_SIZE]).astype(jnp.int32)
    return pl.pallas_call(
        kernel,
        grid_spec=pltpu.PrefetchScalarGridSpec(
            num_scalar_prefetch=1,
            grid=(blocks,),
            in_specs=[ANY] * len(flat)
            + [
                by_block(low.shape[1]),
                by_block(members.shape[1]),
                whole(up_query.shape),
                whole(up_keyval.shape),
            ]
            + [by_block(HEAD_SIZE)] * 4,
            out_specs=[by_block(query_width), by_block(used), by_block(used)],
            scratch_shapes=[
                pltpu.VMEM((rows, query_width), F32),
                pltpu.VMEM((rows, keyval_width), F32),
                pltpu.SemaphoreType.DMA((2,)),
            ],
        ),
        out_shape=[
            jax.ShapeDtypeStruct((total, query_width), BF16),
            jax.ShapeDtypeStruct((total, used), BF16),
            jax.ShapeDtypeStruct((total, used), BF16),
        ],
        compiler_params=params(),
        cost_estimate=pl.CostEstimate(
            flops=2 * total * up_query.shape[0] * (query_width + keyval_width),
            bytes_accessed=8 * total * (query_width + keyval_width),
            transcendentals=0,
        ),
    )(info, *flat, low, members, up_query, up_keyval, *tables)


def finish_late(candidates, pick, chunk_id, weight, sums, low, member, up, cosine, sine, cuts=None):
    rows, chunk = candidates[0].shape
    width = weight.shape[1]
    step_width = min(512, width)
    steps = width // step_width
    count = len(candidates)

    def kernel(info, *refs):
        sources = refs[:count]
        weight_ref, sum_ref, low_ref, member_ref, up_ref, cos_ref, sin_ref = refs[count : count + 7]
        rest = refs[count + 7 :]
        outs, (held, sem) = rest[:-2], rest[-2:]

        @pl.when(pl.program_id(0) == 0)
        def _():
            start_picked(sources, info[0], held, sem.at[0])
            pltpu.make_async_copy(sources[0], held, sem.at[0]).wait()

        update = jnp.dot(
            spread(low_ref[...], member_ref[...].astype(BF16)),
            up_ref[...],
            preferred_element_type=F32,
        )
        raw = (
            jnp.dot(held[...], weight_ref[...], preferred_element_type=F32)
            + sum_ref[...]
            + adapter_scale * update
        )
        parts = [
            rotate(raw[:, h * HEAD_SIZE : (h + 1) * HEAD_SIZE], cos_ref[...], sin_ref[...])
            for h in range(step_width // HEAD_SIZE)
        ]
        if cuts is None:
            for h, part in enumerate(parts):
                outs[0][:, h * HEAD_SIZE : (h + 1) * HEAD_SIZE] = part.astype(BF16)
        else:
            for out, first in ((outs[0], info[2]), (outs[1], info[3])):
                for u in range(cuts[2]):
                    chosen = parts[0]
                    for h in range(1, len(parts)):
                        chosen = jnp.where(first + u == h, parts[h], chosen)
                    out[:, u * HEAD_SIZE : (u + 1) * HEAD_SIZE] = chosen.astype(BF16)

    def column(height):
        return pl.BlockSpec((height, step_width), lambda g, info: (0, g))

    if cuts is None:
        outs = [jax.ShapeDtypeStruct((rows, width), BF16)]
        out_specs = [column(rows)]
        info = [pick, chunk_id]
    else:
        used = cuts[2] * HEAD_SIZE
        outs = [jax.ShapeDtypeStruct((rows, used), BF16)] * 2
        out_specs = [whole((rows, used))] * 2
        info = [pick, chunk_id, cuts[0], cuts[1]]
    return pl.pallas_call(
        kernel,
        grid_spec=pltpu.PrefetchScalarGridSpec(
            num_scalar_prefetch=1,
            grid=(steps,),
            in_specs=[ANY] * count
            + [
                pl.BlockSpec((chunk, step_width), lambda g, info: (info[1], g)),
                column(rows),
                whole(low.shape),
                whole(member.shape),
                column(up.shape[0]),
                whole(cosine.shape),
                whole(sine.shape),
            ],
            out_specs=out_specs,
            scratch_shapes=[pltpu.VMEM((rows, chunk), BF16), pltpu.SemaphoreType.DMA((1,))],
        ),
        out_shape=outs,
        compiler_params=params(),
        cost_estimate=pl.CostEstimate(
            flops=2 * rows * width * (chunk + up.shape[0]),
            bytes_accessed=2 * width * chunk,
            transcendentals=0,
        ),
    )(jnp.stack(info).astype(jnp.int32), *candidates, weight, sums, low, member, up, cosine, sine)


def attend(query, query_late, mine, mine_late, recv, recv_late, ids_column, ids_row, info, blocks):
    total, width = query.shape
    rows = total // blocks
    heads = width // HEAD_SIZE
    used = mine.shape[1] // HEAD_SIZE
    per_kv = heads // used
    together = min(4, per_kv)
    span = together * HEAD_SIZE
    scale = math.log2(math.e) / math.sqrt(HEAD_SIZE)
    tiles = total // TILE
    back = -(-(LONGEST_REQUEST - 1) // TILE)

    def kernel(info, q_ref, ql_ref, m_ref, ml_ref, r_ref, rl_ref, idc_ref, idr_ref, out_ref, k_ref, v_ref):
        step = pl.program_id(0)

        @pl.when(step == 0)
        def _():
            def put(keys_mine):
                own, other = (k_ref, v_ref) if keys_mine else (v_ref, k_ref)
                own[...] = m_ref[...]
                other[...] = r_ref[...]

                @pl.when(info[0] >= 0)
                def _():
                    own[pl.ds(pl.multiple_of(info[0], rows), rows), :] = ml_ref[...]

                @pl.when(info[1] >= 0)
                def _():
                    other[pl.ds(pl.multiple_of(info[1], rows), rows), :] = rl_ref[...]

            pl.when(info[2] == 1)(lambda: put(True))
            pl.when(info[2] == 0)(lambda: put(False))

        @pl.when(info[0] >= 0)
        def _():
            q_ref[pl.ds(pl.multiple_of(info[0], rows), rows), :] = ql_ref[...]

        kv_at = pl.ds(pl.multiple_of((step * together // per_kv) * HEAD_SIZE, HEAD_SIZE), HEAD_SIZE)
        for tile in range(tiles):
            low_tile = max(0, tile - back)
            key_rows = (tile + 1 - low_tile) * TILE
            at = slice(tile * TILE, (tile + 1) * TILE)
            keys = k_ref[low_tile * TILE : low_tile * TILE + key_rows, kv_at]
            values = v_ref[low_tile * TILE : low_tile * TILE + key_rows, kv_at]
            row_index = lax.broadcasted_iota(jnp.int32, (TILE, key_rows), 0) + tile * TILE
            column_index = lax.broadcasted_iota(jnp.int32, (TILE, key_rows), 1) + low_tile * TILE
            allowed = (idc_ref[at, :] == idr_ref[:, low_tile * TILE : low_tile * TILE + key_rows]) & (
                row_index >= column_index
            )
            for h in range(together):
                query_part = q_ref[at, h * HEAD_SIZE : (h + 1) * HEAD_SIZE]
                scores = lax.dot_general(
                    query_part, keys, (((1,), (1,)), ((), ())), preferred_element_type=F32
                )
                scores = jnp.where(allowed, scores * scale, -1e30)
                top = jnp.max(scores, axis=1, keepdims=True)
                weights = jnp.exp2(scores - top)
                norm = jnp.sum(weights, axis=1, keepdims=True)
                mixed = jnp.dot(weights.astype(BF16), values, preferred_element_type=F32)
                out_ref[at, h * HEAD_SIZE : (h + 1) * HEAD_SIZE] = (mixed * (1.0 / norm)).astype(BF16)

    by_heads = pl.BlockSpec((total, span), lambda g, info: (0, g))
    return pl.pallas_call(
        kernel,
        grid_spec=pltpu.PrefetchScalarGridSpec(
            num_scalar_prefetch=1,
            grid=(heads // together,),
            in_specs=[
                by_heads,
                pl.BlockSpec((rows, span), lambda g, info: (0, g)),
                whole(mine.shape),
                whole(mine_late.shape),
                whole(recv.shape),
                whole(recv_late.shape),
                whole(ids_column.shape),
                whole(ids_row.shape),
            ],
            out_specs=by_heads,
            scratch_shapes=[pltpu.VMEM(mine.shape, BF16), pltpu.VMEM(mine.shape, BF16)],
        ),
        out_shape=jax.ShapeDtypeStruct((total, width), BF16),
        compiler_params=params(),
        cost_estimate=pl.CostEstimate(
            flops=4 * total * total * width,
            bytes_accessed=4 * total * width,
            transcendentals=total * total * heads,
        ),
    )(info, query, query_late, mine, mine_late, recv, recv_late, ids_column, ids_row)


def on_device(
    tokens,
    query_weight,
    key_value_weight,
    adapter_down_maps,
    adapter_up_query,
    adapter_up_key_value,
    adapter_row_table,
    request_adapter_ids,
    token_request_ids,
):
    z = lax.axis_index("tensor")
    store = lax.axis_index("store")
    n = lax.axis_size("tensor")
    stores = lax.axis_size("store")
    rows, model_width = tokens.shape
    total = rows * n
    half = n // 2
    late = n - 1
    chunks = CHUNKS
    chunk_width = model_width // chunks
    width_share = model_width // n
    slices = n // chunks
    home_chunk = z // slices
    home_offset = (z % slices) * width_share
    side = (z >= half).astype(jnp.int32)
    query_width = query_weight.shape[1]
    keyval_width = key_value_weight.shape[1]

    down = {(0, c): tokens[:, c * chunk_width : (c + 1) * chunk_width] for c in range(chunks)}
    up = dict(down)
    for k in range(1, n):
        for a in range(chunks):
            c = a
            down[k, c] = lax.ppermute(
                down[k - 1, c], "tensor", [(i, i - 1) for i in range(1, n - k + 1)]
            )
            c = chunks - 1 - a
            up[k, c] = lax.ppermute(up[k - 1, c], "tensor", [(i, i + 1) for i in range(k - 1, n - 1)])

    per_store = adapter_down_maps.shape[0]
    lookup = (
        request_adapter_ids[:, :, None]
        == jnp.arange(adapter_row_table.shape[0], dtype=jnp.int32)[None, None, :]
    ).astype(jnp.int32)
    slot_table = jnp.sum(lookup * adapter_row_table[None, None, :], axis=2)
    here = slot_table // per_store == store
    local = jnp.sum(jnp.where(here, slot_table - store * per_store, 0), axis=1)

    def exchanged(stack):
        got = []
        for d in range(stores):
            target = (store + d) % stores
            row = lax.dynamic_index_in_dim(local, target, 0, keepdims=False)
            part = lax.dynamic_index_in_dim(stack, row, 0, keepdims=False)
            got.append(
                part
                if d == 0
                else lax.ppermute(part, "store", [(i, (i + d) % stores) for i in range(stores)])
            )
        return got

    downs = exchanged(adapter_down_maps)
    up_query = jnp.concatenate(exchanged(adapter_up_query), axis=0)
    up_keyval = jnp.concatenate(exchanged(adapter_up_key_value), axis=0)

    segment_row = token_request_ids[0]
    my_holders = lax.dynamic_index_in_dim(slot_table, store, 0, keepdims=False) // per_store
    requests = jnp.arange(STORE_REQUESTS, dtype=jnp.int32)
    holder_order = (store - jnp.arange(stores, dtype=jnp.int32)) % stores
    served = jnp.max(
        jnp.where(my_holders[None, :] == holder_order[:, None], requests[None, :], -1), axis=1
    )
    members = (segment_row[:, None] == served[None, :]).astype(F32)
    starts = jnp.sum((segment_row[:, None] < requests[None, :]).astype(jnp.int32), axis=0)
    first_index = jnp.sum(
        jnp.where(segment_row[:, None] == requests[None, :], starts[None, :], 0), axis=1
    )
    positions = jnp.arange(total, dtype=jnp.int32) - first_index
    exponent = jnp.arange(HEAD_SIZE // 2, dtype=F32) * (2.0 / HEAD_SIZE)
    frequency = jnp.exp(-exponent * math.log(rope_theta))
    angles = positions.astype(F32)[:, None] * frequency[None, :]
    cosine, sine = jnp.cos(angles), jnp.sin(angles)
    cosine = jnp.concatenate([cosine, cosine], axis=1)
    sine = jnp.concatenate([-sine, sine], axis=1)
    holds_keys = z % 2 == 0
    key_cosine = jnp.where(holds_keys, cosine, 1.0)
    key_sine = jnp.where(holds_keys, sine, 0.0)

    def block_of(array, index):
        return lax.dynamic_slice_in_dim(array, jnp.clip(index, 0, n - 1) * rows, rows, 0)

    def every_chunk(way, k):
        return [way[k, c] for c in range(chunks)]

    parts = {}
    first = low_parts(
        [[tokens]], jnp.int32(0), z * width_share, width_share, downs, [block_of(members, z)]
    )
    low_sum = first
    for k in range(1, n):
        if k < half:
            both = low_parts(
                [every_chunk(down, k), every_chunk(up, k)],
                home_chunk,
                home_offset,
                width_share,
                downs,
                [block_of(members, z + k), block_of(members, z - k)],
            )
            low_sum = low_sum + lax.ppermute(
                both[:rows], "tensor", [(i, i + k) for i in range(n - k)]
            )
            low_sum = low_sum + lax.ppermute(
                both[rows:], "tensor", [(i, i - k) for i in range(k, n)]
            )
        else:
            one = low_parts(
                [
                    [down[k, c] for c in range(chunks // 2)]
                    + [up[k, c] for c in range(chunks // 2, chunks)]
                ],
                home_chunk,
                home_offset,
                width_share,
                downs,
                [block_of(members, jnp.where(side == 0, z + k, z - k))],
            )
            low_sum = low_sum + lax.ppermute(
                one,
                "tensor",
                [(i, i + k) for i in range(n - k)] + [(i, i - k) for i in range(k, n)],
            )
    low_own = low_sum.astype(BF16)
    low_turned = [low_own] + [
        lax.ppermute(low_own, "tensor", [((i + r) % n, i) for i in range(n)]) for r in range(1, n)
    ]
    low = lax.dynamic_slice_in_dim(
        jnp.concatenate(low_turned + low_turned, axis=0), (n - z) % n * rows, total, 0
    )

    weights = [query_weight, key_value_weight]
    sources = []
    own_q, own_kv = project(
        [[[down[0, c]]] for c in range(chunks)], [0], list(range(chunks)), weights
    )
    sources.append((own_q, own_kv, 0, lambda b, zz: b == zz))
    side_chunks = [jnp.where(side == 0, a, chunks - 1 - a) for a in range(chunks)]

    def sided(k, a):
        return [down[k, a], up[k, chunks - 1 - a]]

    for k in range(1, late):
        if k < half:
            q, kv = project(
                [[[down[k, c]], [up[k, c]]] for c in range(chunks)],
                [0, 0],
                list(range(chunks)),
                weights,
            )
            sources.append((q, kv, 0, lambda b, zz, k=k: b == zz + k))
            sources.append((q, kv, rows, lambda b, zz, k=k: b == zz - k))
        else:
            q, kv = project(
                [[sided(k, a)] for a in range(chunks)],
                jnp.stack([side]),
                jnp.stack(side_chunks),
                weights,
            )
            sources.append((q, kv, 0, lambda b, zz, k=k: (b == zz + k) | (b == zz - k)))
    late_q, late_kv = project(
        [[sided(late, a)] for a in range(chunks - 1)],
        jnp.stack([side]),
        jnp.stack(side_chunks[: chunks - 1]),
        weights,
    )

    group_size = QUERY_HEADS // KEY_VALUE_HEADS
    head_local = query_width // HEAD_SIZE
    pair_heads = keyval_width // HEAD_SIZE
    used = max(head_local // group_size, 1)

    def first_used(rank):
        return rank * head_local // group_size - rank // 2 * pair_heads

    partner = z ^ 1
    cuts = (first_used(z), first_used(partner), used)
    query, mine, send = finish(
        sources,
        z,
        low,
        members,
        up_query,
        up_keyval,
        (cosine, sine, key_cosine, key_sine),
        cuts,
        n,
    )
    recv = lax.ppermute(send, "tensor", [(i, i ^ 1) for i in range(n)])

    late_block = jnp.where(side == 0, n - 1, 0)
    late_args = dict(
        candidates=sided(late, chunks - 1), pick=side, chunk_id=side_chunks[chunks - 1]
    )
    late_low = block_of(low, late_block)
    late_member = block_of(members, late_block)
    mine_late, send_late = finish_late(
        **late_args,
        weight=key_value_weight,
        sums=late_kv,
        low=late_low[:, ADAPTER_RANK:],
        member=late_member,
        up=up_keyval,
        cosine=block_of(key_cosine, late_block),
        sine=block_of(key_sine, late_block),
        cuts=cuts,
    )
    recv_late = lax.ppermute(send_late, "tensor", [(0, 1), (n - 1, n - 2)])
    (query_late,) = finish_late(
        **late_args,
        weight=query_weight,
        sums=late_q,
        low=late_low[:, :ADAPTER_RANK],
        member=late_member,
        up=up_query,
        cosine=block_of(cosine, late_block),
        sine=block_of(sine, late_block),
    )
    nowhere = jnp.int32(-1)
    own_late = jnp.where(z == 0, (n - 1) * rows, jnp.where(z == n - 1, 0, nowhere))
    partner_late = jnp.where(partner == 0, (n - 1) * rows, jnp.where(partner == n - 1, 0, nowhere))
    info = jnp.stack([own_late, partner_late, holds_keys.astype(jnp.int32)]).astype(jnp.int32)
    return attend(
        query,
        query_late,
        mine,
        mine_late,
        recv,
        recv_late,
        segment_row[:, None],
        segment_row[None, :],
        info,
        n,
    )


def solution(mesh):
    return jax.shard_map(
        on_device,
        mesh=mesh,
        in_specs=(
            P(("groups", "store", "tensor"), None),
            P(None, "tensor"),
            P(None, "tensor"),
            P("store", None, "tensor"),
            P("store", None, "tensor"),
            P("store", None, "tensor"),
            P("groups"),
            P("groups", None),
            P(("groups", "store"), None),
        ),
        out_specs=P(("groups", "store"), "tensor"),
        check_vma=False,
    )
```

time: 271 us -> 288 us (1.063)
  Pallas kernels: 0 us -> 107 us
  matrix products: 70.9 us -> 0 us
  waiting for transfers between devices: 119 us -> 56.7 us
  starting transfers between devices: 11.6 us -> 73.7 us
  blocking collectives: 21.5 us -> 0 us
  local copies, waits for them, and re-layouts: 10.9 us -> 29.6 us
  other arithmetic: 22.4 us -> 10.4 us
  between operations: 13.7 us -> 9.15 us
    pallas_call x0 -> x12, Pallas kernels: none -> 107 us  [the longest x4 66.9 us: project(): pl.pallas_call(kernel, grid_spec=pltpu.PrefetchScalarGridSpec(num_scalar_...]
    all_gather x1 -> x0, waiting for transfers between devices: 89.2 us -> none  [on_device(): rows_piece = lax.all_gather(tokens, 'tensor', axis=0, tiled=True)]
    ppermute x1 -> x42, starting transfers between devices: 0.07 us -> 73.7 us  [the longest x12 25.8 us: on_device(): lax.ppermute(up[k - 1, c], 'tensor', [(i, i + 1) for i in range(k - 1, n...]
    dot_general x13 -> x0, matrix products: 70.9 us -> none  [the longest x1 23.8 us: on_device(): jnp.dot(rows_piece, query_weight, preferred_element_type=jnp.float32)]
    ppermute x1 -> x42, waiting for transfers between devices: 0.01 us -> 56.7 us  [the longest x12 26 us: on_device(): lax.ppermute(down[k - 1, c], 'tensor', [(i, i - 1) for i in range(1, n -...]
    all_to_all x3 -> x0, waiting for transfers between devices: 29.6 us -> none  [the longest x1 20.5 us: on_device(): lax.all_to_all(out_down, 'store', split_axis=0, concat_axis=0, tiled=True)]
    psum x1 -> x0, blocking collectives: 21.5 us -> none  [on_device(): lax.psum(joined[:, query_width + keyval_width:], 'tensor')]
    sub x3 -> x0, other arithmetic: 17.7 us -> none  [the longest x1 17.2 us: on_device(): scores = scores - jnp.max(scores, axis=-1, keepdims=True)]
  transfers between devices with their start and end apart: 5 -> 42, of which waited for: 4 -> 12; matrix products, arithmetic and copies ran while one was open for 19% -> 7% of each run, Pallas kernels for 0% -> 31%
where the time goes in v1:
time: 288 us; the launch traced here: 286 us
  Pallas kernels  107 us (37%)
  starting transfers between devices  73.7 us (26%)
  waiting for transfers between devices  56.7 us (20%)
  local copies, waits for them, and re-layouts  29.6 us (10%)
  other arithmetic  10.4 us (4%)
  between operations  9.15 us (3%)
    pallas_call x4, Pallas kernels, project(): pl.pallas_call(kernel, grid_spec=pltpu.PrefetchScalarGridSpec(num_scalar_...  66.9 us
    ppermute x12, waiting for transfers between devices, on_device(): lax.ppermute(down[k - 1, c], 'tensor', [(i, i - 1) for i in range(1, n -...  26 us
    ppermute x12, starting transfers between devices, on_device(): lax.ppermute(up[k - 1, c], 'tensor', [(i, i + 1) for i in range(k - 1, n...  25.8 us
    pallas_call x1, Pallas kernels, attend(): pl.pallas_call(kernel, grid_spec=pltpu.PrefetchScalarGridSpec(num_scalar_...  16.5 us
    unnamed x136, local copies, waits for them, and re-layouts  16.5 us
    ppermute x3, waiting for transfers between devices, on_device(): lax.ppermute(low_own, 'tensor', [((i + r) % n, i) for i in range(n)])  15.6 us
    ppermute x12, starting transfers between devices, on_device(): lax.ppermute(down[k - 1, c], 'tensor', [(i, i - 1) for i in range(1, n -...  15.4 us
    ppermute x2, starting transfers between devices, on_device(): lax.ppermute(one, 'tensor', [(i, i + k) for i in range(n - k)] + [(i, i -...  14.5 us
  transfers between devices with their start and end apart: 42, of which 12 were waited for; matrix products, arithmetic and copies ran while one was open for 7% of the time, Pallas kernels for 31%

profile of v1, /device:TPU:0, one launch (start us, length us, event | category | flops | bytes accessed | tf_op | source)
XLA Modules:
  0.0 286.2 jit_solution(6284669559849165113)
XLA Ops:
  9.6 1.7 dynamic-slice_bitcast_fusion.11
  11.8 2.5 collective-permute-start.34
  14.3 1.4 collective-permute-start.35
  15.7 2.7 dynamic-slice_bitcast_fusion
  19.0 1.4 fusion.8
  20.8 2.2 dynamic-slice_bitcast_fusion.7
  24.1 3.6 %copy-done = bf16[8192,512]{1,0:T(8,128)(2,1)S(1)} copy-done((bf16[8192,512]{1,0:T(8,128)(2,1)S(1)}, bf16[8192,512]{1,0:T(8,128)(2,1)}, u32[]{:S(2)}) %copy-start) | copy-done | bytes 8388632
  27.7 16.0 %shard_map.127 = (f32[128,2048]{1,0:T(8,128)S(1)}, f32[128,512]{1,0:T(8,128)S(1)}) custom-call(s32[5]{0:T(128)S(1)} %copy-done.55, bf16[128,2048]{1,0:T(8,128)(2,1)S(1)} %copy-done.19, bf16[128,2048]{1,0:T(8,128)(2,1)S(1)} %copy-done.18, bf16[128,2048]{1,0:T(8,128)(2,1)S(1)} %copy-done.17, bf16[128,2048]{1,0:T(8,128)(2,1)} %get-tuple-element.43.refs_3_, ...), custom_call_target="tpu_custom_call" | custom-call | flops 5368709120 | bytes 44040192 | tf_op jit(solution)/shard_map/pallas_call | solution.py:99
  45.4 1.1 broadcast_select_fusion
  46.5 1.3 collective-permute-start.30
  48.2 1.4 collective-permute-start.18
  49.6 1.5 constant_dynamic-slice_fusion.refs_7_
  51.0 2.4 collective-permute-done.30
  53.5 1.3 collective-permute-start
  54.8 2.6 collective-permute-done.31
  57.4 3.5 %collective-permute-start.1 = (bf16[128,2048]{1,0:T(8,128)(2,1)S(1)}, bf16[128,2048]{1,0:T(8,128)(2,1)S(1)}, u32[]{:S(2)}, u32[]{:S(2)}) collective-permute-start(bf16[128,2048]{1,0:T(8,128)(2,1)S(1)} %copy-done.19), channel_id=1, source_target_pairs={{0,4},{4,8},{8,12},{1,5},{5,9},{9,13},{2,6},{6,10},{10,14},{3,7},{... | collective-permute-start | bytes 1572872 | tf_op jit(solution)/shard_map/ppermute | solution.py:491
  61.7 1.3 collective-permute-start.2
  63.0 4.6 %collective-permute-start.3 = (bf16[128,2048]{1,0:T(8,128)(2,1)S(1)}, bf16[128,2048]{1,0:T(8,128)(2,1)S(1)}, u32[]{:S(2)}, u32[]{:S(2)}) collective-permute-start(bf16[128,2048]{1,0:T(8,128)(2,1)S(1)} %copy-done.18), channel_id=1, source_target_pairs={{0,4},{4,8},{8,12},{1,5},{5,9},{9,13},{2,6},{6,10},{10,14},{3,7},{... | collective-permute-start | bytes 1572872 | tf_op jit(solution)/shard_map/ppermute | solution.py:491
  68.2 1.3 collective-permute-start.4
  69.6 1.6 fusion.1
  71.3 5.4 %collective-permute-start.5 = (bf16[128,2048]{1,0:T(8,128)(2,1)S(1)}, bf16[128,2048]{1,0:T(8,128)(2,1)}, u32[]{:S(2)}, u32[]{:S(2)}) collective-permute-start(bf16[128,2048]{1,0:T(8,128)(2,1)S(1)} %copy-done.17), channel_id=1, source_target_pairs={{0,4},{4,8},{8,12},{1,5},{5,9},{9,13},{2,6},{6,10},{10,14},{3,7},{... | collective-permute-start | bytes 1572872 | tf_op jit(solution)/shard_map/ppermute | solution.py:491
  76.6 3.4 %collective-permute-start.7 = (bf16[128,2048]{1,0:T(8,128)(2,1)}, bf16[128,2048]{1,0:T(8,128)(2,1)}, u32[]{:S(2)}, u32[]{:S(2)}) collective-permute-start(bf16[128,2048]{1,0:T(8,128)(2,1)} %get-tuple-element.43.refs_3_), channel_id=1, source_target_pairs={{0,4},{4,8},{8,12},{1,5},{5,9},{9,13},{2,6},{6,10},{10,14},{3,7},{... | collective-permute-start | bytes 1572872 | tf_op jit(solution)/shard_map/ppermute | solution.py:491
  80.2 1.1 collective-permute-done.2.refs_2_.refs_1_
  81.3 1.3 collective-permute-start.10
  84.3 1.3 collective-permute-start.8
  86.3 6.4 %collective-permute-done.4.refs_4_.refs_2_ = bf16[128,2048]{1,0:T(8,128)(2,1)} collective-permute-done((bf16[128,2048]{1,0:T(8,128)(2,1)S(1)}, bf16[128,2048]{1,0:T(8,128)(2,1)}, u32[]{:S(2)}, u32[]{:S(2)}) %collective-permute-start.4) | collective-permute-done | bytes 524320 | tf_op jit(solution)/shard_map/ppermute | solution.py:487
  92.7 1.3 collective-permute-start.6
  94.8 1.5 collective-permute-start.11
  96.3 9.8 %collective-permute-done.7.refs_7_ = bf16[128,2048]{1,0:T(8,128)(2,1)} collective-permute-done((bf16[128,2048]{1,0:T(8,128)(2,1)}, bf16[128,2048]{1,0:T(8,128)(2,1)}, u32[]{:S(2)}, u32[]{:S(2)}) %collective-permute-start.7) | collective-permute-done | bytes 524320 | tf_op jit(solution)/shard_map/ppermute | solution.py:491
  106.1 1.5 collective-permute-start.9
  108.8 6.3 %collective-permute-done.8.refs_0_ = bf16[128,2048]{1,0:T(8,128)(2,1)} collective-permute-done((bf16[128,2048]{1,0:T(8,128)(2,1)S(1)}, bf16[128,2048]{1,0:T(8,128)(2,1)}, u32[]{:S(2)}, u32[]{:S(2)}) %collective-permute-start.8) | collective-permute-done | bytes 524320 | tf_op jit(solution)/shard_map/ppermute | solution.py:487
  115.1 1.3 collective-permute-start.22
  116.4 1.3 collective-permute-start.23
  119.3 7.1 %collective-permute-done.6.refs_6_.refs_3_ = bf16[128,2048]{1,0:T(8,128)(2,1)} collective-permute-done((bf16[128,2048]{1,0:T(8,128)(2,1)}, bf16[128,2048]{1,0:T(8,128)(2,1)}, u32[]{:S(2)}, u32[]{:S(2)}) %collective-permute-start.6) | collective-permute-done | bytes 524320 | tf_op jit(solution)/shard_map/ppermute | solution.py:487
  130.9 1.0 copy-done.27
  133.9 2.9 %shard_map.131 = f32[256,128]{1,0:T(8,128)S(1)} custom-call(s32[2]{0:T(128)S(1)} %pad_add_fusion.3.info, bf16[128,2048]{1,0:T(8,128)(2,1)S(1)} %copy-done.24, bf16[128,2048]{1,0:T(8,128)(2,1)S(1)} %copy-done.30, bf16[128,2048]{1,0:T(8,128)(2,1)} %collective-permute-done.4.refs_4_.refs_2_, bf16[128,2048]{1,0:T(8,128)(2,1)} %collective-permute-done.6.refs_6_.refs_3_, ...), custom_call_target="tpu_custom_call" | custom-call | flops 536870912 | bytes 3145728 | tf_op jit(solution)/shard_map/pallas_call | solution.py:158
  136.9 1.3 collective-permute-start.12
  139.0 4.5 %collective-permute-start.19 = (f32[128,128]{1,0:T(8,128)S(1)}, f32[128,128]{1,0:T(8,128)S(1)}, u32[]{:S(2)}, u32[]{:S(2)}) collective-permute-start(f32[128,128]{1,0:T(8,128)S(1)} %get-tuple-element.61), channel_id=1, source_target_pairs={{0,4},{4,8},{8,12},{1,5},{5,9},{9,13},{2,6},{6,10},{10,14},{3,7},{... | collective-permute-start | bytes 196616 | tf_op jit(solution)/shard_map/ppermute | solution.py:563
  143.6 5.2 %collective-permute-done.23.refs_1_.refs_2_ = bf16[128,2048]{1,0:T(8,128)(2,1)S(1)} collective-permute-done((bf16[128,2048]{1,0:T(8,128)(2,1)}, bf16[128,2048]{1,0:T(8,128)(2,1)S(1)}, u32[]{:S(2)}, u32[]{:S(2)}) %collective-permute-start.23) | collective-permute-done | bytes 524320 | tf_op jit(solution)/shard_map/ppermute | solution.py:487
  149.5 1.3 collective-permute-start.20
  150.8 1.1 pad_maximum_fusion.refs_10_.refs_6_
  152.0 3.6 %shard_map.132 = f32[128,128]{1,0:T(8,128)S(1)} custom-call(s32[2]{0:T(128)S(1)} %pad_add_fusion.3.info, bf16[128,2048]{1,0:T(8,128)(2,1)} %collective-permute-done.8.refs_0_, bf16[128,2048]{1,0:T(8,128)(2,1)} %collective-permute-done.10.refs_2_.refs_1_, bf16[128,2048]{1,0:T(8,128)(2,1)} %collective-permute-done.11.refs_3_.refs_2_, ...), custom_call_target="tpu_custom_call" | custom-call | flops 268435456 | bytes 2621440 | tf_op jit(solution)/shard_map/pallas_call | solution.py:158
  155.7 1.5 collective-permute-start.13
  157.2 1.3 collective-permute-start.14
  158.6 2.6 shard_map.133
  161.3 1.6 collective-permute-start.15
  162.9 8.9 %collective-permute-start.21 = (f32[128,128]{1,0:T(8,128)S(1)}, f32[128,128]{1,0:T(8,128)S(1)}, u32[]{:S(2)}, u32[]{:S(2)}) collective-permute-start(f32[128,128]{1,0:T(8,128)S(1)} %shard_map.132), channel_id=1, source_target_pairs={{0,8},{4,12},{8,0},{12,4},{1,9},{5,13},{9,1},{13,5},{2,10},{6,14},... | collective-permute-start | bytes 196616 | tf_op jit(solution)/shard_map/ppermute | solution.py:581
  171.8 5.6 %collective-permute-start.26 = (f32[128,128]{1,0:T(8,128)S(1)}, f32[128,128]{1,0:T(8,128)S(1)}, u32[]{:S(2)}, u32[]{:S(2)}) collective-permute-start(f32[128,128]{1,0:T(8,128)S(1)} %shard_map.133), channel_id=1, source_target_pairs={{0,12},{12,0},{1,13},{13,1},{2,14},{14,2},{3,15},{15,3},{16,28},{2... | collective-permute-start | bytes 196616 | tf_op jit(solution)/shard_map/ppermute | solution.py:581
  177.5 20.6 %shard_map.128 = (f32[256,2048]{1,0:T(8,128)S(1)}, f32[256,512]{1,0:T(8,128)S(1)}) custom-call(s32[6]{0:T(128)S(1)} %copy-done.52, bf16[128,2048]{1,0:T(8,128)(2,1)S(1)} %copy-done.25, bf16[128,2048]{1,0:T(8,128)(2,1)S(1)} %copy-done.22, bf16[128,2048]{1,0:T(8,128)(2,1)S(1)} %copy-done.31, bf16[128,2048]{1,0:T(8,128)(2,1)S(1)} %copy-done.28, ...), custom_call_target="tpu_custom_call" | custom-call | flops 10737418240 | bytes 46137344 | tf_op jit(solution)/shard_map/pallas_call | solution.py:99
  198.1 1.3 copy-done.5
  199.5 2.3 shard_map.130
  201.8 1.3 collective-permute-start.38
  203.9 1.3 collective-permute-start.36
  206.3 17.8 %shard_map.129 = (f32[128,2048]{1,0:T(8,128)S(1)}, f32[128,512]{1,0:T(8,128)S(1)}) custom-call(s32[5]{0:T(128)S(1)} %copy-done.51, bf16[128,2048]{1,0:T(8,128)(2,1)} %collective-permute-done.8.refs_0_, bf16[128,2048]{1,0:T(8,128)(2,1)} %collective-permute-done.9.refs_1_.refs_3_, bf16[128,2048]{1,0:T(8,128)(2,1)} %collective-permute-done.10.refs_2_.refs_1_, ...), custom_call_target="tpu_custom_call" | custom-call | flops 5368709120 | bytes 44040192 | tf_op jit(solution)/shard_map/pallas_call | solution.py:99
  224.2 5.1 %collective-permute-done.27 = bf16[128,128]{1,0:T(8,128)(2,1)S(1)} collective-permute-done((bf16[128,128]{1,0:T(8,128)(2,1)S(1)}, bf16[128,128]{1,0:T(8,128)(2,1)S(1)}, u32[]{:S(2)}, u32[]{:S(2)}) %collective-permute-start.27) | collective-permute-done | bytes 32800 | tf_op jit(solution)/shard_map/ppermute | solution.py:588
  229.3 4.8 %collective-permute-done.28 = bf16[128,128]{1,0:T(8,128)(2,1)S(1)} collective-permute-done((bf16[128,128]{1,0:T(8,128)(2,1)S(1)}, bf16[128,128]{1,0:T(8,128)(2,1)S(1)}, u32[]{:S(2)}, u32[]{:S(2)}) %collective-permute-start.28) | collective-permute-done | bytes 32800 | tf_op jit(solution)/shard_map/ppermute | solution.py:588
  234.1 5.7 %collective-permute-done.29 = bf16[128,128]{1,0:T(8,128)(2,1)S(1)} collective-permute-done((bf16[128,128]{1,0:T(8,128)(2,1)S(1)}, bf16[128,128]{1,0:T(8,128)(2,1)S(1)}, u32[]{:S(2)}, u32[]{:S(2)}) %collective-permute-start.29) | collective-permute-done | bytes 32800 | tf_op jit(solution)/shard_map/ppermute | solution.py:588
  240.0 4.0 %shard_map.134 = (bf16[512,2048]{1,0:T(8,128)(2,1)S(1)}, bf16[512,256]{1,0:T(8,128)(2,1)S(1)}, bf16[512,256]{1,0:T(8,128)(2,1)S(1)}) custom-call(s32[3]{0:T(128)S(1)} %copy-done.50, f32[128,2048]{1,0:T(8,128)S(1)} %copy-done.38, f32[128,512]{1,0:T(8,128)S(1)} %copy-done.47, f32[256,2048]{1,0:T(8,128)S(1)} %copy-done.6, f32[256,512]{1,0:T(8,128)S(1)} %copy-done.33, ...), custom_call_target="tpu_custom_call" | custom-call | flops 671088640 | bytes 10485760 | tf_op jit(solution)/shard_map/pallas_call | solution.py:246
  244.0 1.3 copy-done.56
  245.4 12.4 %shard_map.135 = (f32[128,2048]{1,0:T(8,128)S(1)}, f32[128,512]{1,0:T(8,128)S(1)}) custom-call(s32[4]{0:T(128)S(1)} %pad_add_fusion.5.info, bf16[128,2048]{1,0:T(8,128)(2,1)S(1)} %copy-done.9, bf16[128,2048]{1,0:T(8,128)(2,1)S(1)} %copy-done.16, bf16[128,2048]{1,0:T(8,128)(2,1)S(1)} %copy-done.12, bf16[128,2048]{1,0:T(8,128)(2,1)S(1)} %copy-done.14, ...), custom_call_target="tpu_custom_call" | custom-call | flops 4026531840 | bytes 33030144 | tf_op jit(solution)/shard_map/pallas_call | solution.py:99
  258.0 1.3 shard_map.137
  259.3 3.9 %collective-permute-start.41 = (bf16[128,256]{1,0:T(8,128)(2,1)S(1)}, bf16[128,256]{1,0:T(8,128)(2,1)S(1)}, u32[]{:S(2)}, u32[]{:S(2)}) collective-permute-start(bf16[128,256]{1,0:T(8,128)(2,1)S(1)} %get-tuple-element.30), channel_id=1, source_target_pairs={{0,4},{12,8},{1,5},{13,9},{2,6},{14,10},{3,7},{15,11},{16,20},{28,... | collective-permute-start | bytes 196616 | tf_op jit(solution)/shard_map/ppermute | solution.py:670
  263.3 6.3 %shard_map.136.ql_ref = bf16[128,2048]{1,0:T(8,128)(2,1)S(1)} custom-call(s32[2]{0:T(128)S(1)} %copy-done.53, bf16[128,2048]{1,0:T(8,128)(2,1)S(1)} %collective-permute-done.36.refs_0_, bf16[128,2048]{1,0:T(8,128)(2,1)S(1)} %collective-permute-done.37.refs_1_, bf16[8192,2048]{1,0:T(8,128)(2,1)} %refs_2_.2, f32[128,2048]{1,0:T(8,128)S(1)} %get-tuple-element.25.refs_3_, ...), custom_call_target="tpu_custom_call" | custom-call | flops 1207959552 | bytes 8388608 | tf_op jit(solution)/shard_map/pallas_call | solution.py:335
  269.7 16.5 %shard_map.138 = bf16[512,2048]{1,0:T(8,128)(2,1)} custom-call(s32[3]{0:T(128)S(1)} %pad_add_fusion.info, bf16[512,2048]{1,0:T(8,128)(2,1)S(1)} %copy-done.57, bf16[128,2048]{1,0:T(8,128)(2,1)S(1)} %shard_map.136.ql_ref, bf16[512,256]{1,0:T(8,128)(2,1)S(1)} %get-tuple-element.26.m_ref, bf16[128,256]{1,0:T(8,128)(2,1)S(1)} %get-tuple-element.28.ml_ref, ...), custom_call_target="tpu_custom_call" | custom-call | flops 2147483648 | bytes 4194304 | tf_op jit(solution)/shard_map/pallas_call | solution.py:425
  (207 shorter events, 24.2 us)
Async XLA Ops:
  11.3 35.2 %collective-permute-start.33 = (bf16[64,512]{1,0:T(8,128)(2,1)}, bf16[64,512]{1,0:T(8,128)(2,1)S(1)}, u32[]{:S(2)}, u32[]{:S(2)}) collective-permute-start(bf16[64,512]{1,0:T(8,128)(2,1)} %get-tuple-element.48), channel_id=1, source_target_pairs={{0,1},{1,2},{2,3},{3,0},{4,5},{5,6},{6,7},{7,4},{8,9},{9,10},{10,1... | collective-permute-start | bytes 196616 | tf_op jit(solution)/shard_map/ppermute | solution.py:511
  11.8 36.0 %collective-permute-start.34 = (bf16[64,512]{1,0:T(8,128)(2,1)}, bf16[64,512]{1,0:T(8,128)(2,1)}, u32[]{:S(2)}, u32[]{:S(2)}) collective-permute-start(bf16[64,512]{1,0:T(8,128)(2,1)} %get-tuple-element.50), channel_id=1, source_target_pairs={{0,2},{1,3},{2,0},{3,1},{4,6},{5,7},{6,4},{7,5},{8,10},{9,11},{10,... | collective-permute-start | bytes 196616 | tf_op jit(solution)/shard_map/ppermute | solution.py:511
  14.3 33.9 %collective-permute-start.35 = (bf16[64,512]{1,0:T(8,128)(2,1)}, bf16[64,512]{1,0:T(8,128)(2,1)}, u32[]{:S(2)}, u32[]{:S(2)}) collective-permute-start(bf16[64,512]{1,0:T(8,128)(2,1)} %get-tuple-element.49), channel_id=1, source_target_pairs={{0,3},{1,0},{2,1},{3,2},{4,7},{5,4},{6,5},{7,6},{8,11},{9,8},{10,9... | collective-permute-start | bytes 196616 | tf_op jit(solution)/shard_map/ppermute | solution.py:511
  18.5 43.3 %collective-permute-start.16 = (bf16[128,2048]{1,0:T(8,128)(2,1)}, bf16[128,2048]{1,0:T(8,128)(2,1)S(1)}, u32[]{:S(2)}, u32[]{:S(2)}) collective-permute-start(bf16[128,2048]{1,0:T(8,128)(2,1)} %get-tuple-element.36), channel_id=1, source_target_pairs={{0,1},{1,2},{2,3},{3,0},{4,5},{5,6},{6,7},{7,4},{8,9},{9,10},{10,1... | collective-permute-start | bytes 1572872 | tf_op jit(solution)/shard_map/ppermute | solution.py:511
  18.5 44.6 %collective-permute-start.17 = (bf16[128,2048]{1,0:T(8,128)(2,1)}, bf16[128,2048]{1,0:T(8,128)(2,1)}, u32[]{:S(2)}, u32[]{:S(2)}) collective-permute-start(bf16[128,2048]{1,0:T(8,128)(2,1)} %get-tuple-element.38), channel_id=1, source_target_pairs={{0,2},{1,3},{2,0},{3,1},{4,6},{5,7},{6,4},{7,5},{8,10},{9,11},{10,... | collective-permute-start | bytes 1572872 | tf_op jit(solution)/shard_map/ppermute | solution.py:511
  24.0 21.4 %copy-start.58 = (f32[512,64]{1,0:T(8,128)}, f32[512,64]{1,0:T(8,128)S(1)}, u32[]{:S(2)}) copy-start(f32[512,64]{1,0:T(8,128)S(1)} %get-tuple-element.63) | copy-start | bytes 393220
  24.1 21.4 %copy-start.59 = (f32[512,64]{1,0:T(8,128)}, f32[512,64]{1,0:T(8,128)S(1)}, u32[]{:S(2)}) copy-start(f32[512,64]{1,0:T(8,128)S(1)} %get-tuple-element.64) | copy-start | bytes 393220
  46.5 23.0 %copy-start.62 = (bf16[64,512]{1,0:T(8,128)(2,1)}, bf16[64,512]{1,0:T(8,128)(2,1)S(1)}, u32[]{:S(2)}) copy-start(bf16[64,512]{1,0:T(8,128)(2,1)S(1)} %collective-permute-done.33) | copy-start | bytes 196612
  46.5 7.0 %collective-permute-start.30 = (bf16[64,2048]{1,0:T(8,128)(2,1)}, bf16[64,2048]{1,0:T(8,128)(2,1)}, u32[]{:S(2)}, u32[]{:S(2)}) collective-permute-start(bf16[64,2048]{1,0:T(8,128)(2,1)} %get-tuple-element.40), channel_id=1, source_target_pairs={{0,1},{1,2},{2,3},{3,0},{4,5},{5,6},{6,7},{7,4},{8,9},{9,10},{10,1... | collective-permute-start | bytes 786440 | tf_op jit(solution)/shard_map/ppermute | solution.py:511
  47.8 9.6 %collective-permute-start.31 = (bf16[64,2048]{1,0:T(8,128)(2,1)}, bf16[64,2048]{1,0:T(8,128)(2,1)}, u32[]{:S(2)}, u32[]{:S(2)}) collective-permute-start(bf16[64,2048]{1,0:T(8,128)(2,1)} %get-tuple-element.42), channel_id=1, source_target_pairs={{0,2},{1,3},{2,0},{3,1},{4,6},{5,7},{6,4},{7,5},{8,10},{9,11},{10,... | collective-permute-start | bytes 786440 | tf_op jit(solution)/shard_map/ppermute | solution.py:511
  48.2 20.1 %collective-permute-start.18 = (bf16[128,2048]{1,0:T(8,128)(2,1)}, bf16[128,2048]{1,0:T(8,128)(2,1)S(1)}, u32[]{:S(2)}, u32[]{:S(2)}) collective-permute-start(bf16[128,2048]{1,0:T(8,128)(2,1)} %get-tuple-element.35), channel_id=1, source_target_pairs={{0,3},{1,0},{2,1},{3,2},{4,7},{5,4},{6,5},{7,6},{8,11},{9,8},{10,9... | collective-permute-start | bytes 1572872 | tf_op jit(solution)/shard_map/ppermute | solution.py:511
  53.5 17.8 %collective-permute-start = (bf16[128,2048]{1,0:T(8,128)(2,1)S(1)}, bf16[128,2048]{1,0:T(8,128)(2,1)S(1)}, u32[]{:S(2)}, u32[]{:S(2)}) collective-permute-start(bf16[128,2048]{1,0:T(8,128)(2,1)S(1)} %copy-done.19), channel_id=1, source_target_pairs={{4,0},{8,4},{12,8},{5,1},{9,5},{13,9},{6,2},{10,6},{14,10},{7,3},{... | collective-permute-start | bytes 1572872 | tf_op jit(solution)/shard_map/ppermute | solution.py:487
  57.4 19.2 %collective-permute-start.1 = (bf16[128,2048]{1,0:T(8,128)(2,1)S(1)}, bf16[128,2048]{1,0:T(8,128)(2,1)S(1)}, u32[]{:S(2)}, u32[]{:S(2)}) collective-permute-start(bf16[128,2048]{1,0:T(8,128)(2,1)S(1)} %copy-done.19), channel_id=1, source_target_pairs={{0,4},{4,8},{8,12},{1,5},{5,9},{9,13},{2,6},{6,10},{10,14},{3,7},{... | collective-permute-start | bytes 1572872 | tf_op jit(solution)/shard_map/ppermute | solution.py:491
  61.7 96.8 %copy-start.3 = (bf16[128,2048]{1,0:T(8,128)(2,1)}, bf16[128,2048]{1,0:T(8,128)(2,1)S(1)}, u32[]{:S(2)}) copy-start(bf16[128,2048]{1,0:T(8,128)(2,1)S(1)} %collective-permute-done.16.refs_2_.refs_9_.refs_5_) | copy-start | bytes 1572868
  61.7 19.6 %collective-permute-start.2 = (bf16[128,2048]{1,0:T(8,128)(2,1)S(1)}, bf16[128,2048]{1,0:T(8,128)(2,1)S(1)}, u32[]{:S(2)}, u32[]{:S(2)}) collective-permute-start(bf16[128,2048]{1,0:T(8,128)(2,1)S(1)} %copy-done.18), channel_id=1, source_target_pairs={{4,0},{8,4},{12,8},{5,1},{9,5},{13,9},{6,2},{10,6},{14,10},{7,3},{... | collective-permute-start | bytes 1572872 | tf_op jit(solution)/shard_map/ppermute | solution.py:487
  63.0 20.5 %collective-permute-start.3 = (bf16[128,2048]{1,0:T(8,128)(2,1)S(1)}, bf16[128,2048]{1,0:T(8,128)(2,1)S(1)}, u32[]{:S(2)}, u32[]{:S(2)}) collective-permute-start(bf16[128,2048]{1,0:T(8,128)(2,1)S(1)} %copy-done.18), channel_id=1, source_target_pairs={{0,4},{4,8},{8,12},{1,5},{5,9},{9,13},{2,6},{6,10},{10,14},{3,7},{... | collective-permute-start | bytes 1572872 | tf_op jit(solution)/shard_map/ppermute | solution.py:491
  68.2 24.4 %collective-permute-start.4 = (bf16[128,2048]{1,0:T(8,128)(2,1)S(1)}, bf16[128,2048]{1,0:T(8,128)(2,1)}, u32[]{:S(2)}, u32[]{:S(2)}) collective-permute-start(bf16[128,2048]{1,0:T(8,128)(2,1)S(1)} %copy-done.17), channel_id=1, source_target_pairs={{4,0},{8,4},{12,8},{5,1},{9,5},{13,9},{6,2},{10,6},{14,10},{7,3},{... | collective-permute-start | bytes 1572872 | tf_op jit(solution)/shard_map/ppermute | solution.py:487
  71.3 45.2 %copy-start.23 = (bf16[128,2048]{1,0:T(8,128)(2,1)}, bf16[128,2048]{1,0:T(8,128)(2,1)S(1)}, u32[]{:S(2)}) copy-start(bf16[128,2048]{1,0:T(8,128)(2,1)S(1)} %collective-permute-done.refs_0_) | copy-start | bytes 1572868
  71.3 23.5 %collective-permute-start.5 = (bf16[128,2048]{1,0:T(8,128)(2,1)S(1)}, bf16[128,2048]{1,0:T(8,128)(2,1)}, u32[]{:S(2)}, u32[]{:S(2)}) collective-permute-start(bf16[128,2048]{1,0:T(8,128)(2,1)S(1)} %copy-done.17), channel_id=1, source_target_pairs={{0,4},{4,8},{8,12},{1,5},{5,9},{9,13},{2,6},{6,10},{10,14},{3,7},{... | collective-permute-start | bytes 1572872 | tf_op jit(solution)/shard_map/ppermute | solution.py:491
  76.6 39.8 %copy-start.20 = (bf16[128,2048]{1,0:T(8,128)(2,1)}, bf16[128,2048]{1,0:T(8,128)(2,1)S(1)}, u32[]{:S(2)}) copy-start(bf16[128,2048]{1,0:T(8,128)(2,1)S(1)} %collective-permute-done.1.refs_1_.refs_4_) | copy-start | bytes 1572868
  76.6 29.5 %collective-permute-start.7 = (bf16[128,2048]{1,0:T(8,128)(2,1)}, bf16[128,2048]{1,0:T(8,128)(2,1)}, u32[]{:S(2)}, u32[]{:S(2)}) collective-permute-start(bf16[128,2048]{1,0:T(8,128)(2,1)} %get-tuple-element.43.refs_3_), channel_id=1, source_target_pairs={{0,4},{4,8},{8,12},{1,5},{5,9},{9,13},{2,6},{6,10},{10,14},{3,7},{... | collective-permute-start | bytes 1572872 | tf_op jit(solution)/shard_map/ppermute | solution.py:491
  81.3 35.1 %collective-permute-start.10 = (bf16[128,2048]{1,0:T(8,128)(2,1)S(1)}, bf16[128,2048]{1,0:T(8,128)(2,1)}, u32[]{:S(2)}, u32[]{:S(2)}) collective-permute-start(bf16[128,2048]{1,0:T(8,128)(2,1)S(1)} %collective-permute-done.2.refs_2_.refs_1_), channel_id=1, source_target_pairs={{4,0},{8,4},{5,1},{9,5},{6,2},{10,6},{7,3},{11,7},{20,16},{24,20},... | collective-permute-start | bytes 1572872 | tf_op jit(solution)/shard_map/ppermute | solution.py:487
  84.3 30.8 %collective-permute-start.8 = (bf16[128,2048]{1,0:T(8,128)(2,1)S(1)}, bf16[128,2048]{1,0:T(8,128)(2,1)}, u32[]{:S(2)}, u32[]{:S(2)}) collective-permute-start(bf16[128,2048]{1,0:T(8,128)(2,1)S(1)} %collective-permute-done.refs_0_), channel_id=1, source_target_pairs={{4,0},{8,4},{5,1},{9,5},{6,2},{10,6},{7,3},{11,7},{20,16},{24,20},... | collective-permute-start | bytes 1572872 | tf_op jit(solution)/shard_map/ppermute | solution.py:487
  92.7 33.7 %collective-permute-start.6 = (bf16[128,2048]{1,0:T(8,128)(2,1)}, bf16[128,2048]{1,0:T(8,128)(2,1)}, u32[]{:S(2)}, u32[]{:S(2)}) collective-permute-start(bf16[128,2048]{1,0:T(8,128)(2,1)} %get-tuple-element.43.refs_3_), channel_id=1, source_target_pairs={{4,0},{8,4},{12,8},{5,1},{9,5},{13,9},{6,2},{10,6},{14,10},{7,3},{... | collective-permute-start | bytes 1572872 | tf_op jit(solution)/shard_map/ppermute | solution.py:487
  94.8 32.6 %collective-permute-start.11 = (bf16[128,2048]{1,0:T(8,128)(2,1)}, bf16[128,2048]{1,0:T(8,128)(2,1)}, u32[]{:S(2)}, u32[]{:S(2)}) collective-permute-start(bf16[128,2048]{1,0:T(8,128)(2,1)} %collective-permute-done.5.refs_5_.refs_6_), channel_id=1, source_target_pairs={{4,8},{8,12},{5,9},{9,13},{6,10},{10,14},{7,11},{11,15},{20,24},{2... | collective-permute-start | bytes 1572872 | tf_op jit(solution)/shard_map/ppermute | solution.py:491
  106.1 22.0 %collective-permute-start.9 = (bf16[128,2048]{1,0:T(8,128)(2,1)}, bf16[128,2048]{1,0:T(8,128)(2,1)}, u32[]{:S(2)}, u32[]{:S(2)}) collective-permute-start(bf16[128,2048]{1,0:T(8,128)(2,1)} %collective-permute-done.7.refs_7_), channel_id=1, source_target_pairs={{4,8},{8,12},{5,9},{9,13},{6,10},{10,14},{7,11},{11,15},{20,24},{2... | collective-permute-start | bytes 1572872 | tf_op jit(solution)/shard_map/ppermute | solution.py:491
  115.1 23.1 %collective-permute-start.22 = (bf16[128,2048]{1,0:T(8,128)(2,1)}, bf16[128,2048]{1,0:T(8,128)(2,1)S(1)}, u32[]{:S(2)}, u32[]{:S(2)}) collective-permute-start(bf16[128,2048]{1,0:T(8,128)(2,1)} %collective-permute-done.8.refs_0_), channel_id=1, source_target_pairs={{4,0},{5,1},{6,2},{7,3},{20,16},{21,17},{22,18},{23,19}} | collective-permute-start | bytes 1572872 | tf_op jit(solution)/shard_map/ppermute | solution.py:487
  116.4 32.3 %collective-permute-start.23 = (bf16[128,2048]{1,0:T(8,128)(2,1)}, bf16[128,2048]{1,0:T(8,128)(2,1)S(1)}, u32[]{:S(2)}, u32[]{:S(2)}) collective-permute-start(bf16[128,2048]{1,0:T(8,128)(2,1)} %collective-permute-done.10.refs_2_.refs_1_), channel_id=1, source_target_pairs={{4,0},{5,1},{6,2},{7,3},{20,16},{21,17},{22,18},{23,19}} | collective-permute-start | bytes 1572872 | tf_op jit(solution)/shard_map/ppermute | solution.py:487
  126.4 10.5 %collective-permute-start.32 = (bf16[64,2048]{1,0:T(8,128)(2,1)}, bf16[64,2048]{1,0:T(8,128)(2,1)S(1)}, u32[]{:S(2)}, u32[]{:S(2)}) collective-permute-start(bf16[64,2048]{1,0:T(8,128)(2,1)} %get-tuple-element.41), channel_id=1, source_target_pairs={{0,3},{1,0},{2,1},{3,2},{4,7},{5,4},{6,5},{7,6},{8,11},{9,8},{10,9... | collective-permute-start | bytes 786440 | tf_op jit(solution)/shard_map/ppermute | solution.py:511
  127.4 28.3 %collective-permute-start.24 = (bf16[128,2048]{1,0:T(8,128)(2,1)}, bf16[128,2048]{1,0:T(8,128)(2,1)S(1)}, u32[]{:S(2)}, u32[]{:S(2)}) collective-permute-start(bf16[128,2048]{1,0:T(8,128)(2,1)} %collective-permute-done.11.refs_3_.refs_2_), channel_id=1, source_target_pairs={{8,12},{9,13},{10,14},{11,15},{24,28},{25,29},{26,30},{27,31}} | collective-permute-start | bytes 1572872 | tf_op jit(solution)/shard_map/ppermute | solution.py:491
  128.1 29.1 %collective-permute-start.25 = (bf16[128,2048]{1,0:T(8,128)(2,1)}, bf16[128,2048]{1,0:T(8,128)(2,1)S(1)}, u32[]{:S(2)}, u32[]{:S(2)}) collective-permute-start(bf16[128,2048]{1,0:T(8,128)(2,1)} %collective-permute-done.9.refs_1_.refs_3_), channel_id=1, source_target_pairs={{8,12},{9,13},{10,14},{11,15},{24,28},{25,29},{26,30},{27,31}} | collective-permute-start | bytes 1572872 | tf_op jit(solution)/shard_map/ppermute | solution.py:491
  136.9 34.9 %collective-permute-start.12 = (bf16[128,2048]{1,0:T(8,128)(2,1)}, bf16[128,2048]{1,0:T(8,128)(2,1)}, u32[]{:S(2)}, u32[]{:S(2)}) collective-permute-start(bf16[128,2048]{1,0:T(8,128)(2,1)} %collective-permute-done.4.refs_4_.refs_2_), channel_id=1, source_target_pairs={{4,0},{8,4},{5,1},{9,5},{6,2},{10,6},{7,3},{11,7},{20,16},{24,20},... | collective-permute-start | bytes 1572872 | tf_op jit(solution)/shard_map/ppermute | solution.py:487
  139.0 22.3 %collective-permute-start.19 = (f32[128,128]{1,0:T(8,128)S(1)}, f32[128,128]{1,0:T(8,128)S(1)}, u32[]{:S(2)}, u32[]{:S(2)}) collective-permute-start(f32[128,128]{1,0:T(8,128)S(1)} %get-tuple-element.61), channel_id=1, source_target_pairs={{0,4},{4,8},{8,12},{1,5},{5,9},{9,13},{2,6},{6,10},{10,14},{3,7},{... | collective-permute-start | bytes 196616 | tf_op jit(solution)/shard_map/ppermute | solution.py:563
  149.5 13.4 %collective-permute-start.20 = (f32[128,128]{1,0:T(8,128)S(1)}, f32[128,128]{1,0:T(8,128)S(1)}, u32[]{:S(2)}, u32[]{:S(2)}) collective-permute-start(f32[128,128]{1,0:T(8,128)S(1)} %get-tuple-element.62), channel_id=1, source_target_pairs={{4,0},{8,4},{12,8},{5,1},{9,5},{13,9},{6,2},{10,6},{14,10},{7,3},{... | collective-permute-start | bytes 196616 | tf_op jit(solution)/shard_map/ppermute | solution.py:566
  152.0 25.4 %copy-start.25 = (bf16[128,2048]{1,0:T(8,128)(2,1)S(1)}, bf16[128,2048]{1,0:T(8,128)(2,1)}, u32[]{:S(2)}) copy-start(bf16[128,2048]{1,0:T(8,128)(2,1)} %copy-done.23) | copy-start | bytes 1572868
  152.0 25.4 %copy-start.31 = (bf16[128,2048]{1,0:T(8,128)(2,1)S(1)}, bf16[128,2048]{1,0:T(8,128)(2,1)}, u32[]{:S(2)}) copy-start(bf16[128,2048]{1,0:T(8,128)(2,1)} %copy-done.29) | copy-start | bytes 1572868
  155.7 46.1 %collective-permute-start.13 = (bf16[128,2048]{1,0:T(8,128)(2,1)S(1)}, bf16[128,2048]{1,0:T(8,128)(2,1)}, u32[]{:S(2)}, u32[]{:S(2)}) collective-permute-start(bf16[128,2048]{1,0:T(8,128)(2,1)S(1)} %copy-done.28), channel_id=1, source_target_pairs={{4,8},{8,12},{5,9},{9,13},{6,10},{10,14},{7,11},{11,15},{20,24},{2... | collective-permute-start | bytes 1572872 | tf_op jit(solution)/shard_map/ppermute | solution.py:491
  157.2 45.9 %collective-permute-start.14 = (bf16[128,2048]{1,0:T(8,128)(2,1)}, bf16[128,2048]{1,0:T(8,128)(2,1)}, u32[]{:S(2)}, u32[]{:S(2)}) collective-permute-start(bf16[128,2048]{1,0:T(8,128)(2,1)} %collective-permute-done.6.refs_6_.refs_3_), channel_id=1, source_target_pairs={{4,0},{8,4},{5,1},{9,5},{6,2},{10,6},{7,3},{11,7},{20,16},{24,20},... | collective-permute-start | bytes 1572872 | tf_op jit(solution)/shard_map/ppermute | solution.py:487
  158.6 47.8 %slice-start = ((s8[8388608]{0:T(1024)(128)(4,1)}), s8[4194304]{0:T(1024)(128)(4,1)S(1)}, s32[]{:S(2)}) async-start(s8[8388608]{0:T(1024)(128)(4,1)} %bitcast.46), calls=%async_computation | async-start | bytes 8388608
  161.2 38.2 %copy-start.2 = (bf16[128,8192]{1,0:T(8,128)(2,1)S(1)}, bf16[128,8192]{1,0:T(8,128)(2,1)}, u32[]{:S(2)}) copy-start(bf16[128,8192]{1,0:T(8,128)(2,1)} %refs_0_.1) | copy-start | bytes 6291460
  161.2 38.2 %copy-start.4 = (bf16[128,2048]{1,0:T(8,128)(2,1)S(1)}, bf16[128,2048]{1,0:T(8,128)(2,1)}, u32[]{:S(2)}) copy-start(bf16[128,2048]{1,0:T(8,128)(2,1)} %copy-done.3) | copy-start | bytes 1572868
  161.2 38.2 %copy-start.41 = (f32[128,4]{1,0:T(8,128)S(1)}, f32[128,4]{1,0:T(8,128)}, u32[]{:S(2)}) copy-start(f32[128,4]{1,0:T(8,128)} %get-tuple-element.58.refs_5_) | copy-start | bytes 6148
  161.3 38.2 %copy-start.54 = (s32[2]{0:T(128)S(1)}, s32[2]{0:T(128)}, u32[]{:S(2)}) copy-start(s32[2]{0:T(128)} %pad_add_fusion.2.info) | copy-start | bytes 28
  161.3 45.1 %slice-start.1 = ((s8[8388608]{0:T(1024)(128)(4,1)}), s8[4194304]{0:T(1024)(128)(4,1)S(1)}, s32[]{:S(2)}) async-start(s8[8388608]{0:T(1024)(128)(4,1)} %bitcast.46), calls=%async_computation.1 | async-start | bytes 8388608
  161.3 42.5 %collective-permute-start.15 = (bf16[128,2048]{1,0:T(8,128)(2,1)S(1)}, bf16[128,2048]{1,0:T(8,128)(2,1)}, u32[]{:S(2)}, u32[]{:S(2)}) collective-permute-start(bf16[128,2048]{1,0:T(8,128)(2,1)S(1)} %copy-done.22), channel_id=1, source_target_pairs={{4,8},{8,12},{5,9},{9,13},{6,10},{10,14},{7,11},{11,15},{20,24},{2... | collective-permute-start | bytes 1572872 | tf_op jit(solution)/shard_map/ppermute | solution.py:491
  162.9 42.2 %collective-permute-start.21 = (f32[128,128]{1,0:T(8,128)S(1)}, f32[128,128]{1,0:T(8,128)S(1)}, u32[]{:S(2)}, u32[]{:S(2)}) collective-permute-start(f32[128,128]{1,0:T(8,128)S(1)} %shard_map.132), channel_id=1, source_target_pairs={{0,8},{4,12},{8,0},{12,4},{1,9},{5,13},{9,1},{13,5},{2,10},{6,14},... | collective-permute-start | bytes 196616 | tf_op jit(solution)/shard_map/ppermute | solution.py:581
  171.8 34.1 %collective-permute-start.26 = (f32[128,128]{1,0:T(8,128)S(1)}, f32[128,128]{1,0:T(8,128)S(1)}, u32[]{:S(2)}, u32[]{:S(2)}) collective-permute-start(f32[128,128]{1,0:T(8,128)S(1)} %shard_map.133), channel_id=1, source_target_pairs={{0,12},{12,0},{1,13},{13,1},{2,14},{14,2},{3,15},{15,3},{16,28},{2... | collective-permute-start | bytes 196616 | tf_op jit(solution)/shard_map/ppermute | solution.py:581
  201.8 43.5 %collective-permute-start.38 = (bf16[128,2048]{1,0:T(8,128)(2,1)}, bf16[128,2048]{1,0:T(8,128)(2,1)S(1)}, u32[]{:S(2)}, u32[]{:S(2)}) collective-permute-start(bf16[128,2048]{1,0:T(8,128)(2,1)} %collective-permute-done.12.refs_4_), channel_id=1, source_target_pairs={{4,0},{5,1},{6,2},{7,3},{20,16},{21,17},{22,18},{23,19}} | collective-permute-start | bytes 1572872 | tf_op jit(solution)/shard_map/ppermute | solution.py:487
  203.1 42.2 %collective-permute-start.39 = (bf16[128,2048]{1,0:T(8,128)(2,1)}, bf16[128,2048]{1,0:T(8,128)(2,1)S(1)}, u32[]{:S(2)}, u32[]{:S(2)}) collective-permute-start(bf16[128,2048]{1,0:T(8,128)(2,1)} %collective-permute-done.13.refs_5_), channel_id=1, source_target_pairs={{8,12},{9,13},{10,14},{11,15},{24,28},{25,29},{26,30},{27,31}} | collective-permute-start | bytes 1572872 | tf_op jit(solution)/shard_map/ppermute | solution.py:491
  203.9 54.1 %collective-permute-start.36 = (bf16[128,2048]{1,0:T(8,128)(2,1)}, bf16[128,2048]{1,0:T(8,128)(2,1)S(1)}, u32[]{:S(2)}, u32[]{:S(2)}) collective-permute-start(bf16[128,2048]{1,0:T(8,128)(2,1)} %collective-permute-done.14.refs_6_), channel_id=1, source_target_pairs={{4,0},{5,1},{6,2},{7,3},{20,16},{21,17},{22,18},{23,19}} | collective-permute-start | bytes 1572872 | tf_op jit(solution)/shard_map/ppermute | solution.py:487
  205.2 52.8 %collective-permute-start.37 = (bf16[128,2048]{1,0:T(8,128)(2,1)}, bf16[128,2048]{1,0:T(8,128)(2,1)S(1)}, u32[]{:S(2)}, u32[]{:S(2)}) collective-permute-start(bf16[128,2048]{1,0:T(8,128)(2,1)} %collective-permute-done.15.refs_7_), channel_id=1, source_target_pairs={{8,12},{9,13},{10,14},{11,15},{24,28},{25,29},{26,30},{27,31}} | collective-permute-start | bytes 1572872 | tf_op jit(solution)/shard_map/ppermute | solution.py:491
  205.9 34.0 %copy-start.33 = (f32[256,512]{1,0:T(8,128)S(1)}, f32[256,512]{1,0:T(8,128)}, u32[]{:S(2)}) copy-start(f32[256,512]{1,0:T(8,128)} %copy-done.32) | copy-start | bytes 1572868
  205.9 34.0 %copy-start.34 = (f32[512,128]{1,0:T(8,128)S(1)}, f32[512,128]{1,0:T(8,128)}, u32[]{:S(2)}) copy-start(f32[512,128]{1,0:T(8,128)} %get-tuple-element.71.refs_14_) | copy-start | bytes 786436
  205.9 34.0 %copy-start.35 = (f32[512,128]{1,0:T(8,128)S(1)}, f32[512,128]{1,0:T(8,128)}, u32[]{:S(2)}) copy-start(f32[512,128]{1,0:T(8,128)} %get-tuple-element.32.refs_13_) | copy-start | bytes 786436
  205.9 34.0 %copy-start.36 = (f32[512,128]{1,0:T(8,128)S(1)}, f32[512,128]{1,0:T(8,128)}, u32[]{:S(2)}) copy-start(f32[512,128]{1,0:T(8,128)} %get-tuple-element.70.refs_12_) | copy-start | bytes 786436
  205.9 34.0 %copy-start.38 = (f32[128,2048]{1,0:T(8,128)S(1)}, f32[128,2048]{1,0:T(8,128)}, u32[]{:S(2)}) copy-start(f32[128,2048]{1,0:T(8,128)} %copy-done.37) | copy-start | bytes 3145732
  206.0 34.0 %copy-start.47 = (f32[128,512]{1,0:T(8,128)S(1)}, f32[128,512]{1,0:T(8,128)}, u32[]{:S(2)}) copy-start(f32[128,512]{1,0:T(8,128)} %copy-done.46) | copy-start | bytes 786436
  206.0 34.0 %copy-start.50 = (s32[3]{0:T(128)S(1)}, s32[3]{0:T(128)}, u32[]{:S(2)}) copy-start(s32[3]{0:T(128)} %pad_add_fusion.1.info) | copy-start | bytes 40
  206.0 23.3 %collective-permute-start.27 = (bf16[128,128]{1,0:T(8,128)(2,1)S(1)}, bf16[128,128]{1,0:T(8,128)(2,1)S(1)}, u32[]{:S(2)}, u32[]{:S(2)}) collective-permute-start(bf16[128,128]{1,0:T(8,128)(2,1)S(1)} %get-tuple-element.34), channel_id=1, source_target_pairs={{4,0},{8,4},{12,8},{0,12},{5,1},{9,5},{13,9},{1,13},{6,2},{10,6},{... | collective-permute-start | bytes 98312 | tf_op jit(solution)/shard_map/ppermute | solution.py:588
  206.3 33.7 %copy-start.6 = (f32[256,2048]{1,0:T(8,128)S(1)}, f32[256,2048]{1,0:T(8,128)}, u32[]{:S(2)}) copy-start(f32[256,2048]{1,0:T(8,128)} %copy-done.5) | copy-start | bytes 6291460
  229.3 4.8 %collective-permute-start.28 = (bf16[128,128]{1,0:T(8,128)(2,1)S(1)}, bf16[128,128]{1,0:T(8,128)(2,1)S(1)}, u32[]{:S(2)}, u32[]{:S(2)}) collective-permute-start(bf16[128,128]{1,0:T(8,128)(2,1)S(1)} %get-tuple-element.34), channel_id=1, source_target_pairs={{8,0},{12,4},{0,8},{4,12},{9,1},{13,5},{1,9},{5,13},{10,2},{14,6},... | collective-permute-start | bytes 98312 | tf_op jit(solution)/shard_map/ppermute | solution.py:588
  234.1 5.7 %collective-permute-start.29 = (bf16[128,128]{1,0:T(8,128)(2,1)S(1)}, bf16[128,128]{1,0:T(8,128)(2,1)S(1)}, u32[]{:S(2)}, u32[]{:S(2)}) collective-permute-start(bf16[128,128]{1,0:T(8,128)(2,1)S(1)} %get-tuple-element.34), channel_id=1, source_target_pairs={{12,0},{0,4},{4,8},{8,12},{13,1},{1,5},{5,9},{9,13},{14,2},{2,6},{... | collective-permute-start | bytes 98312 | tf_op jit(solution)/shard_map/ppermute | solution.py:588
  245.3 24.3 %collective-permute-start.40 = (bf16[512,256]{1,0:T(8,128)(2,1)S(1)}, bf16[512,256]{1,0:T(8,128)(2,1)S(1)}, u32[]{:S(2)}, u32[]{:S(2)}) collective-permute-start(bf16[512,256]{1,0:T(8,128)(2,1)S(1)} %get-tuple-element.29), channel_id=1, source_target_pairs={{0,4},{4,0},{8,12},{12,8},{1,5},{5,1},{9,13},{13,9},{2,6},{6,2},{1... | collective-permute-start | bytes 786440 | tf_op jit(solution)/shard_map/ppermute | solution.py:651
  259.3 10.3 %collective-permute-start.41 = (bf16[128,256]{1,0:T(8,128)(2,1)S(1)}, bf16[128,256]{1,0:T(8,128)(2,1)S(1)}, u32[]{:S(2)}, u32[]{:S(2)}) collective-permute-start(bf16[128,256]{1,0:T(8,128)(2,1)S(1)} %get-tuple-element.30), channel_id=1, source_target_pairs={{0,4},{12,8},{1,5},{13,9},{2,6},{14,10},{3,7},{15,11},{16,20},{28,... | collective-permute-start | bytes 196616 | tf_op jit(solution)/shard_map/ppermute | solution.py:670
  (43 other events, 231.0 us)

commit v2 on v1

--- a/solution.py
+++ b/solution.py
@@ -23,7 +23,11 @@
 VMEM_LIMIT = 40 * 2**20
 F32 = jnp.float32
 BF16 = jnp.bfloat16
-ANY = pl.BlockSpec(memory_space=pl.ANY)
+ANY = pl.BlockSpec(memory_space=pltpu.HBM)
+
+
+def after(arrays, *others):
+    return lax.optimization_barrier((arrays, others))[0]
 
 
 def params():
@@ -481,14 +485,24 @@
 
     down = {(0, c): tokens[:, c * chunk_width : (c + 1) * chunk_width] for c in range(chunks)}
     up = dict(down)
-    for k in range(1, n):
-        for a in range(chunks):
-            c = a
-            down[k, c] = lax.ppermute(
-                down[k - 1, c], "tensor", [(i, i - 1) for i in range(1, n - k + 1)]
-            )
-            c = chunks - 1 - a
-            up[k, c] = lax.ppermute(up[k - 1, c], "tensor", [(i, i + 1) for i in range(k - 1, n - 1)])
+    ahead = [(k, 0) for k in range(1, n)]
+    behind = [(k, a) for k in range(1, n) for a in range(1, chunks)]
+    turns = [t for both in zip(ahead, behind) for t in both] + behind[len(ahead) :]
+    def send_turn(i, *others):
+        k, a = turns[i]
+        b = chunks - 1 - a
+        if i >= 2:
+            k_before, a_before = turns[i - 2]
+            others += (down[k_before, a_before], up[k_before, chunks - 1 - a_before])
+        send_down, send_up = after((down[k - 1, a], up[k - 1, b]), *others)
+        down[k, a] = lax.ppermute(send_down, "tensor", [(j, j - 1) for j in range(1, n - k + 1)])
+        up[k, b] = lax.ppermute(send_up, "tensor", [(j, j + 1) for j in range(k - 1, n - 1)])
+
+    def turn_of(k):
+        return max(i for i, (j, _) in enumerate(turns) if j == k)
+
+    send_turn(0)
+    send_turn(1)
 
     per_store = adapter_down_maps.shape[0]
     lookup = (
@@ -499,22 +513,25 @@
     here = slot_table // per_store == store
     local = jnp.sum(jnp.where(here, slot_table - store * per_store, 0), axis=1)
 
-    def exchanged(stack):
-        got = []
+    stacks = [adapter_down_maps, adapter_up_key_value, adapter_up_query]
+    got = [[], [], []]
+    last = down[0, 0]
+    sent = []
+    for which, stack in enumerate(stacks):
         for d in range(stores):
             target = (store + d) % stores
             row = lax.dynamic_index_in_dim(local, target, 0, keepdims=False)
             part = lax.dynamic_index_in_dim(stack, row, 0, keepdims=False)
-            got.append(
-                part
-                if d == 0
-                else lax.ppermute(part, "store", [(i, (i + d) % stores) for i in range(stores)])
-            )
-        return got
-
-    downs = exchanged(adapter_down_maps)
-    up_query = jnp.concatenate(exchanged(adapter_up_query), axis=0)
-    up_keyval = jnp.concatenate(exchanged(adapter_up_key_value), axis=0)
+            if d:
+                part = after(part, last)
+                sent.append(part)
+                last = part = lax.ppermute(
+                    part, "store", [(i, (i + d) % stores) for i in range(stores)]
+                )
+            got[which].append(part)
+    downs, up_keyval, up_query = got
+    up_query = jnp.concatenate(up_query, axis=0)
+    up_keyval = jnp.concatenate(up_keyval, axis=0)
 
     segment_row = token_request_ids[0]
     my_holders = lax.dynamic_index_in_dim(slot_table, store, 0, keepdims=False) // per_store
@@ -545,44 +562,78 @@
     def every_chunk(way, k):
         return [way[k, c] for c in range(chunks)]
 
-    parts = {}
-    first = low_parts(
+    weights = [query_weight, key_value_weight]
+    sources = []
+    own_q, own_kv = project(
+        [[[down[0, c]]] for c in range(chunks)],
+        after(jnp.zeros((1,), jnp.int32), downs[0], sent[0]),
+        list(range(chunks)),
+        weights,
+    )
+    sources.append((own_q, own_kv, 0, lambda b, zz: b == zz))
+    side_chunks = [jnp.where(side == 0, a, chunks - 1 - a) for a in range(chunks)]
+
+    def sided(k, a):
+        return [down[k, a], up[k, chunks - 1 - a]]
+
+    hold = {2: own_kv}
+    next_turn = 2
+
+    def send_until(turn):
+        nonlocal next_turn
+        while next_turn <= min(turn, len(turns) - 1):
+            send_turn(next_turn, *([hold[next_turn]] if next_turn in hold else []))
+            next_turn += 1
+
+    def near(k):
+        return [
+            ([down[k, c] for c in range(chunks)], z + k),
+            ([up[k, c] for c in range(chunks)], z - k),
+        ]
+
+    def far(k):
+        return (
+            [down[k, c] for c in range(chunks // 2)] + [up[k, c] for c in range(chunks // 2, chunks)],
+            jnp.where(side == 0, z + k, z - k),
+        )
+
+    def low_of(groups):
+        return low_parts(
+            [g for g, _ in groups],
+            home_chunk,
+            home_offset,
+            width_share,
+            downs,
+            [block_of(members, b) for _, b in groups],
+        )
+
+    low_sum = low_parts(
         [[tokens]], jnp.int32(0), z * width_share, width_share, downs, [block_of(members, z)]
     )
-    low_sum = first
-    for k in range(1, n):
-        if k < half:
-            both = low_parts(
-                [every_chunk(down, k), every_chunk(up, k)],
-                home_chunk,
-                home_offset,
-                width_share,
-                downs,
-                [block_of(members, z + k), block_of(members, z - k)],
-            )
-            low_sum = low_sum + lax.ppermute(
-                both[:rows], "tensor", [(i, i + k) for i in range(n - k)]
-            )
-            low_sum = low_sum + lax.ppermute(
-                both[rows:], "tensor", [(i, i - k) for i in range(k, n)]
-            )
-        else:
-            one = low_parts(
-                [
-                    [down[k, c] for c in range(chunks // 2)]
-                    + [up[k, c] for c in range(chunks // 2, chunks)]
-                ],
-                home_chunk,
-                home_offset,
-                width_share,
-                downs,
-                [block_of(members, jnp.where(side == 0, z + k, z - k))],
-            )
-            low_sum = low_sum + lax.ppermute(
-                one,
-                "tensor",
-                [(i, i + k) for i in range(n - k)] + [(i, i - k) for i in range(k, n)],
-            )
+    projected = {}
+    for k in range(1, half):
+        send_until(turn_of(k) + 2)
+        both = low_of(near(k))
+        low_sum = low_sum + lax.ppermute(both[:rows], "tensor", [(i, i + k) for i in range(n - k)])
+        low_sum = low_sum + lax.ppermute(both[rows:], "tensor", [(i, i - k) for i in range(k, n)])
+        q, kv = project(
+            [[[down[k, c]], [up[k, c]]] for c in range(chunks)],
+            after(jnp.zeros((2,), jnp.int32), both),
+            list(range(chunks)),
+            weights,
+        )
+        hold[turn_of(k) + 3] = kv
+        sources.append((q, kv, 0, lambda b, zz, k=k: b == zz + k))
+        sources.append((q, kv, rows, lambda b, zz, k=k: b == zz - k))
+    far_home = max(i for i, (_, a) in enumerate(turns) if a < chunks // 2)
+    send_until(far_home)
+    far_low = low_of([far(k) for k in range(half, n)])
+    for k in range(half, n):
+        low_sum = low_sum + lax.ppermute(
+            far_low[(k - half) * rows : (k - half + 1) * rows],
+            "tensor",
+            [(i, i + k) for i in range(n - k)] + [(i, i - k) for i in range(k, n)],
+        )
     low_own = low_sum.astype(BF16)
     low_turned = [low_own] + [
         lax.ppermute(low_own, "tensor", [((i + r) % n, i) for i in range(n)]) for r in range(1, n)
@@ -591,42 +642,17 @@
         jnp.concatenate(low_turned + low_turned, axis=0), (n - z) % n * rows, total, 0
     )
 
-    weights = [query_weight, key_value_weight]
-    sources = []
-    own_q, own_kv = project(
-        [[[down[0, c]]] for c in range(chunks)], [0], list(range(chunks)), weights
-    )
-    sources.append((own_q, own_kv, 0, lambda b, zz: b == zz))
-    side_chunks = [jnp.where(side == 0, a, chunks - 1 - a) for a in range(chunks)]
-
-    def sided(k, a):
-        return [down[k, a], up[k, chunks - 1 - a]]
-
-    for k in range(1, late):
-        if k < half:
-            q, kv = project(
-                [[[down[k, c]], [up[k, c]]] for c in range(chunks)],
-                [0, 0],
-                list(range(chunks)),
-                weights,
-            )
-            sources.append((q, kv, 0, lambda b, zz, k=k: b == zz + k))
-            sources.append((q, kv, rows, lambda b, zz, k=k: b == zz - k))
-        else:
-            q, kv = project(
-                [[sided(k, a)] for a in range(chunks)],
-                jnp.stack([side]),
-                jnp.stack(side_chunks),
-                weights,
-            )
-            sources.append((q, kv, 0, lambda b, zz, k=k: (b == zz + k) | (b == zz - k)))
-    late_q, late_kv = project(
-        [[sided(late, a)] for a in range(chunks - 1)],
-        jnp.stack([side]),
-        jnp.stack(side_chunks[: chunks - 1]),
-        weights,
-    )
-
+    for k in range(half, late):
+        send_until(turn_of(k) + 2)
+        q, kv = project(
+            [[sided(k, a)] for a in range(chunks)],
+            after(jnp.stack([side]), low),
+            jnp.stack(side_chunks),
+            weights,
+        )
+        hold[turn_of(k) + 3] = kv
+        sources.append((q, kv, 0, lambda b, zz, k=k: (b == zz + k) | (b == zz - k)))
+    send_until(len(turns))
     group_size = QUERY_HEADS // KEY_VALUE_HEADS
     head_local = query_width // HEAD_SIZE
     pair_heads = keyval_width // HEAD_SIZE
@@ -649,6 +675,12 @@
         n,
     )
     recv = lax.ppermute(send, "tensor", [(i, i ^ 1) for i in range(n)])
+    late_q, late_kv = project(
+        [[sided(late, a)] for a in range(chunks - 1)],
+        after(jnp.stack([side]), mine),
+        jnp.stack(side_chunks[: chunks - 1]),
+        weights,
+    )
 
     late_block = jnp.where(side == 0, n - 1, 0)
     late_args = dict(

time: 288 us -> 290 us (level)
  waiting for transfers between devices: 56.7 us -> 42.9 us
  starting transfers between devices: 73.7 us -> 85.1 us
  local copies, waits for them, and re-layouts: 29.6 us -> 40.7 us
  Pallas kernels: 107 us -> 101 us
    ppermute x3, waiting for transfers between devices: 15.6 us -> 4.68 us  [on_device(): lax.ppermute(low_own, 'tensor', [((i + r) % n, i) for i in range(n)])]
    unnamed x136 -> x150, local copies, waits for them, and re-layouts: 16.5 us -> 26 us
    ppermute x1, starting transfers between devices: 4.54 us -> 12.8 us  [on_device(): lax.ppermute(both[:rows], 'tensor', [(i, i + k) for i in range(n - k)])]
    ppermute x3, starting transfers between devices: 0.35 us -> 8.41 us  [on_device(): lax.ppermute(low_own, 'tensor', [((i + r) % n, i) for i in range(n)])]
    ppermute x35, starting transfers between devices: 63.6 us -> 57.9 us  [the longest x12 30.1 us: send_turn(): lax.ppermute(send_up, 'tensor', [(j, j + 1) for j in range(k - 1, n - 1)])]
    pallas_call x4 -> x3, Pallas kernels: 11.5 us -> 6.09 us  [low_parts(): pl.pallas_call(kernel, grid_spec=pltpu.PrefetchScalarGridSpec(num_scalar_...]
    ppermute x35, waiting for transfers between devices: 41.1 us -> 38.2 us  [the longest x12 22.6 us: send_turn(): lax.ppermute(send_down, 'tensor', [(j, j - 1) for j in range(1, n - k + 1)])]
  transfers between devices with their start and end apart: 42 -> 42, of which waited for: 12 -> 9; matrix products, arithmetic and copies ran while one was open for 7% -> 7% of each run, Pallas kernels for 31% -> 29%
where the time goes in v2:
time: 290 us; the launch traced here: 288 us
  Pallas kernels  101 us (35%)
  starting transfers between devices  85.1 us (29%)
  waiting for transfers between devices  42.9 us (15%)
  local copies, waits for them, and re-layouts  40.7 us (14%)
  other arithmetic  9.39 us (3%)
  between operations  8.73 us (3%)
    pallas_call x4, Pallas kernels, project(): pl.pallas_call(kernel, grid_spec=pltpu.PrefetchScalarGridSpec(num_scalar_...  66.9 us
    ppermute x12, starting transfers between devices, send_turn(): lax.ppermute(send_up, 'tensor', [(j, j + 1) for j in range(k - 1, n - 1)])  30.1 us
    unnamed x150, local copies, waits for them, and re-layouts  26 us
    ppermute x12, waiting for transfers between devices, send_turn(): lax.ppermute(send_down, 'tensor', [(j, j - 1) for j in range(1, n - k + 1)])  22.6 us
    pallas_call x1, Pallas kernels, attend(): pl.pallas_call(kernel, grid_spec=pltpu.PrefetchScalarGridSpec(num_scalar_...  16.5 us
    ppermute x12, starting transfers between devices, send_turn(): lax.ppermute(send_down, 'tensor', [(j, j - 1) for j in range(1, n - k + 1)])  15.4 us
    ppermute x1, starting transfers between devices, on_device(): lax.ppermute(both[:rows], 'tensor', [(i, i + k) for i in range(n - k)])  12.8 us
    ppermute x9, waiting for transfers between devices, on_device(): lax.ppermute(part, 'store', [(i, (i + d) % stores) for i in range(stores)])  9.1 us
  transfers between devices with their start and end apart: 42, of which 9 were waited for; matrix products, arithmetic and copies ran while one was open for 7% of the time, Pallas kernels for 29%

profile of v2, /device:TPU:0, one launch (start us, length us, event | category | flops | bytes accessed | tf_op | source)
XLA Modules:
  0.0 288.0 jit_solution(16756172706587652957)
XLA Ops:
  0.0 2.8 fusion.8
  2.8 1.3 collective-permute-start
  4.1 1.3 collective-permute-start.1
  5.4 7.0 %collective-permute-start.2 = (bf16[128,2048]{1,0:T(8,128)(2,1)}, bf16[128,2048]{1,0:T(8,128)(2,1)}, u32[]{:S(2)}, u32[]{:S(2)}) collective-permute-start(bf16[128,2048]{1,0:T(8,128)(2,1)} %get-tuple-element.62.refs_2_), channel_id=1, source_target_pairs={{0,4},{4,8},{8,12},{1,5},{5,9},{9,13},{2,6},{6,10},{10,14},{3,7},{... | collective-permute-start | bytes 1572872 | tf_op jit(solution)/shard_map/ppermute | solution.py:499
  12.4 3.9 %collective-permute-start.7 = (bf16[128,2048]{1,0:T(8,128)(2,1)}, bf16[128,2048]{1,0:T(8,128)(2,1)}, u32[]{:S(2)}, u32[]{:S(2)}) collective-permute-start(bf16[128,2048]{1,0:T(8,128)(2,1)} %get-tuple-element.66.refs_3_), channel_id=1, source_target_pairs={{0,4},{4,8},{8,12},{1,5},{5,9},{9,13},{2,6},{6,10},{10,14},{3,7},{... | collective-permute-start | bytes 1572872 | tf_op jit(solution)/shard_map/ppermute | solution.py:499
  24.8 2.8 dynamic-slice_bitcast_fusion
  32.0 3.4 %copy-done = bf16[8192,512]{1,0:T(8,128)(2,1)S(1)} copy-done((bf16[8192,512]{1,0:T(8,128)(2,1)S(1)}, bf16[8192,512]{1,0:T(8,128)(2,1)}, u32[]{:S(2)}) %copy-start) | copy-done | bytes 8388632
  35.4 16.1 %shard_map.109 = (f32[128,2048]{1,0:T(8,128)S(1)}, f32[128,512]{1,0:T(8,128)S(1)}) custom-call(s32[5]{0:T(128)S(1)} %pad_add_fusion.2.info, bf16[128,2048]{1,0:T(8,128)(2,1)S(1)} %get-tuple-element.65.refs_0_, bf16[128,2048]{1,0:T(8,128)(2,1)} %get-tuple-element.63.refs_1_, bf16[128,2048]{1,0:T(8,128)(2,1)} %get-tuple-element.62.refs_2_, ...), custom_call_target="tpu_custom_call" | custom-call | flops 5368709120 | bytes 44040192 | tf_op jit(solution)/shard_map/pallas_call | solution.py:103
  53.2 2.0 collective-permute-start.9
  55.9 1.3 collective-permute-start.3
  57.2 5.4 %collective-permute-start.4 = (bf16[128,2048]{1,0:T(8,128)(2,1)}, bf16[128,2048]{1,0:T(8,128)(2,1)}, u32[]{:S(2)}, u32[]{:S(2)}) collective-permute-start(bf16[128,2048]{1,0:T(8,128)(2,1)} %get-tuple-element.63.refs_1_), channel_id=1, source_target_pairs={{0,4},{4,8},{8,12},{1,5},{5,9},{9,13},{2,6},{6,10},{10,14},{3,7},{... | collective-permute-start | bytes 1572872 | tf_op jit(solution)/shard_map/ppermute | solution.py:499
  62.6 1.3 collective-permute-start.13
  63.8 1.5 collective-permute-start.14
  67.4 1.6 collective-permute-start.10
  69.6 3.2 %collective-permute-done.3.refs_2_.refs_4_ = bf16[128,2048]{1,0:T(8,128)(2,1)} collective-permute-done((bf16[128,2048]{1,0:T(8,128)(2,1)}, bf16[128,2048]{1,0:T(8,128)(2,1)}, u32[]{:S(2)}, u32[]{:S(2)}) %collective-permute-start.3) | collective-permute-done | bytes 524320 | tf_op jit(solution)/shard_map/ppermute | solution.py:498
  73.2 1.3 collective-permute-start.5
  74.5 5.0 %collective-permute-start.6 = (bf16[128,2048]{1,0:T(8,128)(2,1)}, bf16[128,2048]{1,0:T(8,128)(2,1)S(1)}, u32[]{:S(2)}, u32[]{:S(2)}) collective-permute-start(bf16[128,2048]{1,0:T(8,128)(2,1)} %copy-done.13), channel_id=1, source_target_pairs={{0,4},{4,8},{8,12},{1,5},{5,9},{9,13},{2,6},{6,10},{10,14},{3,7},{... | collective-permute-start | bytes 1572872 | tf_op jit(solution)/shard_map/ppermute | solution.py:499
  79.6 4.5 %collective-permute-done.13.refs_0_ = bf16[128,2048]{1,0:T(8,128)(2,1)} collective-permute-done((bf16[128,2048]{1,0:T(8,128)(2,1)S(1)}, bf16[128,2048]{1,0:T(8,128)(2,1)}, u32[]{:S(2)}, u32[]{:S(2)}) %collective-permute-start.13) | collective-permute-done | bytes 524320 | tf_op jit(solution)/shard_map/ppermute | solution.py:498
  84.1 1.3 collective-permute-start.15
  86.2 1.6 dynamic-slice_bitcast_fusion.8
  87.8 2.2 dynamic-slice_bitcast_fusion.7
  90.8 14.8 %collective-permute-done.15.refs_4_.refs_0_ = bf16[128,2048]{1,0:T(8,128)(2,1)S(1)} collective-permute-done((bf16[128,2048]{1,0:T(8,128)(2,1)}, bf16[128,2048]{1,0:T(8,128)(2,1)S(1)}, u32[]{:S(2)}, u32[]{:S(2)}) %collective-permute-start.15) | collective-permute-done | bytes 524320 | tf_op jit(solution)/shard_map/ppermute | solution.py:498
  107.3 1.3 collective-permute-start.17
  108.5 1.5 collective-permute-start.18
  111.7 1.3 collective-permute-start.19
  113.0 1.5 collective-permute-start.20
  115.1 3.9 %collective-permute-done.31 = bf16[64,512]{1,0:T(8,128)(2,1)} collective-permute-done((bf16[64,512]{1,0:T(8,128)(2,1)}, bf16[64,512]{1,0:T(8,128)(2,1)}, u32[]{:S(2)}, u32[]{:S(2)}) %collective-permute-start.31) | collective-permute-done | bytes 65568 | tf_op jit(solution)/shard_map/ppermute | solution.py:528
  120.6 1.0 copy-done.21
  121.6 1.0 copy-done.24
  123.6 1.9 shard_map.110
  126.2 5.2 %collective-permute-done.33 = bf16[64,2048]{1,0:T(8,128)(2,1)S(1)} collective-permute-done((bf16[64,2048]{1,0:T(8,128)(2,1)S(1)}, bf16[64,2048]{1,0:T(8,128)(2,1)S(1)}, u32[]{:S(2)}, u32[]{:S(2)}) %collective-permute-start.33) | collective-permute-done | bytes 262176 | tf_op jit(solution)/shard_map/ppermute | solution.py:528
  131.4 1.3 collective-permute-start.12
  132.7 12.8 %collective-permute-start.11 = (f32[128,128]{1,0:T(8,128)S(1)}, f32[128,128]{1,0:T(8,128)S(1)}, u32[]{:S(2)}, u32[]{:S(2)}) collective-permute-start(f32[128,128]{1,0:T(8,128)S(1)} %get-tuple-element.135), channel_id=1, source_target_pairs={{0,4},{4,8},{8,12},{1,5},{5,9},{9,13},{2,6},{6,10},{10,14},{3,7},{... | collective-permute-start | bytes 196616 | tf_op jit(solution)/shard_map/ppermute | solution.py:617
  145.6 1.3 collective-permute-start.34
  146.9 1.3 collective-permute-start.21
  150.0 1.0 copy-done.12
  151.0 20.6 %shard_map.111 = (f32[256,2048]{1,0:T(8,128)S(1)}, f32[256,512]{1,0:T(8,128)S(1)}) custom-call(s32[6]{0:T(128)S(1)} %pad_add_fusion.4.info, bf16[128,2048]{1,0:T(8,128)(2,1)S(1)} %copy-done.10, bf16[128,2048]{1,0:T(8,128)(2,1)S(1)} %copy-done.25, bf16[128,2048]{1,0:T(8,128)(2,1)S(1)} %copy-done.12, bf16[128,2048]{1,0:T(8,128)(2,1)} %collective-permute-done.4.refs_5_.refs_3_, ...), custom_call_target="tpu_custom_call" | custom-call | flops 10737418240 | bytes 46137344 | tf_op jit(solution)/shard_map/pallas_call | solution.py:103
  171.8 1.3 shard_map.112
  173.1 1.3 collective-permute-start.28
  175.4 2.9 shard_map.113
  178.3 1.9 collective-permute-start.24
  180.3 4.8 %collective-permute-start.23 = (f32[128,128]{1,0:T(8,128)S(1)}, f32[128,128]{1,0:T(8,128)S(1)}, u32[]{:S(2)}, u32[]{:S(2)}) collective-permute-start(f32[128,128]{1,0:T(8,128)S(1)} %get-tuple-element.137), channel_id=1, source_target_pairs={{0,8},{4,12},{8,0},{12,4},{1,9},{5,13},{9,1},{13,5},{2,10},{6,14},... | collective-permute-start | bytes 196616 | tf_op jit(solution)/shard_map/ppermute | solution.py:632
  185.1 1.6 pad_maximum_fusion.1.refs_11_.refs_6_
  186.7 6.0 %collective-permute-done.23 = f32[128,128]{1,0:T(8,128)S(1)} collective-permute-done((f32[128,128]{1,0:T(8,128)S(1)}, f32[128,128]{1,0:T(8,128)S(1)}, u32[]{:S(2)}, u32[]{:S(2)}) %collective-permute-start.23) | collective-permute-done | bytes 65568 | tf_op jit(solution)/shard_map/ppermute | solution.py:632
  192.7 5.0 %collective-permute-start.25 = (bf16[128,128]{1,0:T(8,128)(2,1)S(1)}, bf16[128,128]{1,0:T(8,128)(2,1)S(1)}, u32[]{:S(2)}, u32[]{:S(2)}) collective-permute-start(bf16[128,128]{1,0:T(8,128)(2,1)S(1)} %get-tuple-element.108), channel_id=1, source_target_pairs={{4,0},{8,4},{12,8},{0,12},{5,1},{9,5},{13,9},{1,13},{6,2},{10,6},{... | collective-permute-start | bytes 98312 | tf_op jit(solution)/shard_map/ppermute | solution.py:639
  199.5 1.3 collective-permute-start.38
  200.7 1.5 collective-permute-start.39
  202.2 2.0 collective-permute-start.26
  204.2 1.4 collective-permute-start.27
  205.7 1.5 collective-permute-done.26
  207.1 3.2 %collective-permute-done.27 = bf16[128,128]{1,0:T(8,128)(2,1)S(1)} collective-permute-done((bf16[128,128]{1,0:T(8,128)(2,1)S(1)}, bf16[128,128]{1,0:T(8,128)(2,1)S(1)}, u32[]{:S(2)}, u32[]{:S(2)}) %collective-permute-start.27) | collective-permute-done | bytes 32800 | tf_op jit(solution)/shard_map/ppermute | solution.py:639
  211.3 3.4 %copy-done.1 = bf16[8192,512]{1,0:T(8,128)(2,1)S(1)} copy-done((bf16[8192,512]{1,0:T(8,128)(2,1)S(1)}, bf16[8192,512]{1,0:T(8,128)(2,1)}, u32[]{:S(2)}) %copy-start.1) | copy-done | bytes 8388632
  214.7 1.0 copy-done.41
  216.8 17.8 %shard_map.114 = (f32[128,2048]{1,0:T(8,128)S(1)}, f32[128,512]{1,0:T(8,128)S(1)}) custom-call(s32[5]{0:T(128)S(1)} %concatenate.38.info, bf16[128,2048]{1,0:T(8,128)(2,1)} %collective-permute-done.13.refs_0_, bf16[128,2048]{1,0:T(8,128)(2,1)} %collective-permute-done.14.refs_3_.refs_1_, bf16[128,2048]{1,0:T(8,128)(2,1)} %collective-permute-done.17.refs_1_.refs_2_, ...), custom_call_target="tpu_custom_call" | custom-call | flops 5368709120 | bytes 44040192 | tf_op jit(solution)/shard_map/pallas_call | solution.py:103
  234.6 1.3 collective-permute-start.36
  236.7 4.0 %shard_map.115 = (bf16[512,2048]{1,0:T(8,128)(2,1)S(1)}, bf16[512,256]{1,0:T(8,128)(2,1)S(1)}, bf16[512,256]{1,0:T(8,128)(2,1)S(1)}) custom-call(s32[3]{0:T(128)S(1)} %pad_add_fusion.1.info, f32[128,2048]{1,0:T(8,128)S(1)} %copy-done.39, f32[128,512]{1,0:T(8,128)S(1)} %copy-done.52, f32[256,2048]{1,0:T(8,128)S(1)} %get-tuple-element.70.refs_2_.refs_4_, ...), custom_call_target="tpu_custom_call" | custom-call | flops 671088640 | bytes 10485760 | tf_op jit(solution)/shard_map/pallas_call | solution.py:250
  240.8 1.3 copy-done.58
  242.2 2.8 collective-permute-start.40
  245.9 3.4 %copy-done.2 = bf16[8192,512]{1,0:T(8,128)(2,1)S(1)} copy-done((bf16[8192,512]{1,0:T(8,128)(2,1)S(1)}, bf16[8192,512]{1,0:T(8,128)(2,1)}, u32[]{:S(2)}) %copy-start.2) | copy-done | bytes 8388632
  249.3 12.4 %shard_map.116 = (f32[128,2048]{1,0:T(8,128)S(1)}, f32[128,512]{1,0:T(8,128)S(1)}) custom-call(s32[4]{0:T(128)S(1)} %pad_add_fusion.7.info, bf16[128,2048]{1,0:T(8,128)(2,1)S(1)} %copy-done.16, bf16[128,2048]{1,0:T(8,128)(2,1)S(1)} %copy-done.19, bf16[128,2048]{1,0:T(8,128)(2,1)S(1)} %copy-done.27, bf16[128,2048]{1,0:T(8,128)(2,1)S(1)} %copy-done.29, ...), custom_call_target="tpu_custom_call" | custom-call | flops 4026531840 | bytes 33030144 | tf_op jit(solution)/shard_map/pallas_call | solution.py:103
  261.8 1.3 shard_map.118
  263.1 1.9 collective-permute-start.41
  265.1 6.3 %shard_map.117.ql_ref = bf16[128,2048]{1,0:T(8,128)(2,1)S(1)} custom-call(s32[2]{0:T(128)S(1)} %copy-done.55, bf16[128,2048]{1,0:T(8,128)(2,1)S(1)} %collective-permute-done.36.refs_0_, bf16[128,2048]{1,0:T(8,128)(2,1)S(1)} %collective-permute-done.37.refs_1_, bf16[8192,2048]{1,0:T(8,128)(2,1)} %refs_2_.2, f32[128,2048]{1,0:T(8,128)S(1)} %get-tuple-element.100.refs_3_, ...), custom_call_target="tpu_custom_call" | custom-call | flops 1207959552 | bytes 8388608 | tf_op jit(solution)/shard_map/pallas_call | solution.py:339
  271.5 16.5 %shard_map.119 = bf16[512,2048]{1,0:T(8,128)(2,1)} custom-call(s32[3]{0:T(128)S(1)} %copy-done.57, bf16[512,2048]{1,0:T(8,128)(2,1)S(1)} %copy-done.59, bf16[128,2048]{1,0:T(8,128)(2,1)S(1)} %shard_map.117.ql_ref, bf16[512,256]{1,0:T(8,128)(2,1)S(1)} %get-tuple-element.96.m_ref, bf16[128,256]{1,0:T(8,128)(2,1)S(1)} %get-tuple-element.102.ml_ref, ...), custom_call_target="tpu_custom_call" | custom-call | flops 2147483648 | bytes 4194304 | tf_op jit(solution)/shard_map/pallas_call | solution.py:429
  (225 shorter events, 27.5 us)
Async XLA Ops:
  2.8 48.7 %copy-start.13 = (bf16[128,2048]{1,0:T(8,128)(2,1)}, bf16[128,2048]{1,0:T(8,128)(2,1)S(1)}, u32[]{:S(2)}) copy-start(bf16[128,2048]{1,0:T(8,128)(2,1)S(1)} %get-tuple-element.65.refs_0_) | copy-start | bytes 1572868
  2.8 59.8 %collective-permute-start = (bf16[128,2048]{1,0:T(8,128)(2,1)S(1)}, bf16[128,2048]{1,0:T(8,128)(2,1)S(1)}, u32[]{:S(2)}, u32[]{:S(2)}) collective-permute-start(bf16[128,2048]{1,0:T(8,128)(2,1)S(1)} %get-tuple-element.65.refs_0_), channel_id=1, source_target_pairs={{4,0},{8,4},{12,8},{5,1},{9,5},{13,9},{6,2},{10,6},{14,10},{7,3},{... | collective-permute-start | bytes 1572872 | tf_op jit(solution)/shard_map/ppermute | solution.py:498
  4.1 51.8 %collective-permute-start.1 = (bf16[128,2048]{1,0:T(8,128)(2,1)}, bf16[128,2048]{1,0:T(8,128)(2,1)S(1)}, u32[]{:S(2)}, u32[]{:S(2)}) collective-permute-start(bf16[128,2048]{1,0:T(8,128)(2,1)} %get-tuple-element.63.refs_1_), channel_id=1, source_target_pairs={{4,0},{8,4},{12,8},{5,1},{9,5},{13,9},{6,2},{10,6},{14,10},{7,3},{... | collective-permute-start | bytes 1572872 | tf_op jit(solution)/shard_map/ppermute | solution.py:498
  5.4 50.5 %collective-permute-start.2 = (bf16[128,2048]{1,0:T(8,128)(2,1)}, bf16[128,2048]{1,0:T(8,128)(2,1)}, u32[]{:S(2)}, u32[]{:S(2)}) collective-permute-start(bf16[128,2048]{1,0:T(8,128)(2,1)} %get-tuple-element.62.refs_2_), channel_id=1, source_target_pairs={{0,4},{4,8},{8,12},{1,5},{5,9},{9,13},{2,6},{6,10},{10,14},{3,7},{... | collective-permute-start | bytes 1572872 | tf_op jit(solution)/shard_map/ppermute | solution.py:499
  12.4 50.2 %collective-permute-start.7 = (bf16[128,2048]{1,0:T(8,128)(2,1)}, bf16[128,2048]{1,0:T(8,128)(2,1)}, u32[]{:S(2)}, u32[]{:S(2)}) collective-permute-start(bf16[128,2048]{1,0:T(8,128)(2,1)} %get-tuple-element.66.refs_3_), channel_id=1, source_target_pairs={{0,4},{4,8},{8,12},{1,5},{5,9},{9,13},{2,6},{6,10},{10,14},{3,7},{... | collective-permute-start | bytes 1572872 | tf_op jit(solution)/shard_map/ppermute | solution.py:499
  27.7 25.5 %collective-permute-start.8 = (bf16[128,2048]{1,0:T(8,128)(2,1)}, bf16[128,2048]{1,0:T(8,128)(2,1)S(1)}, u32[]{:S(2)}, u32[]{:S(2)}) collective-permute-start(bf16[128,2048]{1,0:T(8,128)(2,1)} %get-tuple-element.55), channel_id=1, source_target_pairs={{0,1},{1,2},{2,3},{3,0},{4,5},{5,6},{6,7},{7,4},{8,9},{9,10},{10,1... | collective-permute-start | bytes 1572872 | tf_op jit(solution)/shard_map/ppermute | solution.py:528
  30.5 21.0 %copy-start.34 = (f32[512,128]{1,0:T(8,128)}, f32[512,128]{1,0:T(8,128)S(1)}, u32[]{:S(2)}) copy-start(f32[512,128]{1,0:T(8,128)S(1)} %get-tuple-element.147.refs_14_) | copy-start | bytes 786436
  30.5 24.7 %copy-start.32 = (f32[512,128]{1,0:T(8,128)}, f32[512,128]{1,0:T(8,128)S(1)}, u32[]{:S(2)}) copy-start(f32[512,128]{1,0:T(8,128)S(1)} %get-tuple-element.105.refs_15_) | copy-start | bytes 786436
  53.2 14.2 %collective-permute-start.9 = (bf16[128,2048]{1,0:T(8,128)(2,1)}, bf16[128,2048]{1,0:T(8,128)(2,1)S(1)}, u32[]{:S(2)}, u32[]{:S(2)}) collective-permute-start(bf16[128,2048]{1,0:T(8,128)(2,1)} %get-tuple-element.67), channel_id=1, source_target_pairs={{0,2},{1,3},{2,0},{3,1},{4,6},{5,7},{6,4},{7,5},{8,10},{9,11},{10,... | collective-permute-start | bytes 1572872 | tf_op jit(solution)/shard_map/ppermute | solution.py:528
  55.9 64.7 %copy-start.11 = (bf16[128,2048]{1,0:T(8,128)(2,1)}, bf16[128,2048]{1,0:T(8,128)(2,1)S(1)}, u32[]{:S(2)}) copy-start(bf16[128,2048]{1,0:T(8,128)(2,1)S(1)} %collective-permute-done.1.refs_1_.refs_2_) | copy-start | bytes 1572868
  55.9 17.0 %collective-permute-start.3 = (bf16[128,2048]{1,0:T(8,128)(2,1)}, bf16[128,2048]{1,0:T(8,128)(2,1)}, u32[]{:S(2)}, u32[]{:S(2)}) collective-permute-start(bf16[128,2048]{1,0:T(8,128)(2,1)} %get-tuple-element.62.refs_2_), channel_id=1, source_target_pairs={{4,0},{8,4},{12,8},{5,1},{9,5},{13,9},{6,2},{10,6},{14,10},{7,3},{... | collective-permute-start | bytes 1572872 | tf_op jit(solution)/shard_map/ppermute | solution.py:498
  57.2 16.0 %collective-permute-start.4 = (bf16[128,2048]{1,0:T(8,128)(2,1)}, bf16[128,2048]{1,0:T(8,128)(2,1)}, u32[]{:S(2)}, u32[]{:S(2)}) collective-permute-start(bf16[128,2048]{1,0:T(8,128)(2,1)} %get-tuple-element.63.refs_1_), channel_id=1, source_target_pairs={{0,4},{4,8},{8,12},{1,5},{5,9},{9,13},{2,6},{6,10},{10,14},{3,7},{... | collective-permute-start | bytes 1572872 | tf_op jit(solution)/shard_map/ppermute | solution.py:499
  62.5 58.0 %copy-start.9 = (bf16[128,2048]{1,0:T(8,128)(2,1)}, bf16[128,2048]{1,0:T(8,128)(2,1)S(1)}, u32[]{:S(2)}) copy-start(bf16[128,2048]{1,0:T(8,128)(2,1)S(1)} %collective-permute-done.refs_0_) | copy-start | bytes 1572868
  62.6 21.5 %collective-permute-start.13 = (bf16[128,2048]{1,0:T(8,128)(2,1)S(1)}, bf16[128,2048]{1,0:T(8,128)(2,1)}, u32[]{:S(2)}, u32[]{:S(2)}) collective-permute-start(bf16[128,2048]{1,0:T(8,128)(2,1)S(1)} %collective-permute-done.refs_0_), channel_id=1, source_target_pairs={{4,0},{8,4},{5,1},{9,5},{6,2},{10,6},{7,3},{11,7},{20,16},{24,20},... | collective-permute-start | bytes 1572872 | tf_op jit(solution)/shard_map/ppermute | solution.py:498
  63.8 20.3 %collective-permute-start.14 = (bf16[128,2048]{1,0:T(8,128)(2,1)}, bf16[128,2048]{1,0:T(8,128)(2,1)}, u32[]{:S(2)}, u32[]{:S(2)}) collective-permute-start(bf16[128,2048]{1,0:T(8,128)(2,1)} %collective-permute-done.7.refs_7_), channel_id=1, source_target_pairs={{4,8},{8,12},{5,9},{9,13},{6,10},{10,14},{7,11},{11,15},{20,24},{2... | collective-permute-start | bytes 1572872 | tf_op jit(solution)/shard_map/ppermute | solution.py:499
  67.4 58.1 %copy-start.4 = (bf16[128,2048]{1,0:T(8,128)(2,1)}, bf16[128,2048]{1,0:T(8,128)(2,1)S(1)}, u32[]{:S(2)}) copy-start(bf16[128,2048]{1,0:T(8,128)(2,1)S(1)} %collective-permute-done.9.refs_10_.refs_3_) | copy-start | bytes 1572868
  67.4 22.7 %collective-permute-start.10 = (bf16[128,2048]{1,0:T(8,128)(2,1)}, bf16[128,2048]{1,0:T(8,128)(2,1)S(1)}, u32[]{:S(2)}, u32[]{:S(2)}) collective-permute-start(bf16[128,2048]{1,0:T(8,128)(2,1)} %get-tuple-element.68), channel_id=1, source_target_pairs={{0,3},{1,0},{2,1},{3,2},{4,7},{5,4},{6,5},{7,6},{8,11},{9,8},{10,9... | collective-permute-start | bytes 1572872 | tf_op jit(solution)/shard_map/ppermute | solution.py:528
  73.2 36.8 %collective-permute-start.5 = (bf16[128,2048]{1,0:T(8,128)(2,1)}, bf16[128,2048]{1,0:T(8,128)(2,1)S(1)}, u32[]{:S(2)}, u32[]{:S(2)}) collective-permute-start(bf16[128,2048]{1,0:T(8,128)(2,1)} %get-tuple-element.66.refs_3_), channel_id=1, source_target_pairs={{4,0},{8,4},{12,8},{5,1},{9,5},{13,9},{6,2},{10,6},{14,10},{7,3},{... | collective-permute-start | bytes 1572872 | tf_op jit(solution)/shard_map/ppermute | solution.py:498
  74.5 36.4 %collective-permute-start.6 = (bf16[128,2048]{1,0:T(8,128)(2,1)}, bf16[128,2048]{1,0:T(8,128)(2,1)S(1)}, u32[]{:S(2)}, u32[]{:S(2)}) collective-permute-start(bf16[128,2048]{1,0:T(8,128)(2,1)} %copy-done.13), channel_id=1, source_target_pairs={{0,4},{4,8},{8,12},{1,5},{5,9},{9,13},{2,6},{6,10},{10,14},{3,7},{... | collective-permute-start | bytes 1572872 | tf_op jit(solution)/shard_map/ppermute | solution.py:499
  84.1 21.5 %collective-permute-start.15 = (bf16[128,2048]{1,0:T(8,128)(2,1)}, bf16[128,2048]{1,0:T(8,128)(2,1)S(1)}, u32[]{:S(2)}, u32[]{:S(2)}) collective-permute-start(bf16[128,2048]{1,0:T(8,128)(2,1)} %collective-permute-done.13.refs_0_), channel_id=1, source_target_pairs={{4,0},{5,1},{6,2},{7,3},{20,16},{21,17},{22,18},{23,19}} | collective-permute-start | bytes 1572872 | tf_op jit(solution)/shard_map/ppermute | solution.py:498
  85.4 21.1 %collective-permute-start.16 = (bf16[128,2048]{1,0:T(8,128)(2,1)}, bf16[128,2048]{1,0:T(8,128)(2,1)S(1)}, u32[]{:S(2)}, u32[]{:S(2)}) collective-permute-start(bf16[128,2048]{1,0:T(8,128)(2,1)} %collective-permute-done.14.refs_3_.refs_1_), channel_id=1, source_target_pairs={{8,12},{9,13},{10,14},{11,15},{24,28},{25,29},{26,30},{27,31}} | collective-permute-start | bytes 1572872 | tf_op jit(solution)/shard_map/ppermute | solution.py:499
  90.0 35.5 %copy-start.6 = (bf16[128,2048]{1,0:T(8,128)(2,1)}, bf16[128,2048]{1,0:T(8,128)(2,1)S(1)}, u32[]{:S(2)}) copy-start(bf16[128,2048]{1,0:T(8,128)(2,1)S(1)} %collective-permute-done.10.refs_11_.refs_4_) | copy-start | bytes 1572868
  90.0 24.4 %collective-permute-start.30 = (bf16[64,512]{1,0:T(8,128)(2,1)S(1)}, bf16[64,512]{1,0:T(8,128)(2,1)S(1)}, u32[]{:S(2)}, u32[]{:S(2)}) collective-permute-start(bf16[64,512]{1,0:T(8,128)(2,1)S(1)} %get-tuple-element.87), channel_id=1, source_target_pairs={{0,1},{1,2},{2,3},{3,0},{4,5},{5,6},{6,7},{7,4},{8,9},{9,10},{10,1... | collective-permute-start | bytes 196616 | tf_op jit(solution)/shard_map/ppermute | solution.py:528
  107.3 25.4 %collective-permute-start.17 = (bf16[128,2048]{1,0:T(8,128)(2,1)S(1)}, bf16[128,2048]{1,0:T(8,128)(2,1)}, u32[]{:S(2)}, u32[]{:S(2)}) collective-permute-start(bf16[128,2048]{1,0:T(8,128)(2,1)S(1)} %collective-permute-done.1.refs_1_.refs_2_), channel_id=1, source_target_pairs={{4,0},{8,4},{5,1},{9,5},{6,2},{10,6},{7,3},{11,7},{20,16},{24,20},... | collective-permute-start | bytes 1572872 | tf_op jit(solution)/shard_map/ppermute | solution.py:498
  108.5 37.0 %collective-permute-start.18 = (bf16[128,2048]{1,0:T(8,128)(2,1)}, bf16[128,2048]{1,0:T(8,128)(2,1)}, u32[]{:S(2)}, u32[]{:S(2)}) collective-permute-start(bf16[128,2048]{1,0:T(8,128)(2,1)} %collective-permute-done.2.refs_6_.refs_5_), channel_id=1, source_target_pairs={{4,8},{8,12},{5,9},{9,13},{6,10},{10,14},{7,11},{11,15},{20,24},{2... | collective-permute-start | bytes 1572872 | tf_op jit(solution)/shard_map/ppermute | solution.py:499
  111.7 35.2 %collective-permute-start.19 = (bf16[128,2048]{1,0:T(8,128)(2,1)}, bf16[128,2048]{1,0:T(8,128)(2,1)}, u32[]{:S(2)}, u32[]{:S(2)}) collective-permute-start(bf16[128,2048]{1,0:T(8,128)(2,1)} %collective-permute-done.3.refs_2_.refs_4_), channel_id=1, source_target_pairs={{4,0},{8,4},{5,1},{9,5},{6,2},{10,6},{7,3},{11,7},{20,16},{24,20},... | collective-permute-start | bytes 1572872 | tf_op jit(solution)/shard_map/ppermute | solution.py:498
  113.0 33.9 %collective-permute-start.20 = (bf16[128,2048]{1,0:T(8,128)(2,1)}, bf16[128,2048]{1,0:T(8,128)(2,1)}, u32[]{:S(2)}, u32[]{:S(2)}) collective-permute-start(bf16[128,2048]{1,0:T(8,128)(2,1)} %collective-permute-done.4.refs_5_.refs_3_), channel_id=1, source_target_pairs={{4,8},{8,12},{5,9},{9,13},{6,10},{10,14},{7,11},{11,15},{20,24},{2... | collective-permute-start | bytes 1572872 | tf_op jit(solution)/shard_map/ppermute | solution.py:499
  114.5 4.6 %collective-permute-start.31 = (bf16[64,512]{1,0:T(8,128)(2,1)}, bf16[64,512]{1,0:T(8,128)(2,1)}, u32[]{:S(2)}, u32[]{:S(2)}) collective-permute-start(bf16[64,512]{1,0:T(8,128)(2,1)} %get-tuple-element.88), channel_id=1, source_target_pairs={{0,2},{1,3},{2,0},{3,1},{4,6},{5,7},{6,4},{7,5},{8,10},{9,11},{10,... | collective-permute-start | bytes 196616 | tf_op jit(solution)/shard_map/ppermute | solution.py:528
  119.0 6.5 %collective-permute-start.32 = (bf16[64,512]{1,0:T(8,128)(2,1)}, bf16[64,512]{1,0:T(8,128)(2,1)}, u32[]{:S(2)}, u32[]{:S(2)}) collective-permute-start(bf16[64,512]{1,0:T(8,128)(2,1)} %get-tuple-element.89), channel_id=1, source_target_pairs={{0,3},{1,0},{2,1},{3,2},{4,7},{5,4},{6,5},{7,6},{8,11},{9,8},{10,9... | collective-permute-start | bytes 196616 | tf_op jit(solution)/shard_map/ppermute | solution.py:528
  123.6 22.0 %copy-start.62 = (bf16[64,2048]{1,0:T(8,128)(2,1)S(1)}, bf16[64,2048]{1,0:T(8,128)(2,1)}, u32[]{:S(2)}) copy-start(bf16[64,2048]{1,0:T(8,128)(2,1)} %get-tuple-element.91) | copy-start | bytes 786436
  123.6 25.3 %copy-start.22 = (bf16[128,2048]{1,0:T(8,128)(2,1)S(1)}, bf16[128,2048]{1,0:T(8,128)(2,1)}, u32[]{:S(2)}) copy-start(bf16[128,2048]{1,0:T(8,128)(2,1)} %copy-done.20) | copy-start | bytes 1572868
  123.6 25.4 %copy-start.25 = (bf16[128,2048]{1,0:T(8,128)(2,1)S(1)}, bf16[128,2048]{1,0:T(8,128)(2,1)}, u32[]{:S(2)}) copy-start(bf16[128,2048]{1,0:T(8,128)(2,1)} %copy-done.23) | copy-start | bytes 1572868
  125.5 5.8 %collective-permute-start.33 = (bf16[64,2048]{1,0:T(8,128)(2,1)S(1)}, bf16[64,2048]{1,0:T(8,128)(2,1)S(1)}, u32[]{:S(2)}, u32[]{:S(2)}) collective-permute-start(bf16[64,2048]{1,0:T(8,128)(2,1)S(1)} %copy-done.63), channel_id=1, source_target_pairs={{0,1},{1,2},{2,3},{3,0},{4,5},{5,6},{6,7},{7,4},{8,9},{9,10},{10,1... | collective-permute-start | bytes 786440 | tf_op jit(solution)/shard_map/ppermute | solution.py:528
  131.4 46.9 %collective-permute-start.12 = (f32[128,128]{1,0:T(8,128)S(1)}, f32[128,128]{1,0:T(8,128)S(1)}, u32[]{:S(2)}, u32[]{:S(2)}) collective-permute-start(f32[128,128]{1,0:T(8,128)S(1)} %get-tuple-element.136), channel_id=1, source_target_pairs={{4,0},{8,4},{12,8},{5,1},{9,5},{13,9},{6,2},{10,6},{14,10},{7,3},{... | collective-permute-start | bytes 196616 | tf_op jit(solution)/shard_map/ppermute | solution.py:618
  132.7 39.0 %copy-start.56 = (s32[2]{0:T(128)S(1)}, s32[2]{0:T(128)}, u32[]{:S(2)}) copy-start(s32[2]{0:T(128)} %pad_add_fusion.5.info) | copy-start | bytes 28
  132.7 39.0 %copy-start.3 = (bf16[128,8192]{1,0:T(8,128)(2,1)S(1)}, bf16[128,8192]{1,0:T(8,128)(2,1)}, u32[]{:S(2)}) copy-start(bf16[128,8192]{1,0:T(8,128)(2,1)} %refs_0_.1) | copy-start | bytes 6291460
  132.7 39.0 %copy-start.5 = (bf16[128,2048]{1,0:T(8,128)(2,1)S(1)}, bf16[128,2048]{1,0:T(8,128)(2,1)}, u32[]{:S(2)}) copy-start(bf16[128,2048]{1,0:T(8,128)(2,1)} %copy-done.4) | copy-start | bytes 1572868
  132.7 39.0 %copy-start.7 = (bf16[128,2048]{1,0:T(8,128)(2,1)S(1)}, bf16[128,2048]{1,0:T(8,128)(2,1)}, u32[]{:S(2)}) copy-start(bf16[128,2048]{1,0:T(8,128)(2,1)} %copy-done.6) | copy-start | bytes 1572868
  132.7 47.5 %collective-permute-start.11 = (f32[128,128]{1,0:T(8,128)S(1)}, f32[128,128]{1,0:T(8,128)S(1)}, u32[]{:S(2)}, u32[]{:S(2)}) collective-permute-start(f32[128,128]{1,0:T(8,128)S(1)} %get-tuple-element.135), channel_id=1, source_target_pairs={{0,4},{4,8},{8,12},{1,5},{5,9},{9,13},{2,6},{6,10},{10,14},{3,7},{... | collective-permute-start | bytes 196616 | tf_op jit(solution)/shard_map/ppermute | solution.py:617
  145.6 27.5 %collective-permute-start.34 = (bf16[64,2048]{1,0:T(8,128)(2,1)S(1)}, bf16[64,2048]{1,0:T(8,128)(2,1)S(1)}, u32[]{:S(2)}, u32[]{:S(2)}) collective-permute-start(bf16[64,2048]{1,0:T(8,128)(2,1)S(1)} %copy-done.62), channel_id=1, source_target_pairs={{0,2},{1,3},{2,0},{3,1},{4,6},{5,7},{6,4},{7,5},{8,10},{9,11},{10,... | collective-permute-start | bytes 786440 | tf_op jit(solution)/shard_map/ppermute | solution.py:528
  146.9 27.5 %collective-permute-start.21 = (bf16[128,2048]{1,0:T(8,128)(2,1)}, bf16[128,2048]{1,0:T(8,128)(2,1)S(1)}, u32[]{:S(2)}, u32[]{:S(2)}) collective-permute-start(bf16[128,2048]{1,0:T(8,128)(2,1)} %collective-permute-done.17.refs_1_.refs_2_), channel_id=1, source_target_pairs={{4,0},{5,1},{6,2},{7,3},{20,16},{21,17},{22,18},{23,19}} | collective-permute-start | bytes 1572872 | tf_op jit(solution)/shard_map/ppermute | solution.py:498
  148.2 27.1 %collective-permute-start.22 = (bf16[128,2048]{1,0:T(8,128)(2,1)}, bf16[128,2048]{1,0:T(8,128)(2,1)S(1)}, u32[]{:S(2)}, u32[]{:S(2)}) collective-permute-start(bf16[128,2048]{1,0:T(8,128)(2,1)} %collective-permute-done.18.refs_2_.refs_3_), channel_id=1, source_target_pairs={{8,12},{9,13},{10,14},{11,15},{24,28},{25,29},{26,30},{27,31}} | collective-permute-start | bytes 1572872 | tf_op jit(solution)/shard_map/ppermute | solution.py:499
  151.0 20.7 %copy-start.48 = (f32[128,4]{1,0:T(8,128)S(1)}, f32[128,4]{1,0:T(8,128)}, u32[]{:S(2)}) copy-start(f32[128,4]{1,0:T(8,128)} %get-tuple-element.130.refs_5_) | copy-start | bytes 6148
  173.1 24.7 %collective-permute-start.28 = (bf16[128,2048]{1,0:T(8,128)(2,1)S(1)}, bf16[128,2048]{1,0:T(8,128)(2,1)S(1)}, u32[]{:S(2)}, u32[]{:S(2)}) collective-permute-start(bf16[128,2048]{1,0:T(8,128)(2,1)S(1)} %copy-done.22), channel_id=1, source_target_pairs={{4,0},{8,4},{5,1},{9,5},{6,2},{10,6},{7,3},{11,7},{20,16},{24,20},... | collective-permute-start | bytes 1572872 | tf_op jit(solution)/shard_map/ppermute | solution.py:498
  174.4 23.3 %copy-start.60 = (bf16[64,2048]{1,0:T(8,128)(2,1)S(1)}, bf16[64,2048]{1,0:T(8,128)(2,1)}, u32[]{:S(2)}) copy-start(bf16[64,2048]{1,0:T(8,128)(2,1)} %get-tuple-element.113) | copy-start | bytes 786436
  174.4 24.2 %collective-permute-start.29 = (bf16[128,2048]{1,0:T(8,128)(2,1)S(1)}, bf16[128,2048]{1,0:T(8,128)(2,1)S(1)}, u32[]{:S(2)}, u32[]{:S(2)}) collective-permute-start(bf16[128,2048]{1,0:T(8,128)(2,1)S(1)} %copy-done.25), channel_id=1, source_target_pairs={{4,8},{8,12},{5,9},{9,13},{6,10},{10,14},{7,11},{11,15},{20,24},{2... | collective-permute-start | bytes 1572872 | tf_op jit(solution)/shard_map/ppermute | solution.py:499
  175.3 22.4 %collective-permute-start.35 = (bf16[64,2048]{1,0:T(8,128)(2,1)S(1)}, bf16[64,2048]{1,0:T(8,128)(2,1)S(1)}, u32[]{:S(2)}, u32[]{:S(2)}) collective-permute-start(bf16[64,2048]{1,0:T(8,128)(2,1)S(1)} %copy-done.61), channel_id=1, source_target_pairs={{0,3},{1,0},{2,1},{3,2},{4,7},{5,4},{6,5},{7,6},{8,11},{9,8},{10,9... | collective-permute-start | bytes 786440 | tf_op jit(solution)/shard_map/ppermute | solution.py:528
  178.3 8.3 %collective-permute-start.24 = (f32[128,128]{1,0:T(8,128)S(1)}, f32[128,128]{1,0:T(8,128)S(1)}, u32[]{:S(2)}, u32[]{:S(2)}) collective-permute-start(f32[128,128]{1,0:T(8,128)S(1)} %get-tuple-element.138), channel_id=1, source_target_pairs={{0,12},{12,0},{1,13},{13,1},{2,14},{14,2},{3,15},{15,3},{16,28},{2... | collective-permute-start | bytes 196616 | tf_op jit(solution)/shard_map/ppermute | solution.py:632
  180.3 12.4 %collective-permute-start.23 = (f32[128,128]{1,0:T(8,128)S(1)}, f32[128,128]{1,0:T(8,128)S(1)}, u32[]{:S(2)}, u32[]{:S(2)}) collective-permute-start(f32[128,128]{1,0:T(8,128)S(1)} %get-tuple-element.137), channel_id=1, source_target_pairs={{0,8},{4,12},{8,0},{12,4},{1,9},{5,13},{9,1},{13,5},{2,10},{6,14},... | collective-permute-start | bytes 196616 | tf_op jit(solution)/shard_map/ppermute | solution.py:632
  192.7 12.9 %collective-permute-start.25 = (bf16[128,128]{1,0:T(8,128)(2,1)S(1)}, bf16[128,128]{1,0:T(8,128)(2,1)S(1)}, u32[]{:S(2)}, u32[]{:S(2)}) collective-permute-start(bf16[128,128]{1,0:T(8,128)(2,1)S(1)} %get-tuple-element.108), channel_id=1, source_target_pairs={{4,0},{8,4},{12,8},{0,12},{5,1},{9,5},{13,9},{1,13},{6,2},{10,6},{... | collective-permute-start | bytes 98312 | tf_op jit(solution)/shard_map/ppermute | solution.py:639
  199.5 46.4 %collective-permute-start.38 = (bf16[128,2048]{1,0:T(8,128)(2,1)}, bf16[128,2048]{1,0:T(8,128)(2,1)}, u32[]{:S(2)}, u32[]{:S(2)}) collective-permute-start(bf16[128,2048]{1,0:T(8,128)(2,1)} %collective-permute-done.19.refs_4_), channel_id=1, source_target_pairs={{4,0},{5,1},{6,2},{7,3},{20,16},{21,17},{22,18},{23,19}} | collective-permute-start | bytes 1572872 | tf_op jit(solution)/shard_map/ppermute | solution.py:498
  200.7 45.1 %collective-permute-start.39 = (bf16[128,2048]{1,0:T(8,128)(2,1)}, bf16[128,2048]{1,0:T(8,128)(2,1)}, u32[]{:S(2)}, u32[]{:S(2)}) collective-permute-start(bf16[128,2048]{1,0:T(8,128)(2,1)} %collective-permute-done.20.refs_5_), channel_id=1, source_target_pairs={{8,12},{9,13},{10,14},{11,15},{24,28},{25,29},{26,30},{27,31}} | collective-permute-start | bytes 1572872 | tf_op jit(solution)/shard_map/ppermute | solution.py:499
  202.2 4.9 %collective-permute-start.26 = (bf16[128,128]{1,0:T(8,128)(2,1)S(1)}, bf16[128,128]{1,0:T(8,128)(2,1)S(1)}, u32[]{:S(2)}, u32[]{:S(2)}) collective-permute-start(bf16[128,128]{1,0:T(8,128)(2,1)S(1)} %get-tuple-element.108), channel_id=1, source_target_pairs={{8,0},{12,4},{0,8},{4,12},{9,1},{13,5},{1,9},{5,13},{10,2},{14,6},... | collective-permute-start | bytes 98312 | tf_op jit(solution)/shard_map/ppermute | solution.py:639
  204.2 6.1 %collective-permute-start.27 = (bf16[128,128]{1,0:T(8,128)(2,1)S(1)}, bf16[128,128]{1,0:T(8,128)(2,1)S(1)}, u32[]{:S(2)}, u32[]{:S(2)}) collective-permute-start(bf16[128,128]{1,0:T(8,128)(2,1)S(1)} %get-tuple-element.108), channel_id=1, source_target_pairs={{12,0},{0,4},{4,8},{8,12},{13,1},{1,5},{5,9},{9,13},{14,2},{2,6},{... | collective-permute-start | bytes 98312 | tf_op jit(solution)/shard_map/ppermute | solution.py:639
  216.7 19.9 %copy-start.35 = (f32[512,128]{1,0:T(8,128)S(1)}, f32[512,128]{1,0:T(8,128)}, u32[]{:S(2)}) copy-start(f32[512,128]{1,0:T(8,128)} %copy-done.34) | copy-start | bytes 786436
  216.7 19.9 %copy-start.36 = (f32[512,128]{1,0:T(8,128)S(1)}, f32[512,128]{1,0:T(8,128)}, u32[]{:S(2)}) copy-start(f32[512,128]{1,0:T(8,128)} %get-tuple-element.106.refs_13_) | copy-start | bytes 786436
  216.8 19.9 %copy-start.37 = (f32[512,128]{1,0:T(8,128)S(1)}, f32[512,128]{1,0:T(8,128)}, u32[]{:S(2)}) copy-start(f32[512,128]{1,0:T(8,128)} %get-tuple-element.146.refs_12_) | copy-start | bytes 786436
  216.8 19.9 %copy-start.39 = (f32[128,2048]{1,0:T(8,128)S(1)}, f32[128,2048]{1,0:T(8,128)}, u32[]{:S(2)}) copy-start(f32[128,2048]{1,0:T(8,128)} %copy-done.38) | copy-start | bytes 3145732
  216.8 19.9 %copy-start.44 = (bf16[512,128]{1,0:T(8,128)(2,1)S(1)}, bf16[512,128]{1,0:T(8,128)(2,1)}, u32[]{:S(2)}) copy-start(bf16[512,128]{1,0:T(8,128)(2,1)} %constant_dynamic-slice_fusion.4.refs_8_) | copy-start | bytes 393220
  216.8 19.9 %copy-start.52 = (f32[128,512]{1,0:T(8,128)S(1)}, f32[128,512]{1,0:T(8,128)}, u32[]{:S(2)}) copy-start(f32[128,512]{1,0:T(8,128)} %copy-done.51) | copy-start | bytes 786436
  234.6 27.2 %collective-permute-start.36 = (bf16[128,2048]{1,0:T(8,128)(2,1)S(1)}, bf16[128,2048]{1,0:T(8,128)(2,1)S(1)}, u32[]{:S(2)}, u32[]{:S(2)}) collective-permute-start(bf16[128,2048]{1,0:T(8,128)(2,1)S(1)} %copy-done.41), channel_id=1, source_target_pairs={{4,0},{5,1},{6,2},{7,3},{20,16},{21,17},{22,18},{23,19}} | collective-permute-start | bytes 1572872 | tf_op jit(solution)/shard_map/ppermute | solution.py:498
  235.9 25.9 %collective-permute-start.37 = (bf16[128,2048]{1,0:T(8,128)(2,1)S(1)}, bf16[128,2048]{1,0:T(8,128)(2,1)S(1)}, u32[]{:S(2)}, u32[]{:S(2)}) collective-permute-start(bf16[128,2048]{1,0:T(8,128)(2,1)S(1)} %copy-done.43), channel_id=1, source_target_pairs={{8,12},{9,13},{10,14},{11,15},{24,28},{25,29},{26,30},{27,31}} | collective-permute-start | bytes 1572872 | tf_op jit(solution)/shard_map/ppermute | solution.py:499
  242.2 29.3 %collective-permute-start.40 = (bf16[512,256]{1,0:T(8,128)(2,1)S(1)}, bf16[512,256]{1,0:T(8,128)(2,1)S(1)}, u32[]{:S(2)}, u32[]{:S(2)}) collective-permute-start(bf16[512,256]{1,0:T(8,128)(2,1)S(1)} %get-tuple-element.103), channel_id=1, source_target_pairs={{0,4},{4,0},{8,12},{12,8},{1,5},{5,1},{9,13},{13,9},{2,6},{6,2},{1... | collective-permute-start | bytes 786440 | tf_op jit(solution)/shard_map/ppermute | solution.py:677
  263.1 8.3 %collective-permute-start.41 = (bf16[128,256]{1,0:T(8,128)(2,1)S(1)}, bf16[128,256]{1,0:T(8,128)(2,1)S(1)}, u32[]{:S(2)}, u32[]{:S(2)}) collective-permute-start(bf16[128,256]{1,0:T(8,128)(2,1)S(1)} %get-tuple-element.104), channel_id=1, source_target_pairs={{0,4},{12,8},{1,5},{13,9},{2,6},{14,10},{3,7},{15,11},{16,20},{28,... | collective-permute-start | bytes 196616 | tf_op jit(solution)/shard_map/ppermute | solution.py:702
  (50 other events, 286.1 us)

commit v3 on v2

--- a/solution.py
+++ b/solution.py
@@ -20,54 +20,105 @@
 
 CHUNKS = 4
 TILE = 128
-VMEM_LIMIT = 40 * 2**20
+MIB = 2**20
 F32 = jnp.float32
 BF16 = jnp.bfloat16
-ANY = pl.BlockSpec(memory_space=pltpu.HBM)
+ANY = pl.BlockSpec(memory_space=pl.ANY)
 
 
 def after(arrays, *others):
     return lax.optimization_barrier((arrays, others))[0]
 
 
-def params():
-    return pltpu.CompilerParams(vmem_limit_bytes=VMEM_LIMIT)
+def params(held):
+    return pltpu.CompilerParams(vmem_limit_bytes=max(int(held) + 8 * MIB, 58 * MIB))
 
 
 def whole(shape):
     return pl.BlockSpec(shape, lambda *_: (0,) * len(shape))
 
 
-def start_picked(candidates, pick, target, semaphore, columns=None):
-    def start(source):
-        view = source if columns is None else source.at[:, columns]
-        pltpu.make_async_copy(view, target, semaphore).start()
+def unique(arrays):
+    kept, places = [], []
+    for x in arrays:
+        at = next((i for i, y in enumerate(kept) if y is x), len(kept))
+        if at == len(kept):
+            kept.append(x)
+        places.append(at)
+    return kept, places
+
+
+def start_picked(candidates, pick, width, target, semaphore):
+    def start(source, first):
+        pltpu.make_async_copy(source.at[:, pl.ds(first, width)], target, semaphore).start()
 
     if len(candidates) == 1:
-        start(candidates[0])
+        start(*candidates[0])
         return
-    for index, source in enumerate(candidates):
-        pl.when(pick == index)(functools.partial(start, source))
-
-
-def project(candidates, picks, chunk_ids, weights, starts=None):
+    for index, (source, first) in enumerate(candidates):
+        pl.when(pick == index)(functools.partial(start, source, first))
+
+
+def pack(down_maps, up_query, up_keyval, local):
+    stores = local.shape[0]
+    _, down_rows, width = down_maps.shape
+    _, rank, keyval_width = up_keyval.shape
+    cut = width // keyval_width
+    strip = rank // cut
+
+    def kernel(rows, down_ref, upq_ref, upkv_ref, *rest):
+        outs, sems = rest[:stores], rest[stores]
+        copies = []
+        for d in range(stores):
+            out = outs[d]
+            copies.append((down_ref.at[rows[d]], out.at[pl.ds(0, down_rows), :]))
+            copies.append((upq_ref.at[rows[d]], out.at[pl.ds(down_rows, rank), :]))
+            for i in range(cut):
+                copies.append(
+                    (
+                        upkv_ref.at[rows[d], pl.ds(i * strip, strip), :],
+                        out.at[
+                            pl.ds(down_rows + rank, strip), pl.ds(i * keyval_width, keyval_width)
+                        ],
+                    )
+                )
+        copies = [
+            pltpu.make_async_copy(source, target, sems.at[i])
+            for i, (source, target) in enumerate(copies)
+        ]
+        for copy in copies:
+            copy.start()
+        for copy in copies:
+            copy.wait()
+
+    return pl.pallas_call(
+        kernel,
+        grid_spec=pltpu.PrefetchScalarGridSpec(
+            num_scalar_prefetch=1,
+            grid=(1,),
+            in_specs=[ANY] * 3,
+            out_specs=[ANY] * stores,
+            scratch_shapes=[pltpu.SemaphoreType.DMA((stores * (2 + cut),))],
+        ),
+        out_shape=[jax.ShapeDtypeStruct((down_rows + rank + strip, width), BF16)] * stores,
+        compiler_params=params(0),
+    )(local, down_maps, up_query, up_keyval)
+
+
+def project(candidates, picks, chunk_ids, chunk, weights):
     steps, groups = len(candidates), len(candidates[0])
-    rows, chunk = candidates[0][0][0].shape
+    rows = candidates[0][0][0][0].shape[0]
     block = min(1024, chunk)
     sub = chunk // block
-    flat = [x for at_chunk in candidates for group in at_chunk for x in group]
+    arrays, places = unique([x for a in candidates for group in a for x, _ in group])
     widths = [w.shape[1] for w in weights]
     count = len(weights)
 
     def kernel(info, *refs):
-        tokens_in = iter(refs[: len(flat)])
-        sources = [[[next(tokens_in) for _ in group] for group in at_chunk] for at_chunk in candidates]
-        rest = refs[len(flat) :]
-        weight_refs, rest = rest[:count], rest[count:]
-        start_refs = ()
-        if starts is not None:
-            start_refs, rest = rest[:count], rest[count:]
-        out_refs, (held, sems) = rest[:count], rest[count:]
+        place = iter(places)
+        sources = [[[(refs[next(place)], c) for _, c in group] for group in a] for a in candidates]
+        rest = refs[len(arrays) :]
+        weight_refs, out_refs, (held, sems) = rest[:count], rest[count : 2 * count], rest[2 * count :]
         step = pl.program_id(0)
         at = step // sub
 
@@ -75,15 +126,16 @@
         def _():
             for a in range(steps):
                 for r in range(groups):
-                    start_picked(
-                        sources[a][r], info[r], held.at[a, pl.ds(r * rows, rows), :], sems.at[a, r]
-                    )
+                    target = held.at[a, pl.ds(r * rows, rows), :]
+                    start_picked(sources[a][r], info[r], chunk, target, sems.at[a, r])
 
         @pl.when(step % sub == 0)
         def _():
             for r in range(groups):
                 pltpu.make_async_copy(
-                    sources[0][r][0], held.at[at, pl.ds(r * rows, rows), :], sems.at[at, r]
+                    sources[0][r][0][0].at[:, pl.ds(0, chunk)],
+                    held.at[at, pl.ds(r * rows, rows), :],
+                    sems.at[at, r],
                 ).wait()
 
         part = held[at, :, pl.ds(pl.multiple_of((step % sub) * block, block), block)]
@@ -92,7 +144,7 @@
 
             @pl.when(step == 0)
             def _(i=i, product=product):
-                out_refs[i][...] = product if starts is None else start_refs[i][...] + product
+                out_refs[i][...] = product
 
             @pl.when(step > 0)
             def _(i=i, product=product):
@@ -100,19 +152,18 @@
 
     height = groups * rows
     info = jnp.concatenate([jnp.asarray(picks, jnp.int32), jnp.asarray(chunk_ids, jnp.int32)])
-    results = pl.pallas_call(
+    return pl.pallas_call(
         kernel,
         grid_spec=pltpu.PrefetchScalarGridSpec(
             num_scalar_prefetch=1,
             grid=(steps * sub,),
-            in_specs=[ANY] * len(flat)
+            in_specs=[ANY] * len(arrays)
             + [
                 pl.BlockSpec(
                     (block, w), lambda g, info: (info[groups + g // sub] * sub + g % sub, 0)
                 )
                 for w in widths
-            ]
-            + ([whole((height, w)) for w in widths] if starts is not None else []),
+            ],
             out_specs=[whole((height, w)) for w in widths],
             scratch_shapes=[
                 pltpu.VMEM((steps, height, chunk), BF16),
@@ -120,67 +171,96 @@
             ],
         ),
         out_shape=[jax.ShapeDtypeStruct((height, w), F32) for w in widths],
-        compiler_params=params(),
+        compiler_params=params(
+            2 * steps * height * chunk + (4 * block + 8 * height) * sum(widths)
+        ),
         cost_estimate=pl.CostEstimate(
             flops=2 * height * steps * chunk * sum(widths),
             bytes_accessed=2 * steps * chunk * (sum(widths) + height),
             transcendentals=0,
         ),
-    )(info, *flat, *weights, *(starts or []))
-    return results
-
-
-def low_parts(candidates, pick, offset, width, downs, member_groups):
-    groups = len(candidates)
-    rows = candidates[0][0].shape[0]
-    flat = [x for group in candidates for x in group]
-    holders = len(downs)
-    rank = downs[0].shape[0]
-    members = jnp.concatenate(member_groups, axis=0)
+    )(info, *arrays, *weights)
+
+
+def low_parts(slots, pick, width, packed, members):
+    arrays, places = unique([x for group, _, _ in slots for x, _ in group])
+    count, holders = len(slots), len(packed)
+    rows = arrays[0].shape[0]
+    total = members.shape[0]
+    rank = 2 * ADAPTER_RANK
+    firsts = jnp.stack([jnp.asarray(c, jnp.int32) for group, _, _ in slots for _, c in group])
+    info = jnp.concatenate(
+        [
+            jnp.stack([pick]),
+            jnp.stack([b for _, b, _ in slots]),
+            jnp.stack([v.astype(jnp.int32) for _, _, v in slots]),
+            firsts,
+        ]
+    ).astype(jnp.int32)
 
     def kernel(info, *refs):
-        tokens_in = iter(refs[: len(flat)])
-        sources = [[next(tokens_in) for _ in group] for group in candidates]
-        down_refs = refs[len(flat) : len(flat) + holders]
-        member_ref, out_ref, held, sems = refs[len(flat) + holders :]
-        columns = pl.ds(pl.multiple_of(info[1], 128), width)
-        for r in range(groups):
-            start_picked(sources[r], info[0], held.at[pl.ds(r * rows, rows), :], sems.at[r], columns)
-        for r in range(groups):
-            pltpu.make_async_copy(
-                sources[r][0].at[:, columns], held.at[pl.ds(r * rows, rows), :], sems.at[r]
-            ).wait()
-        total = None
-        for d in range(holders):
-            product = lax.dot_general(
-                held[...], down_refs[d][...], (((1,), (1,)), ((), ())), preferred_element_type=F32
+        place = iter(enumerate(places))
+        sources = []
+        for group, _, _ in slots:
+            at = [next(place) for _ in group]
+            sources.append(
+                [(refs[p], pl.multiple_of(info[1 + 2 * count + i], HEAD_SIZE)) for i, p in at]
             )
-            term = product * member_ref[:, d : d + 1]
-            total = term if total is None else total + term
-        out_ref[...] = total
+        pack_refs = refs[len(arrays) : len(arrays) + holders]
+        member_ref, out_ref, held, sems = refs[len(arrays) + holders :]
+        for i in range(count):
+            pl.when(info[1 + count + i] == 1)(
+                functools.partial(
+                    start_picked, sources[i], info[0], width, held.at[i], sems.at[i]
+                )
+            )
+        for i in range(count):
+
+            @pl.when(info[1 + count + i] == 1)
+            def _(i=i):
+                pltpu.make_async_copy(
+                    sources[i][0][0].at[:, pl.ds(0, width)], held.at[i], sems.at[i]
+                ).wait()
+                here = pl.ds(pl.multiple_of(info[1 + i] * rows, rows), rows)
+                member = member_ref[here, :]
+                sum_ = None
+                for d in range(holders):
+                    product = lax.dot_general(
+                        held[i],
+                        pack_refs[d][:rank, :],
+                        (((1,), (1,)), ((), ())),
+                        preferred_element_type=F32,
+                    )
+                    term = product * member[:, d : d + 1]
+                    sum_ = term if sum_ is None else sum_ + term
+                out_ref[here, :] = sum_
 
     return pl.pallas_call(
         kernel,
         grid_spec=pltpu.PrefetchScalarGridSpec(
             num_scalar_prefetch=1,
             grid=(1,),
-            in_specs=[ANY] * len(flat)
-            + [whole(d.shape) for d in downs]
+            in_specs=[ANY] * len(arrays)
+            + [whole(p.shape) for p in packed]
             + [whole(members.shape)],
-            out_specs=whole((groups * rows, rank)),
+            out_specs=whole((total, rank)),
             scratch_shapes=[
-                pltpu.VMEM((groups * rows, width), BF16),
-                pltpu.SemaphoreType.DMA((groups,)),
+                pltpu.VMEM((count, rows, width), BF16),
+                pltpu.SemaphoreType.DMA((count,)),
             ],
         ),
-        out_shape=jax.ShapeDtypeStruct((groups * rows, rank), F32),
-        compiler_params=params(),
+        out_shape=jax.ShapeDtypeStruct((total, rank), F32),
+        compiler_params=params(
+            2 * count * rows * width
+            + 4 * holders * packed[0].size
+            + 16 * total * HEAD_SIZE
+        ),
         cost_estimate=pl.CostEstimate(
-            flops=2 * groups * rows * width * rank * holders,
-            bytes_accessed=2 * width * (groups * rows + rank * holders),
+            flops=2 * total * width * rank * holders,
+            bytes_accessed=2 * width * (total + rank * holders),
             transcendentals=0,
         ),
-    )(jnp.stack([pick, offset]).astype(jnp.int32), *flat, *downs, members)
+    )(info, *arrays, *packed, members)
 
 
 def spread(low, member):
@@ -191,22 +271,37 @@
     return block * cosine + pltpu.roll(block, HEAD_SIZE // 2, 1) * sine
 
 
-def finish(sources, rank_index, low, members, up_query, up_keyval, tables, firsts, blocks):
+def finish(sources, rank_index, low, members, packed, tables, firsts, blocks):
     rows = low.shape[0] // blocks
-    query_width = up_query.shape[1]
-    keyval_width = up_keyval.shape[1]
+    query_width = sources[0][0].shape[1]
+    keyval_width = sources[0][1].shape[1]
     used = firsts[2] * HEAD_SIZE
     rank = ADAPTER_RANK
     count = len(sources)
+    holders = len(packed)
+    cut = query_width // keyval_width
+    strip = rank // cut
+    sums_in, places = unique([x for q, kv, _, _ in sources for x in (q, kv)])
 
     def kernel(info, *refs):
-        sums = refs[: 2 * count]
-        (low_ref, member_ref, upq_ref, upkv_ref, cos_ref, sin_ref, kcos_ref, ksin_ref) = refs[
-            2 * count : 2 * count + 8
-        ]
-        query_ref, mine_ref, send_ref, held_q, held_kv, sems = refs[2 * count + 8 :]
+        sums = [refs[p] for p in places]
+        rest = refs[len(sums_in) :]
+        pack_refs, rest = rest[:holders], rest[holders:]
+        low_ref, member_ref, cos_ref, sin_ref, kcos_ref, ksin_ref = rest[:6]
+        query_ref, mine_ref, send_ref, upq_ref, upkv_ref, held_q, held_kv, sems = rest[6:]
         block = pl.program_id(0)
         z = info[0]
+
+        @pl.when(block == 0)
+        def _():
+            for d, packed_ref in enumerate(pack_refs):
+                at = d * rank
+                upq_ref[at : at + rank, :] = packed_ref[2 * rank : 3 * rank, :]
+                for i in range(cut):
+                    upkv_ref[at + i * strip : at + (i + 1) * strip, :] = packed_ref[
+                        3 * rank : 3 * rank + strip, i * keyval_width : (i + 1) * keyval_width
+                    ]
+
         for i, (_, _, first, test) in enumerate(sources):
 
             @pl.when(test(block, z))
@@ -244,7 +339,6 @@
     def by_block(width):
         return pl.BlockSpec((rows, width), lambda b, info: (b, 0))
 
-    flat = [x for q, kv, _, _ in sources for x in (q, kv)]
     total = rows * blocks
     info = jnp.stack([rank_index, firsts[0] * HEAD_SIZE, firsts[1] * HEAD_SIZE]).astype(jnp.int32)
     return pl.pallas_call(
@@ -252,15 +346,17 @@
         grid_spec=pltpu.PrefetchScalarGridSpec(
             num_scalar_prefetch=1,
             grid=(blocks,),
-            in_specs=[ANY] * len(flat)
-            + [
-                by_block(low.shape[1]),
-                by_block(members.shape[1]),
-                whole(up_query.shape),
-                whole(up_keyval.shape),
-            ]
+            in_specs=[ANY] * len(sums_in)
+            + [whole(p.shape) for p in packed]
+            + [by_block(low.shape[1]), by_block(members.shape[1])]
             + [by_block(HEAD_SIZE)] * 4,
-            out_specs=[by_block(query_width), by_block(used), by_block(used)],
+            out_specs=[
+                by_block(query_width),
+                by_block(used),
+                by_block(used),
+                whole((holders * rank, query_width)),
+                whole((holders * rank, keyval_width)),
+            ],
             scratch_shapes=[
                 pltpu.VMEM((rows, query_width), F32),
                 pltpu.VMEM((rows, keyval_width), F32),
@@ -271,33 +367,41 @@
             jax.ShapeDtypeStruct((total, query_width), BF16),
             jax.ShapeDtypeStruct((total, used), BF16),
             jax.ShapeDtypeStruct((total, used), BF16),
+            jax.ShapeDtypeStruct((holders * rank, query_width), BF16),
+            jax.ShapeDtypeStruct((holders * rank, keyval_width), BF16),
         ],
-        compiler_params=params(),
+        compiler_params=params(
+            4 * holders * packed[0].size
+            + (12 * rows + 4 * holders * rank) * (query_width + keyval_width)
+        ),
         cost_estimate=pl.CostEstimate(
-            flops=2 * total * up_query.shape[0] * (query_width + keyval_width),
+            flops=2 * total * holders * rank * (query_width + keyval_width),
             bytes_accessed=8 * total * (query_width + keyval_width),
             transcendentals=0,
         ),
-    )(info, *flat, low, members, up_query, up_keyval, *tables)
+    )(info, *sums_in, *packed, low, members, *tables)
 
 
 def finish_late(candidates, pick, chunk_id, weight, sums, low, member, up, cosine, sine, cuts=None):
-    rows, chunk = candidates[0].shape
+    rows = candidates[0][0].shape[0]
+    chunk = weight.shape[0] // CHUNKS
     width = weight.shape[1]
     step_width = min(512, width)
     steps = width // step_width
     count = len(candidates)
 
     def kernel(info, *refs):
-        sources = refs[:count]
+        sources = [(ref, c) for ref, (_, c) in zip(refs, candidates)]
         weight_ref, sum_ref, low_ref, member_ref, up_ref, cos_ref, sin_ref = refs[count : count + 7]
         rest = refs[count + 7 :]
         outs, (held, sem) = rest[:-2], rest[-2:]
 
         @pl.when(pl.program_id(0) == 0)
         def _():
-            start_picked(sources, info[0], held, sem.at[0])
-            pltpu.make_async_copy(sources[0], held, sem.at[0]).wait()
+            start_picked(sources, info[0], chunk, held, sem.at[0])
+            pltpu.make_async_copy(
+                sources[0][0].at[:, pl.ds(0, chunk)], held, sem.at[0]
+            ).wait()
 
         update = jnp.dot(
             spread(low_ref[...], member_ref[...].astype(BF16)),
@@ -355,13 +459,13 @@
             scratch_shapes=[pltpu.VMEM((rows, chunk), BF16), pltpu.SemaphoreType.DMA((1,))],
         ),
         out_shape=outs,
-        compiler_params=params(),
+        compiler_params=params(4 * (chunk + up.shape[0] + 4 * rows) * step_width + 2 * rows * chunk),
         cost_estimate=pl.CostEstimate(
             flops=2 * rows * width * (chunk + up.shape[0]),
             bytes_accessed=2 * width * chunk,
             transcendentals=0,
         ),
-    )(jnp.stack(info).astype(jnp.int32), *candidates, weight, sums, low, member, up, cosine, sine)
+    )(jnp.stack(info).astype(jnp.int32), *[x for x, _ in candidates], weight, sums, low, member, up, cosine, sine)
 
 
 def attend(query, query_late, mine, mine_late, recv, recv_late, ids_column, ids_row, info, blocks):
@@ -445,7 +549,7 @@
             scratch_shapes=[pltpu.VMEM(mine.shape, BF16), pltpu.VMEM(mine.shape, BF16)],
         ),
         out_shape=jax.ShapeDtypeStruct((total, width), BF16),
-        compiler_params=params(),
+        compiler_params=params(8 * total * span + 12 * mine.size + 4 * MIB),
         cost_estimate=pl.CostEstimate(
             flops=4 * total * total * width,
             bytes_accessed=4 * total * width,
@@ -483,26 +587,70 @@
     query_width = query_weight.shape[1]
     keyval_width = key_value_weight.shape[1]
 
-    down = {(0, c): tokens[:, c * chunk_width : (c + 1) * chunk_width] for c in range(chunks)}
+    front, back = (0, 1), (1, chunks)
+    late_pieces = [front, (1, chunks - 1), (chunks - 1, chunks)]
+    turns = [(k, piece) for k in range(1, late) for piece in (front, back)]
+    turns += [(late, piece) for piece in late_pieces]
+    down = {(0, (0, chunks)): tokens}
     up = dict(down)
-    ahead = [(k, 0) for k in range(1, n)]
-    behind = [(k, a) for k in range(1, n) for a in range(1, chunks)]
-    turns = [t for both in zip(ahead, behind) for t in both] + behind[len(ahead) :]
+
+    def mirrored(piece):
+        return (chunks - piece[1], chunks - piece[0])
+
+    def piece_at(way, k, chunk):
+        for (j, (first, end)), x in way.items():
+            if j == k and first <= chunk < end:
+                return x, (chunk - first) * chunk_width
+
+    def cut_out(way, k, piece):
+        x, first = piece_at(way, k, piece[0])
+        wide = (piece[1] - piece[0]) * chunk_width
+        return x if x.shape[1] == wide else x[:, first : first + wide]
+
+    came = {}
+
     def send_turn(i, *others):
-        k, a = turns[i]
-        b = chunks - 1 - a
+        k, piece = turns[i]
+        other_piece = mirrored(piece)
         if i >= 2:
-            k_before, a_before = turns[i - 2]
-            others += (down[k_before, a_before], up[k_before, chunks - 1 - a_before])
-        send_down, send_up = after((down[k - 1, a], up[k - 1, b]), *others)
-        down[k, a] = lax.ppermute(send_down, "tensor", [(j, j - 1) for j in range(1, n - k + 1)])
-        up[k, b] = lax.ppermute(send_up, "tensor", [(j, j + 1) for j in range(k - 1, n - 1)])
+            others += came[i - 2]
+        sends = (cut_out(down, k - 1, piece), cut_out(up, k - 1, other_piece))
+        if k == late:
+            send = after(jnp.where(side == 0, *sends), *others)
+            last_out[piece] = send
+            came[i] = (lax.ppermute(send, "tensor", [(1, 0), (n - 2, n - 1)]),)
+            last_in[piece] = came[i][0]
+            return
+        if i == 0:
+            first_sends.extend(sends)
+        if i == 1:
+            others += tuple(first_sends)
+        send_down, send_up = after(sends, *others)
+        if i == 1:
+            first_sends.extend((send_down, send_up))
+        down[k, piece] = lax.ppermute(
+            send_down, "tensor", [(j, j - 1) for j in range(1, n - k + 1)]
+        )
+        up[k, other_piece] = lax.ppermute(
+            send_up, "tensor", [(j, j + 1) for j in range(k - 1, n - 1)]
+        )
+        came[i] = (down[k, piece], up[k, other_piece])
 
     def turn_of(k):
         return max(i for i, (j, _) in enumerate(turns) if j == k)
 
-    send_turn(0)
-    send_turn(1)
+    hold = {}
+    first_sends = []
+    last_in, last_out = {}, {}
+    next_turn = 0
+
+    def send_until(turn):
+        nonlocal next_turn
+        while next_turn <= min(turn, len(turns) - 1):
+            send_turn(next_turn, *([hold[next_turn]] if next_turn in hold else []))
+            next_turn += 1
+
+    send_until(1)
 
     per_store = adapter_down_maps.shape[0]
     lookup = (
@@ -513,25 +661,19 @@
     here = slot_table // per_store == store
     local = jnp.sum(jnp.where(here, slot_table - store * per_store, 0), axis=1)
 
-    stacks = [adapter_down_maps, adapter_up_key_value, adapter_up_query]
-    got = [[], [], []]
-    last = down[0, 0]
-    sent = []
-    for which, stack in enumerate(stacks):
-        for d in range(stores):
-            target = (store + d) % stores
-            row = lax.dynamic_index_in_dim(local, target, 0, keepdims=False)
-            part = lax.dynamic_index_in_dim(stack, row, 0, keepdims=False)
-            if d:
-                part = after(part, last)
-                sent.append(part)
-                last = part = lax.ppermute(
-                    part, "store", [(i, (i + d) % stores) for i in range(stores)]
-                )
-            got[which].append(part)
-    downs, up_keyval, up_query = got
-    up_query = jnp.concatenate(up_query, axis=0)
-    up_keyval = jnp.concatenate(up_keyval, axis=0)
+    packed = pack(
+        adapter_down_maps,
+        adapter_up_query,
+        adapter_up_key_value,
+        after(
+            lax.dynamic_slice_in_dim(jnp.concatenate([local, local]), store, stores, 0), *first_sends
+        ),
+    )
+    packed = list(packed)
+    for d in range(1, stores):
+        packed[d] = lax.ppermute(
+            after(packed[d], packed[d - 1]), "store", [(i, (i + d) % stores) for i in range(stores)]
+        )
 
     segment_row = token_request_ids[0]
     my_holders = lax.dynamic_index_in_dim(slot_table, store, 0, keepdims=False) // per_store
@@ -559,100 +701,62 @@
     def block_of(array, index):
         return lax.dynamic_slice_in_dim(array, jnp.clip(index, 0, n - 1) * rows, rows, 0)
 
-    def every_chunk(way, k):
-        return [way[k, c] for c in range(chunks)]
-
     weights = [query_weight, key_value_weight]
     sources = []
-    own_q, own_kv = project(
-        [[[down[0, c]]] for c in range(chunks)],
-        after(jnp.zeros((1,), jnp.int32), downs[0], sent[0]),
-        list(range(chunks)),
-        weights,
-    )
-    sources.append((own_q, own_kv, 0, lambda b, zz: b == zz))
     side_chunks = [jnp.where(side == 0, a, chunks - 1 - a) for a in range(chunks)]
 
     def sided(k, a):
-        return [down[k, a], up[k, chunks - 1 - a]]
-
-    hold = {2: own_kv}
-    next_turn = 2
-
-    def send_until(turn):
-        nonlocal next_turn
-        while next_turn <= min(turn, len(turns) - 1):
-            send_turn(next_turn, *([hold[next_turn]] if next_turn in hold else []))
-            next_turn += 1
-
-    def near(k):
-        return [
-            ([down[k, c] for c in range(chunks)], z + k),
-            ([up[k, c] for c in range(chunks)], z - k),
-        ]
-
-    def far(k):
-        return (
-            [down[k, c] for c in range(chunks // 2)] + [up[k, c] for c in range(chunks // 2, chunks)],
-            jnp.where(side == 0, z + k, z - k),
-        )
-
-    def low_of(groups):
-        return low_parts(
-            [g for g, _ in groups],
-            home_chunk,
-            home_offset,
-            width_share,
-            downs,
-            [block_of(members, b) for _, b in groups],
-        )
-
-    low_sum = low_parts(
-        [[tokens]], jnp.int32(0), z * width_share, width_share, downs, [block_of(members, z)]
-    )
-    projected = {}
+        return [piece_at(down, k, a), piece_at(up, k, chunks - 1 - a)]
+
     for k in range(1, half):
         send_until(turn_of(k) + 2)
-        both = low_of(near(k))
-        low_sum = low_sum + lax.ppermute(both[:rows], "tensor", [(i, i + k) for i in range(n - k)])
-        low_sum = low_sum + lax.ppermute(both[rows:], "tensor", [(i, i - k) for i in range(k, n)])
+        ways = ([(down, 0)] if k == 1 else []) + [(down, k), (up, k)]
         q, kv = project(
-            [[[down[k, c]], [up[k, c]]] for c in range(chunks)],
-            after(jnp.zeros((2,), jnp.int32), both),
+            [[[piece_at(way, j, c)] for way, j in ways] for c in range(chunks)],
+            after(jnp.zeros((len(ways),), jnp.int32), *came[turn_of(k) + 1]),
             list(range(chunks)),
+            chunk_width,
             weights,
         )
-        hold[turn_of(k) + 3] = kv
-        sources.append((q, kv, 0, lambda b, zz, k=k: b == zz + k))
-        sources.append((q, kv, rows, lambda b, zz, k=k: b == zz - k))
-    far_home = max(i for i, (_, a) in enumerate(turns) if a < chunks // 2)
-    send_until(far_home)
-    far_low = low_of([far(k) for k in range(half, n)])
-    for k in range(half, n):
-        low_sum = low_sum + lax.ppermute(
-            far_low[(k - half) * rows : (k - half + 1) * rows],
-            "tensor",
-            [(i, i + k) for i in range(n - k)] + [(i, i - k) for i in range(k, n)],
-        )
-    low_own = low_sum.astype(BF16)
-    low_turned = [low_own] + [
-        lax.ppermute(low_own, "tensor", [((i + r) % n, i) for i in range(n)]) for r in range(1, n)
-    ]
-    low = lax.dynamic_slice_in_dim(
-        jnp.concatenate(low_turned + low_turned, axis=0), (n - z) % n * rows, total, 0
-    )
-
+        hold[turn_of(k) + 4] = kv
+        first = 0
+        if k == 1:
+            sources.append((q, kv, 0, lambda b, zz: b == zz))
+            first = rows
+        sources.append((q, kv, first, lambda b, zz, k=k: b == zz + k))
+        sources.append((q, kv, first + rows, lambda b, zz, k=k: b == zz - k))
     for k in range(half, late):
         send_until(turn_of(k) + 2)
         q, kv = project(
             [[sided(k, a)] for a in range(chunks)],
-            after(jnp.stack([side]), low),
+            jnp.stack([side]),
             jnp.stack(side_chunks),
+            chunk_width,
             weights,
         )
         hold[turn_of(k) + 3] = kv
         sources.append((q, kv, 0, lambda b, zz, k=k: (b == zz + k) | (b == zz - k)))
     send_until(len(turns))
+
+    def home(way, k, c):
+        x, first = piece_at(way, k, c)
+        return x, first + home_offset
+
+    slots = [([(tokens, z * width_share)], z, z >= 0)]
+    for k in range(1, half):
+        slots.append(([home(down, k, c) for c in range(chunks)], z + k, z + k < n))
+        slots.append(([home(up, k, c) for c in range(chunks)], z - k, z >= k))
+    for k in range(half, late):
+        from_both = [home(down, k, c) for c in range(chunks // 2)]
+        from_both += [home(up, k, c) for c in range(chunks // 2, chunks)]
+        slots.append((from_both, jnp.where(side == 0, z + k, z - k), (z + k < n) | (z >= k)))
+    front_in, middle_in, back_in = (last_in[piece] for piece in late_pieces)
+    slots.append(([(front_in, home_offset)], jnp.where(side == 0, late, 0), (z == 0) | (z == late)))
+    low_part = low_parts(
+        slots, after(home_chunk, last_out[late_pieces[1]]), width_share, packed, members
+    )
+    low = lax.psum(low_part, "tensor").astype(BF16)
+
     group_size = QUERY_HEADS // KEY_VALUE_HEADS
     head_local = query_width // HEAD_SIZE
     pair_heads = keyval_width // HEAD_SIZE
@@ -663,28 +767,28 @@
 
     partner = z ^ 1
     cuts = (first_used(z), first_used(partner), used)
-    query, mine, send = finish(
+    query, mine, send, up_query, up_keyval = finish(
         sources,
         z,
         low,
         members,
-        up_query,
-        up_keyval,
+        packed,
         (cosine, sine, key_cosine, key_sine),
         cuts,
         n,
     )
     recv = lax.ppermute(send, "tensor", [(i, i ^ 1) for i in range(n)])
     late_q, late_kv = project(
-        [[sided(late, a)] for a in range(chunks - 1)],
-        after(jnp.stack([side]), mine),
-        jnp.stack(side_chunks[: chunks - 1]),
+        [[[(front_in, 0)]]] + [[[(middle_in, a * chunk_width)]] for a in range(chunks - 2)],
+        after(jnp.zeros((1,), jnp.int32), low_part),
+        jnp.stack([side_chunks[0]] + list(range(1, chunks - 1))),
+        chunk_width,
         weights,
     )
 
     late_block = jnp.where(side == 0, n - 1, 0)
     late_args = dict(
-        candidates=sided(late, chunks - 1), pick=side, chunk_id=side_chunks[chunks - 1]
+        candidates=[(back_in, 0)], pick=side, chunk_id=side_chunks[chunks - 1]
     )
     late_low = block_of(low, late_block)
     late_member = block_of(members, late_block)

time: 290 us -> 337 us (1.16)
  Pallas kernels: 101 us -> 222 us
  starting transfers between devices: 85.1 us -> 28.8 us
  blocking collectives: 0 us -> 33.2 us
  local copies, waits for them, and re-layouts: 40.7 us -> 12.7 us
  waiting for transfers between devices: 42.9 us -> 27.3 us
  between operations: 8.73 us -> 0.57 us
    pallas_call x0 -> x1, Pallas kernels: none -> 105 us  [pack(): pl.pallas_call(kernel, grid_spec=pltpu.PrefetchScalarGridSpec(num_scalar_...]
    psum x0 -> x1, blocking collectives: none -> 33.2 us  [on_device(): low = lax.psum(low_part, 'tensor').astype(BF16)]
    ppermute x16 -> x6, starting transfers between devices: 34.9 us -> 7.4 us  [the longest x3 3.85 us: send_turn(): came[i] = (lax.ppermute(send, 'tensor', [(1, 0), (n - 2, n - 1)]),)]
    unnamed x150 -> x42, local copies, waits for them, and re-layouts: 26 us -> 3.18 us
    ppermute x16 -> x6, waiting for transfers between devices: 19.8 us -> 0.7 us  [the longest x3 0.69 us: on_device(): lax.ppermute(after(packed[d], packed[d - 1]), 'store', [(i, (i + d) % sto...]
    ppermute x12 -> x4, starting transfers between devices: 30.1 us -> 12.1 us  [send_turn(): lax.ppermute(send_up, 'tensor', [(j, j + 1) for j in range(k - 1, n - 1)])]
    ppermute x12 -> x4, starting transfers between devices: 15.4 us -> 5.28 us  [send_turn(): lax.ppermute(send_down, 'tensor', [(j, j - 1) for j in range(1, n - k + 1)])]
    pallas_call x1, Pallas kernels: 4.04 us -> 11.7 us  [finish(): pl.pallas_call(kernel, grid_spec=pltpu.PrefetchScalarGridSpec(num_scalar_...]
  transfers between devices with their start and end apart: 42 -> 16, of which waited for: 9 -> 3; matrix products, arithmetic and copies ran while one was open for 7% -> 5% of each run, Pallas kernels for 29% -> 61%
where the time goes in v3:
time: 337 us; the launch traced here: 336 us
  Pallas kernels  222 us (66%)
  blocking collectives  33.2 us (10%)
  starting transfers between devices  28.8 us (9%)
  waiting for transfers between devices  27.3 us (8%)
  local copies, waits for them, and re-layouts  12.7 us (4%)
  other arithmetic  11.2 us (3%)
    pallas_call x1, Pallas kernels, pack(): pl.pallas_call(kernel, grid_spec=pltpu.PrefetchScalarGridSpec(num_scalar_...  105 us
    pallas_call x3, Pallas kernels, project(): pl.pallas_call(kernel, grid_spec=pltpu.PrefetchScalarGridSpec(num_scalar_...  66.3 us
    psum x1, blocking collectives, on_device(): low = lax.psum(low_part, 'tensor').astype(BF16)  33.2 us
    ppermute x4, waiting for transfers between devices, send_turn(): lax.ppermute(send_down, 'tensor', [(j, j - 1) for j in range(1, n - k + 1)])  26.6 us
    pallas_call x1, Pallas kernels, attend(): pl.pallas_call(kernel, grid_spec=pltpu.PrefetchScalarGridSpec(num_scalar_...  17.8 us
    pallas_call x2, Pallas kernels, finish_late(): pl.pallas_call(kernel, grid_spec=pltpu.PrefetchScalarGridSpec(num_scalar_...  13.4 us
    ppermute x4, starting transfers between devices, send_turn(): lax.ppermute(send_up, 'tensor', [(j, j + 1) for j in range(k - 1, n - 1)])  12.1 us
    pallas_call x1, Pallas kernels, finish(): pl.pallas_call(kernel, grid_spec=pltpu.PrefetchScalarGridSpec(num_scalar_...  11.7 us
  transfers between devices with their start and end apart: 16, of which 3 were waited for; matrix products, arithmetic and copies ran while one was open for 5% of the time, Pallas kernels for 61%

profile of v3, /device:TPU:0, one launch (start us, length us, event | category | flops | bytes accessed | tf_op | source)
XLA Modules:
  0.0 335.6 jit_solution(3676335579229738862)
XLA Ops:
  0.0 2.2 fusion.9
  2.2 1.4 collective-permute-start
  3.7 6.4 %collective-permute-start.1 = (bf16[128,2048]{1,0:T(8,128)(2,1)S(1)}, bf16[128,2048]{1,0:T(8,128)(2,1)}, u32[]{:S(2)}, u32[]{:S(2)}) collective-permute-start(bf16[128,2048]{1,0:T(8,128)(2,1)S(1)} %get-tuple-element.41), channel_id=1, source_target_pairs={{0,4},{4,8},{8,12},{1,5},{5,9},{9,13},{2,6},{6,10},{10,14},{3,7},{... | collective-permute-start | bytes 1572872 | tf_op jit(solution)/shard_map/ppermute | solution.py:634
  10.0 1.9 fusion.8
  12.0 4.3 %collective-permute-start.4 = (bf16[128,6144]{1,0:T(8,128)(2,1)}, bf16[128,6144]{1,0:T(8,128)(2,1)}, u32[]{:S(2)}, u32[]{:S(2)}) collective-permute-start(bf16[128,6144]{1,0:T(8,128)(2,1)} %get-tuple-element.45), channel_id=1, source_target_pairs={{0,4},{4,8},{8,12},{1,5},{5,9},{9,13},{2,6},{6,10},{10,14},{3,7},{... | collective-permute-start | bytes 4718600 | tf_op jit(solution)/shard_map/ppermute | solution.py:634
  16.3 1.3 collective-permute-start.5
  17.6 0.2 select_reduce_fusion.1
  17.8 0.1 select_reduce_fusion.3
  17.9 0.1 pad_add_fusion.3
  18.0 0.6 dynamic_slice.25.rows
  18.6 105.3 %shard_map.102 = (bf16[208,2048]{1,0:T(8,128)(2,1)}, bf16[208,2048]{1,0:T(8,128)(2,1)}, bf16[208,2048]{1,0:T(8,128)(2,1)}, bf16[208,2048]{1,0:T(8,128)(2,1)}) custom-call(s32[4]{0:T(128)} %dynamic_slice.25.rows, bf16[8,128,2048]{2,1,0:T(8,128)(2,1)} %down_ref.1, bf16[8,64,2048]{2,1,0:T(8,128)(2,1)} %upq_ref.1, bf16[8,64,512]{2,1,0:T(8,128)(2,1)} %upkv_ref.1), custom_call_target="tpu_custom_call" | custom-call | tf_op jit(solution)/shard_map/pallas_call | solution.py:94
  123.9 0.1 collective-permute-start.8
  124.1 0.1 convert_reduce_fusion
  124.3 0.2 select_reduce_fusion
  124.6 0.2 select_reduce_fusion.2
  124.8 1.0 fusion
  125.8 0.6 pad_add_fusion.4.info
  126.3 0.6 pad_add_fusion.6.info
  127.0 1.0 broadcast_select_fusion.1
  128.0 0.7 pad_add_fusion.1.info
  128.8 0.8 copy.12.idc_ref
  129.6 0.6 concatenate.22.info
  130.2 0.6 constant_dynamic-slice_fusion.refs_7_
  130.8 0.6 constant_dynamic-slice_fusion.1.refs_6_
  131.4 1.3 collective-permute-start.2
  132.7 0.7 collective-permute-start.3
  133.4 0.6 pad_add_fusion.info
  134.0 0.1 compare_convert_fusion.refs_14_.refs_9_
  134.2 0.7 constant_dynamic-slice_fusion.3.refs_4_
  134.9 0.7 fusion.1
  135.6 0.7 collective-permute-done.8.refs_11_.refs_5_
  136.3 1.5 collective-permute-start.9
  137.8 10.1 %collective-permute-done.2.refs_0_.refs_5_ = bf16[128,2048]{1,0:T(8,128)(2,1)S(1)} collective-permute-done((bf16[128,2048]{1,0:T(8,128)(2,1)S(1)}, bf16[128,2048]{1,0:T(8,128)(2,1)S(1)}, u32[]{:S(2)}, u32[]{:S(2)}) %collective-permute-start.2) | collective-permute-done | bytes 524320 | tf_op jit(solution)/shard_map/ppermute | solution.py:631
  147.9 0.9 broadcast_select_fusion
  148.8 1.3 collective-permute-start.11
  150.2 1.3 collective-permute-start.6
  151.5 0.8 collective-permute-start.7
  152.3 0.6 pad_add_fusion.2.info
  152.8 29.5 %shard_map.100 = (f32[384,2048]{1,0:T(8,128)}, f32[384,512]{1,0:T(8,128)}) custom-call(s32[7]{0:T(128)} %pad_add_fusion.2.info, bf16[128,8192]{1,0:T(8,128)(2,1)} %refs_0_.3, bf16[128,2048]{1,0:T(8,128)(2,1)} %copy-done.14, bf16[128,6144]{1,0:T(8,128)(2,1)} %collective-permute-done.4.refs_2_.refs_3_, ...), custom_call_target="tpu_custom_call" | custom-call | flops 16106127360 | bytes 48234496 | tf_op jit(solution)/shard_map/pallas_call | solution.py:155
  182.4 2.0 collective-permute-start.10
  184.4 16.5 %collective-permute-done.6.refs_2_.refs_6_ = bf16[128,6144]{1,0:T(8,128)(2,1)S(1)} collective-permute-done((bf16[128,6144]{1,0:T(8,128)(2,1)}, bf16[128,6144]{1,0:T(8,128)(2,1)S(1)}, u32[]{:S(2)}, u32[]{:S(2)}) %collective-permute-start.6) | collective-permute-done | bytes 1572896 | tf_op jit(solution)/shard_map/ppermute | solution.py:631
  200.9 1.3 slice_select_fusion
  202.2 0.1 copy-done.1
  202.4 0.5 copy-done.2
  202.9 1.3 collective-permute-start.13
  204.2 0.7 concatenate.24.info
  204.9 7.3 %shard_map.103 = f32[512,128]{1,0:T(8,128)} custom-call(s32[25]{0:T(128)} %concatenate.24.info, bf16[128,8192]{1,0:T(8,128)(2,1)} %refs_0_.3, bf16[128,2048]{1,0:T(8,128)(2,1)} %copy-done.14, bf16[128,6144]{1,0:T(8,128)(2,1)} %collective-permute-done.5.refs_3_.refs_2_, bf16[128,6144]{1,0:T(8,128)(2,1)} %collective-permute-done.4.refs_2_.refs_3_, ...), custom_call_target="tpu_custom_call" | custom-call | flops 1073741824 | bytes 4194304 | tf_op jit(solution)/shard_map/pallas_call | solution.py:238
  212.1 1.3 slice_select_fusion.1
  213.4 20.4 %shard_map.101 = (f32[128,2048]{1,0:T(8,128)}, f32[128,512]{1,0:T(8,128)}) custom-call(s32[5]{0:T(128)} %concatenate.22.info, bf16[128,2048]{1,0:T(8,128)(2,1)} %copy-done.3, bf16[128,2048]{1,0:T(8,128)(2,1)} %copy-done.4, bf16[128,6144]{1,0:T(8,128)(2,1)} %copy-done.1, bf16[128,6144]{1,0:T(8,128)(2,1)} %copy-done.2, bf16[8192,2048]{1,0:T(8,128)(2,1)} %refs_1_.2, ...), custom_call_target="tpu_custom_call" | custom-call | flops 5368709120 | bytes 44040192 | tf_op jit(solution)/shard_map/pallas_call | solution.py:155
  233.8 1.3 collective-permute-start.12
  235.1 33.2 %all-reduce.1.refs_8_ = bf16[512,128]{1,0:T(8,128)(2,1)} all-reduce(f32[512,128]{1,0:T(8,128)S(1)} %copy-done.11), channel_id=1, replica_groups=mesh['groups'=2,'tensor'=4,'store'=4] {'tensor'}, use_global_device_ids=true, to_apply=%region_3.4 | all-reduce | flops 65536 | bytes 393216 | tf_op jit(solution)/shard_map/psum | solution.py:758
  268.3 11.7 %shard_map.104 = (bf16[512,2048]{1,0:T(8,128)(2,1)}, bf16[512,256]{1,0:T(8,128)(2,1)}, bf16[512,256]{1,0:T(8,128)(2,1)}, bf16[256,2048]{1,0:T(8,128)(2,1)}, bf16[256,512]{1,0:T(8,128)(2,1)}) custom-call(s32[3]{0:T(128)} %pad_add_fusion.1.info, f32[384,2048]{1,0:T(8,128)} %get-tuple-element.47.refs_0_, f32[384,512]{1,0:T(8,128)} %get-tuple-element.48.refs_1_, ...), custom_call_target="tpu_custom_call" | custom-call | flops 671088640 | bytes 10485760 | tf_op jit(solution)/shard_map/pallas_call | solution.py:344
  280.0 0.1 collective-permute-start.14
  280.1 0.7 pad_add_fusion.5.info
  280.8 0.7 fusion.10
  281.5 1.0 copy-done.12
  282.4 16.4 %shard_map.105 = (f32[128,2048]{1,0:T(8,128)}, f32[128,512]{1,0:T(8,128)}) custom-call(s32[4]{0:T(128)} %pad_add_fusion.5.info, bf16[128,2048]{1,0:T(8,128)(2,1)} %collective-permute-done.11.refs_9_.refs_0_, bf16[128,4096]{1,0:T(8,128)(2,1)} %copy-done.12, bf16[8192,2048]{1,0:T(8,128)(2,1)} %refs_1_.2, bf16[8192,512]{1,0:T(8,128)(2,1)} %refs_1_.3), custom_call_target="tpu_custom_call" | custom-call | flops 4026531840 | bytes 33030144 | tf_op jit(solution)/shard_map/pallas_call | solution.py:155
  298.9 0.8 copy-done.8
  299.7 4.8 %shard_map.107 = (bf16[128,256]{1,0:T(8,128)(2,1)}, bf16[128,256]{1,0:T(8,128)(2,1)}) custom-call(s32[4]{0:T(128)} %pad_add_fusion.6.info, bf16[128,2048]{1,0:T(8,128)(2,1)} %copy-done.8, bf16[8192,512]{1,0:T(8,128)(2,1)} %refs_1_.3, f32[128,512]{1,0:T(8,128)} %get-tuple-element.70.refs_2_, bf16[128,64]{1,0:T(8,128)(2,1)} %get-tuple-element.83.refs_3_, ...), custom_call_target="tpu_custom_call" | custom-call | flops 301989888 | bytes 2097152 | tf_op jit(solution)/shard_map/pallas_call | solution.py:443
  304.5 3.9 %collective-permute-start.15 = (bf16[128,256]{1,0:T(8,128)(2,1)}, bf16[128,256]{1,0:T(8,128)(2,1)S(1)}, u32[]{:S(2)}, u32[]{:S(2)}) collective-permute-start(bf16[128,256]{1,0:T(8,128)(2,1)} %get-tuple-element.74), channel_id=1, source_target_pairs={{0,4},{12,8},{1,5},{13,9},{2,6},{14,10},{3,7},{15,11},{16,20},{28,... | collective-permute-start | bytes 196616 | tf_op jit(solution)/shard_map/ppermute | solution.py:806
  308.5 8.6 %shard_map.106.ql_ref = bf16[128,2048]{1,0:T(8,128)(2,1)} custom-call(s32[2]{0:T(128)} %pad_add_fusion.4.info, bf16[128,2048]{1,0:T(8,128)(2,1)} %copy-done.8, bf16[8192,2048]{1,0:T(8,128)(2,1)} %refs_1_.2, f32[128,2048]{1,0:T(8,128)} %get-tuple-element.67.refs_2_, bf16[128,64]{1,0:T(8,128)(2,1)} %get-tuple-element.84.refs_3_, ...), custom_call_target="tpu_custom_call" | custom-call | flops 1207959552 | bytes 8388608 | tf_op jit(solution)/shard_map/pallas_call | solution.py:443
  317.1 0.7 copy-done.19
  317.8 0.0 copy-done.20
  317.8 17.8 %shard_map.108 = bf16[512,2048]{1,0:T(8,128)(2,1)} custom-call(s32[3]{0:T(128)} %pad_add_fusion.info, bf16[512,2048]{1,0:T(8,128)(2,1)} %get-tuple-element.64.q_ref, bf16[128,2048]{1,0:T(8,128)(2,1)} %shard_map.106.ql_ref, bf16[512,256]{1,0:T(8,128)(2,1)} %get-tuple-element.69.m_ref, bf16[128,256]{1,0:T(8,128)(2,1)} %get-tuple-element.72.ml_ref, ...), custom_call_target="tpu_custom_call" | custom-call | flops 2147483648 | bytes 4194304 | tf_op jit(solution)/shard_map/pallas_call | solution.py:533
  (55 shorter events, 0.2 us)
Async XLA Ops:
  0.0 10.0 %copy-start = (bf16[128,8192]{1,0:T(8,128)(2,1)S(1)}, bf16[128,8192]{1,0:T(8,128)(2,1)}, u32[]{:S(2)}) copy-start(bf16[128,8192]{1,0:T(8,128)(2,1)} %refs_0_.3) | copy-start | bytes 6291460
  2.2 15.3 %copy-start.16 = (s32[4,4]{1,0:T(4,128)S(1)}, s32[4,4]{1,0:T(4,128)}, u32[]{:S(2)}) copy-start(s32[4,4]{1,0:T(4,128)} %param.17) | copy-start | bytes 196
  2.2 15.3 %copy-start.17 = (s32[32]{0:T(128)S(1)}, s32[32]{0:T(128)}, u32[]{:S(2)}) copy-start(s32[32]{0:T(128)} %param.16) | copy-start | bytes 388
  2.2 129.2 %collective-permute-start = (bf16[128,2048]{1,0:T(8,128)(2,1)}, bf16[128,2048]{1,0:T(8,128)(2,1)S(1)}, u32[]{:S(2)}, u32[]{:S(2)}) collective-permute-start(bf16[128,2048]{1,0:T(8,128)(2,1)} %get-tuple-element.40), channel_id=1, source_target_pairs={{4,0},{8,4},{12,8},{5,1},{9,5},{13,9},{6,2},{10,6},{14,10},{7,3},{... | collective-permute-start | bytes 1572872 | tf_op jit(solution)/shard_map/ppermute | solution.py:631
  3.7 127.8 %collective-permute-start.1 = (bf16[128,2048]{1,0:T(8,128)(2,1)S(1)}, bf16[128,2048]{1,0:T(8,128)(2,1)}, u32[]{:S(2)}, u32[]{:S(2)}) collective-permute-start(bf16[128,2048]{1,0:T(8,128)(2,1)S(1)} %get-tuple-element.41), channel_id=1, source_target_pairs={{0,4},{4,8},{8,12},{1,5},{5,9},{9,13},{2,6},{6,10},{10,14},{3,7},{... | collective-permute-start | bytes 1572872 | tf_op jit(solution)/shard_map/ppermute | solution.py:634
  12.0 138.2 %collective-permute-start.4 = (bf16[128,6144]{1,0:T(8,128)(2,1)}, bf16[128,6144]{1,0:T(8,128)(2,1)}, u32[]{:S(2)}, u32[]{:S(2)}) collective-permute-start(bf16[128,6144]{1,0:T(8,128)(2,1)} %get-tuple-element.45), channel_id=1, source_target_pairs={{0,4},{4,8},{8,12},{1,5},{5,9},{9,13},{2,6},{6,10},{10,14},{3,7},{... | collective-permute-start | bytes 4718600 | tf_op jit(solution)/shard_map/ppermute | solution.py:634
  16.3 133.9 %collective-permute-start.5 = (bf16[128,6144]{1,0:T(8,128)(2,1)}, bf16[128,6144]{1,0:T(8,128)(2,1)}, u32[]{:S(2)}, u32[]{:S(2)}) collective-permute-start(bf16[128,6144]{1,0:T(8,128)(2,1)} %get-tuple-element.46), channel_id=1, source_target_pairs={{4,0},{8,4},{12,8},{5,1},{9,5},{13,9},{6,2},{10,6},{14,10},{7,3},{... | collective-permute-start | bytes 4718600 | tf_op jit(solution)/shard_map/ppermute | solution.py:631
  18.6 105.5 %copy-start.15 = (s32[1,512]{1,0:T(1,128)S(1)}, s32[1,512]{1,0:T(1,128)}, u32[]{:S(2)}) copy-start(s32[1,512]{1,0:T(1,128)} %idr_ref.1) | copy-start | bytes 6148
  123.9 12.4 %collective-permute-start.8 = (bf16[208,2048]{1,0:T(8,128)(2,1)}, bf16[208,2048]{1,0:T(8,128)(2,1)S(1)}, u32[]{:S(2)}, u32[]{:S(2)}) collective-permute-start(bf16[208,2048]{1,0:T(8,128)(2,1)} %get-tuple-element.56), channel_id=1, source_target_pairs={{0,1},{1,2},{2,3},{3,0},{4,5},{5,6},{6,7},{7,4},{8,9},{9,10},{10,1... | collective-permute-start | bytes 2555912 | tf_op jit(solution)/shard_map/ppermute | solution.py:674
  128.0 20.8 %copy-start.9 = (f32[512,128]{1,0:T(8,128)}, f32[512,128]{1,0:T(8,128)S(1)}, u32[]{:S(2)}) copy-start(f32[512,128]{1,0:T(8,128)S(1)} %get-tuple-element.75.refs_13_) | copy-start | bytes 786436
  128.0 20.8 %copy-start.10 = (f32[512,128]{1,0:T(8,128)}, f32[512,128]{1,0:T(8,128)S(1)}, u32[]{:S(2)}) copy-start(f32[512,128]{1,0:T(8,128)S(1)} %get-tuple-element.89.refs_12_) | copy-start | bytes 786436
  130.2 6.1 %copy-start.18 = (bf16[208,2048]{1,0:T(8,128)(2,1)S(1)}, bf16[208,2048]{1,0:T(8,128)(2,1)}, u32[]{:S(2)}) copy-start(bf16[208,2048]{1,0:T(8,128)(2,1)} %get-tuple-element.58) | copy-start | bytes 2555908
  131.4 18.7 %copy-start.14 = (bf16[128,2048]{1,0:T(8,128)(2,1)}, bf16[128,2048]{1,0:T(8,128)(2,1)S(1)}, u32[]{:S(2)}) copy-start(bf16[128,2048]{1,0:T(8,128)(2,1)S(1)} %collective-permute-done.refs_1_) | copy-start | bytes 1572868
  131.4 16.4 %collective-permute-start.2 = (bf16[128,2048]{1,0:T(8,128)(2,1)S(1)}, bf16[128,2048]{1,0:T(8,128)(2,1)S(1)}, u32[]{:S(2)}, u32[]{:S(2)}) collective-permute-start(bf16[128,2048]{1,0:T(8,128)(2,1)S(1)} %collective-permute-done.refs_1_), channel_id=1, source_target_pairs={{4,0},{8,4},{5,1},{9,5},{6,2},{10,6},{7,3},{11,7},{20,16},{24,20},... | collective-permute-start | bytes 1572872 | tf_op jit(solution)/shard_map/ppermute | solution.py:631
  132.7 15.2 %collective-permute-start.3 = (bf16[128,2048]{1,0:T(8,128)(2,1)}, bf16[128,2048]{1,0:T(8,128)(2,1)S(1)}, u32[]{:S(2)}, u32[]{:S(2)}) collective-permute-start(bf16[128,2048]{1,0:T(8,128)(2,1)} %collective-permute-done.1.refs_4_), channel_id=1, source_target_pairs={{4,8},{8,12},{5,9},{9,13},{6,10},{10,14},{7,11},{11,15},{20,24},{2... | collective-permute-start | bytes 1572872 | tf_op jit(solution)/shard_map/ppermute | solution.py:634
  134.2 48.2 %copy-start.7 = (f32[512,4]{1,0:T(8,128)}, f32[512,4]{1,0:T(8,128)S(1)}, u32[]{:S(2)}) copy-start(f32[512,4]{1,0:T(8,128)S(1)} %compare_convert_fusion.refs_14_.refs_9_) | copy-start | bytes 24580
  136.3 13.8 %copy-start.5 = (bf16[208,2048]{1,0:T(8,128)(2,1)}, bf16[208,2048]{1,0:T(8,128)(2,1)S(1)}, u32[]{:S(2)}) copy-start(bf16[208,2048]{1,0:T(8,128)(2,1)S(1)} %collective-permute-done.8.refs_11_.refs_5_) | copy-start | bytes 2555908
  136.3 46.0 %collective-permute-start.9 = (bf16[208,2048]{1,0:T(8,128)(2,1)S(1)}, bf16[208,2048]{1,0:T(8,128)(2,1)S(1)}, u32[]{:S(2)}, u32[]{:S(2)}) collective-permute-start(bf16[208,2048]{1,0:T(8,128)(2,1)S(1)} %copy-done.18), channel_id=1, source_target_pairs={{0,2},{1,3},{2,0},{3,1},{4,6},{5,7},{6,4},{7,5},{8,10},{9,11},{10,... | collective-permute-start | bytes 2555912 | tf_op jit(solution)/shard_map/ppermute | solution.py:674
  147.9 2.3 copy-start.3
  147.9 3.6 %copy-start.4 = (bf16[128,2048]{1,0:T(8,128)(2,1)}, bf16[128,2048]{1,0:T(8,128)(2,1)S(1)}, u32[]{:S(2)}) copy-start(bf16[128,2048]{1,0:T(8,128)(2,1)S(1)} %collective-permute-done.3.refs_1_.refs_8_) | copy-start | bytes 1572868
  148.8 56.0 %collective-permute-start.11 = (bf16[128,2048]{1,0:T(8,128)(2,1)}, bf16[128,2048]{1,0:T(8,128)(2,1)}, u32[]{:S(2)}, u32[]{:S(2)}) collective-permute-start(bf16[128,2048]{1,0:T(8,128)(2,1)} %broadcast_select_fusion), channel_id=1, source_target_pairs={{4,0},{8,12},{5,1},{9,13},{6,2},{10,14},{7,3},{11,15},{20,16},{24,... | collective-permute-start | bytes 1572872 | tf_op jit(solution)/shard_map/ppermute | solution.py:621
  150.2 50.7 %collective-permute-start.6 = (bf16[128,6144]{1,0:T(8,128)(2,1)}, bf16[128,6144]{1,0:T(8,128)(2,1)S(1)}, u32[]{:S(2)}, u32[]{:S(2)}) collective-permute-start(bf16[128,6144]{1,0:T(8,128)(2,1)} %collective-permute-done.5.refs_3_.refs_2_), channel_id=1, source_target_pairs={{4,0},{8,4},{5,1},{9,5},{6,2},{10,6},{7,3},{11,7},{20,16},{24,20},... | collective-permute-start | bytes 4718600 | tf_op jit(solution)/shard_map/ppermute | solution.py:631
  151.5 49.4 %collective-permute-start.7 = (bf16[128,6144]{1,0:T(8,128)(2,1)}, bf16[128,6144]{1,0:T(8,128)(2,1)S(1)}, u32[]{:S(2)}, u32[]{:S(2)}) collective-permute-start(bf16[128,6144]{1,0:T(8,128)(2,1)} %collective-permute-done.4.refs_2_.refs_3_), channel_id=1, source_target_pairs={{4,8},{8,12},{5,9},{9,13},{6,10},{10,14},{7,11},{11,15},{20,24},{2... | collective-permute-start | bytes 4718600 | tf_op jit(solution)/shard_map/ppermute | solution.py:634
  182.4 20.5 %copy-start.6 = (bf16[208,2048]{1,0:T(8,128)(2,1)}, bf16[208,2048]{1,0:T(8,128)(2,1)S(1)}, u32[]{:S(2)}) copy-start(bf16[208,2048]{1,0:T(8,128)(2,1)S(1)} %collective-permute-done.9.refs_12_.refs_6_) | copy-start | bytes 2555908
  182.4 22.5 %collective-permute-start.10 = (bf16[208,2048]{1,0:T(8,128)(2,1)}, bf16[208,2048]{1,0:T(8,128)(2,1)}, u32[]{:S(2)}, u32[]{:S(2)}) collective-permute-start(bf16[208,2048]{1,0:T(8,128)(2,1)} %get-tuple-element.60), channel_id=1, source_target_pairs={{0,3},{1,0},{2,1},{3,2},{4,7},{5,4},{6,5},{7,6},{8,11},{9,8},{10,9... | collective-permute-start | bytes 2555912 | tf_op jit(solution)/shard_map/ppermute | solution.py:674
  200.9 1.5 copy-start.1
  200.9 2.0 copy-start.2
  202.9 78.6 %collective-permute-start.13 = (bf16[128,4096]{1,0:T(8,128)(2,1)}, bf16[128,4096]{1,0:T(8,128)(2,1)S(1)}, u32[]{:S(2)}, u32[]{:S(2)}) collective-permute-start(bf16[128,4096]{1,0:T(8,128)(2,1)} %slice_select_fusion), channel_id=1, source_target_pairs={{4,0},{8,12},{5,1},{9,13},{6,2},{10,14},{7,3},{11,15},{20,16},{24,... | collective-permute-start | bytes 3145736 | tf_op jit(solution)/shard_map/ppermute | solution.py:621
  213.4 21.7 %copy-start.11 = (f32[512,128]{1,0:T(8,128)S(1)}, f32[512,128]{1,0:T(8,128)}, u32[]{:S(2)}) copy-start(f32[512,128]{1,0:T(8,128)} %shard_map.103) | copy-start | bytes 786436
  233.8 65.1 %collective-permute-start.12 = (bf16[128,2048]{1,0:T(8,128)(2,1)S(1)}, bf16[128,2048]{1,0:T(8,128)(2,1)S(1)}, u32[]{:S(2)}, u32[]{:S(2)}) collective-permute-start(bf16[128,2048]{1,0:T(8,128)(2,1)S(1)} %slice_select_fusion.1), channel_id=1, source_target_pairs={{4,0},{8,12},{5,1},{9,13},{6,2},{10,14},{7,3},{11,15},{20,16},{24,... | collective-permute-start | bytes 1572872 | tf_op jit(solution)/shard_map/ppermute | solution.py:621
  268.3 12.4 %copy-start.13 = (bf16[512,128]{1,0:T(8,128)(2,1)S(1)}, bf16[512,128]{1,0:T(8,128)(2,1)}, u32[]{:S(2)}) copy-start(bf16[512,128]{1,0:T(8,128)(2,1)} %all-reduce.1.refs_8_) | copy-start | bytes 393220
  280.0 37.0 %collective-permute-start.14 = (bf16[512,256]{1,0:T(8,128)(2,1)}, bf16[512,256]{1,0:T(8,128)(2,1)S(1)}, u32[]{:S(2)}, u32[]{:S(2)}) collective-permute-start(bf16[512,256]{1,0:T(8,128)(2,1)} %get-tuple-element.73), channel_id=1, source_target_pairs={{0,4},{4,0},{8,12},{12,8},{1,5},{5,1},{9,13},{13,9},{2,6},{6,2},{1... | collective-permute-start | bytes 786440 | tf_op jit(solution)/shard_map/ppermute | solution.py:780
  281.5 1.0 copy-start.12
  298.9 0.8 copy-start.8
  304.5 12.5 %collective-permute-start.15 = (bf16[128,256]{1,0:T(8,128)(2,1)}, bf16[128,256]{1,0:T(8,128)(2,1)S(1)}, u32[]{:S(2)}, u32[]{:S(2)}) collective-permute-start(bf16[128,256]{1,0:T(8,128)(2,1)} %get-tuple-element.74), channel_id=1, source_target_pairs={{0,4},{12,8},{1,5},{13,9},{2,6},{14,10},{3,7},{15,11},{16,20},{28,... | collective-permute-start | bytes 196616 | tf_op jit(solution)/shard_map/ppermute | solution.py:806
  317.1 0.7 copy-start.19
  317.1 0.7 copy-start.20

commit v4 on v3

--- a/solution.py
+++ b/solution.py
@@ -66,30 +66,42 @@
     cut = width // keyval_width
     strip = rank // cut
 
+    height = down_rows + rank + strip
+
     def kernel(rows, down_ref, upq_ref, upkv_ref, *rest):
-        outs, sems = rest[:stores], rest[stores]
-        copies = []
+        outs, (held, sems, out_sems) = rest[:stores], rest[stores:]
+        copies, writes = [], []
         for d in range(stores):
-            out = outs[d]
-            copies.append((down_ref.at[rows[d]], out.at[pl.ds(0, down_rows), :]))
-            copies.append((upq_ref.at[rows[d]], out.at[pl.ds(down_rows, rank), :]))
+            here = held.at[d]
+            sources = [
+                (down_ref.at[rows[d]], here.at[pl.ds(0, down_rows), :]),
+                (upq_ref.at[rows[d]], here.at[pl.ds(down_rows, rank), :]),
+            ]
             for i in range(cut):
-                copies.append(
+                sources.append(
                     (
                         upkv_ref.at[rows[d], pl.ds(i * strip, strip), :],
-                        out.at[
+                        here.at[
                             pl.ds(down_rows + rank, strip), pl.ds(i * keyval_width, keyval_width)
                         ],
                     )
                 )
-        copies = [
-            pltpu.make_async_copy(source, target, sems.at[i])
-            for i, (source, target) in enumerate(copies)
-        ]
-        for copy in copies:
-            copy.start()
-        for copy in copies:
-            copy.wait()
+            copies.append(
+                [
+                    pltpu.make_async_copy(source, target, sems.at[d, i])
+                    for i, (source, target) in enumerate(sources)
+                ]
+            )
+            writes.append(pltpu.make_async_copy(here, outs[d], out_sems.at[d]))
+        for group in copies:
+            for copy in group:
+                copy.start()
+        for group, write in zip(copies, writes):
+            for copy in group:
+                copy.wait()
+            write.start()
+        for write in writes:
+            write.wait()
 
     return pl.pallas_call(
         kernel,
@@ -98,88 +110,116 @@
             grid=(1,),
             in_specs=[ANY] * 3,
             out_specs=[ANY] * stores,
-            scratch_shapes=[pltpu.SemaphoreType.DMA((stores * (2 + cut),))],
-        ),
-        out_shape=[jax.ShapeDtypeStruct((down_rows + rank + strip, width), BF16)] * stores,
-        compiler_params=params(0),
+            scratch_shapes=[
+                pltpu.VMEM((stores, height, width), BF16),
+                pltpu.SemaphoreType.DMA((stores, 2 + cut)),
+                pltpu.SemaphoreType.DMA((stores,)),
+            ],
+        ),
+        out_shape=[jax.ShapeDtypeStruct((height, width), BF16)] * stores,
+        compiler_params=params(2 * stores * height * width),
     )(local, down_maps, up_query, up_keyval)
 
 
-def project(candidates, picks, chunk_ids, chunk, weights):
+def project(candidates, picks, chunk_ids, chunk, weights, starts=None):
     steps, groups = len(candidates), len(candidates[0])
     rows = candidates[0][0][0][0].shape[0]
     block = min(1024, chunk)
     sub = chunk // block
+    blocks = steps * sub
+    ahead = min(3, blocks)
     arrays, places = unique([x for a in candidates for group in a for x, _ in group])
     widths = [w.shape[1] for w in weights]
     count = len(weights)
+    height = groups * rows
 
     def kernel(info, *refs):
         place = iter(places)
         sources = [[[(refs[next(place)], c) for _, c in group] for group in a] for a in candidates]
         rest = refs[len(arrays) :]
-        weight_refs, out_refs, (held, sems) = rest[:count], rest[count : 2 * count], rest[2 * count :]
-        step = pl.program_id(0)
-        at = step // sub
-
-        @pl.when(step == 0)
-        def _():
-            for a in range(steps):
+        weight_refs, rest = rest[:count], rest[count:]
+        if starts is not None:
+            start_refs, rest = rest[:count], rest[count:]
+        out_refs, rest = rest[:count], rest[count:]
+        streams, (held, sems, stream_sems) = rest[:count], rest[count:]
+
+        def loads(i, slot):
+            at = info[groups + i // sub] * sub + i % sub
+            here = pl.ds(pl.multiple_of(at * block, block), block)
+            return [
+                pltpu.make_async_copy(
+                    weight_refs[w].at[here, :], streams[w].at[slot], stream_sems.at[slot, w]
+                )
+                for w in range(count)
+            ]
+
+        for a in range(steps):
+            for r in range(groups):
+                target = held.at[a, pl.ds(r * rows, rows), :]
+                start_picked(sources[a][r], info[r], chunk, target, sems.at[a, r])
+            if a == 0:
+                for i in range(ahead):
+                    for load in loads(i, i):
+                        load.start()
+        for w in range(count):
+            out_refs[w][...] = jnp.zeros_like(out_refs[w]) if starts is None else start_refs[w][...]
+
+        def body(i, carry):
+            slot = lax.rem(i, ahead)
+            at, part_at = i // sub, lax.rem(i, sub)
+
+            @pl.when(part_at == 0)
+            def _():
                 for r in range(groups):
-                    target = held.at[a, pl.ds(r * rows, rows), :]
-                    start_picked(sources[a][r], info[r], chunk, target, sems.at[a, r])
-
-        @pl.when(step % sub == 0)
-        def _():
-            for r in range(groups):
-                pltpu.make_async_copy(
-                    sources[0][r][0][0].at[:, pl.ds(0, chunk)],
-                    held.at[at, pl.ds(r * rows, rows), :],
-                    sems.at[at, r],
-                ).wait()
-
-        part = held[at, :, pl.ds(pl.multiple_of((step % sub) * block, block), block)]
-        for i in range(count):
-            product = jnp.dot(part, weight_refs[i][...], preferred_element_type=F32)
-
-            @pl.when(step == 0)
-            def _(i=i, product=product):
-                out_refs[i][...] = product
-
-            @pl.when(step > 0)
-            def _(i=i, product=product):
-                out_refs[i][...] += product
-
-    height = groups * rows
+                    pltpu.make_async_copy(
+                        sources[0][r][0][0].at[:, pl.ds(0, chunk)],
+                        held.at[at, pl.ds(r * rows, rows), :],
+                        sems.at[at, r],
+                    ).wait()
+
+            for load in loads(i, slot):
+                load.wait()
+            part = held[at, :, pl.ds(pl.multiple_of(part_at * block, block), block)]
+            for w in range(count):
+                out_refs[w][...] += jnp.dot(
+                    part, streams[w][slot], preferred_element_type=F32
+                )
+
+            @pl.when(i + ahead < blocks)
+            def _():
+                for load in loads(i + ahead, slot):
+                    load.start()
+
+            return carry
+
+        lax.fori_loop(0, blocks, body, 0)
+
     info = jnp.concatenate([jnp.asarray(picks, jnp.int32), jnp.asarray(chunk_ids, jnp.int32)])
     return pl.pallas_call(
         kernel,
         grid_spec=pltpu.PrefetchScalarGridSpec(
             num_scalar_prefetch=1,
-            grid=(steps * sub,),
-            in_specs=[ANY] * len(arrays)
+            grid=(1,),
+            in_specs=[ANY] * (len(arrays) + count)
+            + ([whole((height, w)) for w in widths] if starts is not None else []),
+            out_specs=[whole((height, w)) for w in widths],
+            scratch_shapes=[pltpu.VMEM((ahead, block, w), BF16) for w in widths]
             + [
-                pl.BlockSpec(
-                    (block, w), lambda g, info: (info[groups + g // sub] * sub + g % sub, 0)
-                )
-                for w in widths
-            ],
-            out_specs=[whole((height, w)) for w in widths],
-            scratch_shapes=[
                 pltpu.VMEM((steps, height, chunk), BF16),
                 pltpu.SemaphoreType.DMA((steps, groups)),
+                pltpu.SemaphoreType.DMA((ahead, count)),
             ],
         ),
         out_shape=[jax.ShapeDtypeStruct((height, w), F32) for w in widths],
         compiler_params=params(
-            2 * steps * height * chunk + (4 * block + 8 * height) * sum(widths)
+            2 * steps * height * chunk + (2 * ahead * block + 16 * height) * sum(widths)
         ),
         cost_estimate=pl.CostEstimate(
             flops=2 * height * steps * chunk * sum(widths),
             bytes_accessed=2 * steps * chunk * (sum(widths) + height),
             transcendentals=0,
         ),
-    )(info, *arrays, *weights)
+    )(info, *arrays, *weights, *(starts or []))
 
 
 def low_parts(slots, pick, width, packed, members):
@@ -207,13 +247,25 @@
                 [(refs[p], pl.multiple_of(info[1 + 2 * count + i], HEAD_SIZE)) for i, p in at]
             )
         pack_refs = refs[len(arrays) : len(arrays) + holders]
-        member_ref, out_ref, held, sems = refs[len(arrays) + holders :]
+        member_ref, out_ref, held, maps, sems, map_sems = refs[len(arrays) + holders :]
+        loads = [
+            pltpu.make_async_copy(
+                pack_refs[d].at[pl.ds(0, rank), :],
+                maps.at[pl.ds(d * rank, rank), :],
+                map_sems.at[d],
+            )
+            for d in range(holders)
+        ]
+        for load in loads:
+            load.start()
         for i in range(count):
             pl.when(info[1 + count + i] == 1)(
                 functools.partial(
                     start_picked, sources[i], info[0], width, held.at[i], sems.at[i]
                 )
             )
+        for load in loads:
+            load.wait()
         for i in range(count):
 
             @pl.when(info[1 + count + i] == 1)
@@ -223,33 +275,29 @@
                 ).wait()
                 here = pl.ds(pl.multiple_of(info[1 + i] * rows, rows), rows)
                 member = member_ref[here, :]
-                sum_ = None
-                for d in range(holders):
-                    product = lax.dot_general(
-                        held[i],
-                        pack_refs[d][:rank, :],
-                        (((1,), (1,)), ((), ())),
-                        preferred_element_type=F32,
-                    )
-                    term = product * member[:, d : d + 1]
-                    sum_ = term if sum_ is None else sum_ + term
-                out_ref[here, :] = sum_
+                product = lax.dot_general(
+                    held[i], maps[...], (((1,), (1,)), ((), ())), preferred_element_type=F32
+                )
+                sum_ = product[:, :rank] * member[:, 0:1]
+                for d in range(1, holders):
+                    sum_ += product[:, d * rank : (d + 1) * rank] * member[:, d : d + 1]
+                out_ref[here, :] = sum_.astype(BF16)
 
     return pl.pallas_call(
         kernel,
         grid_spec=pltpu.PrefetchScalarGridSpec(
             num_scalar_prefetch=1,
             grid=(1,),
-            in_specs=[ANY] * len(arrays)
-            + [whole(p.shape) for p in packed]
-            + [whole(members.shape)],
+            in_specs=[ANY] * (len(arrays) + holders) + [whole(members.shape)],
             out_specs=whole((total, rank)),
             scratch_shapes=[
                 pltpu.VMEM((count, rows, width), BF16),
+                pltpu.VMEM((holders * rank, width), BF16),
                 pltpu.SemaphoreType.DMA((count,)),
+                pltpu.SemaphoreType.DMA((holders,)),
             ],
         ),
-        out_shape=jax.ShapeDtypeStruct((total, rank), F32),
+        out_shape=jax.ShapeDtypeStruct((total, rank), BF16),
         compiler_params=params(
             2 * count * rows * width
             + 4 * holders * packed[0].size
@@ -288,53 +336,81 @@
         rest = refs[len(sums_in) :]
         pack_refs, rest = rest[:holders], rest[holders:]
         low_ref, member_ref, cos_ref, sin_ref, kcos_ref, ksin_ref = rest[:6]
-        query_ref, mine_ref, send_ref, upq_ref, upkv_ref, held_q, held_kv, sems = rest[6:]
+        query_ref, mine_ref, send_ref, upq_ref, upkv_ref = rest[6:11]
+        held_q, held_kv, turned, sems, up_sems = rest[11:]
         block = pl.program_id(0)
         z = info[0]
 
+        def loads(b, i):
+            first = sources[i][2]
+            return [
+                pltpu.make_async_copy(
+                    sums[2 * i + j].at[pl.ds(first, rows), :], held.at[b], sems.at[b, j]
+                )
+                for j, held in enumerate((held_q, held_kv))
+            ]
+
+        ups = []
+        for d, packed_ref in enumerate(pack_refs):
+            at = d * rank
+            ups.append(
+                (packed_ref.at[pl.ds(2 * rank, rank), :], upq_ref.at[pl.ds(at, rank), :])
+            )
+            for i in range(cut):
+                ups.append(
+                    (
+                        packed_ref.at[
+                            pl.ds(3 * rank, strip), pl.ds(i * keyval_width, keyval_width)
+                        ],
+                        upkv_ref.at[pl.ds(at + i * strip, strip), :],
+                    )
+                )
+        ups = [pltpu.make_async_copy(a, b, up_sems.at[i]) for i, (a, b) in enumerate(ups)]
+
         @pl.when(block == 0)
         def _():
-            for d, packed_ref in enumerate(pack_refs):
-                at = d * rank
-                upq_ref[at : at + rank, :] = packed_ref[2 * rank : 3 * rank, :]
-                for i in range(cut):
-                    upkv_ref[at + i * strip : at + (i + 1) * strip, :] = packed_ref[
-                        3 * rank : 3 * rank + strip, i * keyval_width : (i + 1) * keyval_width
-                    ]
-
-        for i, (_, _, first, test) in enumerate(sources):
-
-            @pl.when(test(block, z))
-            def _(i=i, first=first):
-                a = pltpu.make_async_copy(sums[2 * i].at[pl.ds(first, rows), :], held_q, sems.at[0])
-                b = pltpu.make_async_copy(
-                    sums[2 * i + 1].at[pl.ds(first, rows), :], held_kv, sems.at[1]
+            for b in range(blocks):
+                for i, (_, _, _, test) in enumerate(sources):
+
+                    @pl.when(test(b, z))
+                    def _(b=b, i=i):
+                        for load in loads(b, i):
+                            load.start()
+
+            for load in ups:
+                load.start()
+            for load in ups:
+                load.wait()
+
+        def add_and_turn(b):
+            member = member_ref[...].astype(BF16)
+            low_block = low_ref[...]
+            update = jnp.dot(
+                spread(low_block[:, :rank], member), upq_ref[...], preferred_element_type=F32
+            )
+            for h in range(query_width // HEAD_SIZE):
+                at = slice(h * HEAD_SIZE, (h + 1) * HEAD_SIZE)
+                query_ref[:, at] = rotate(
+                    held_q[b, :, at] + adapter_scale * update[:, at], cos_ref[...], sin_ref[...]
+                ).astype(BF16)
+            update = jnp.dot(
+                spread(low_block[:, rank:], member), upkv_ref[...], preferred_element_type=F32
+            )
+            for h in range(keyval_width // HEAD_SIZE):
+                at = slice(h * HEAD_SIZE, (h + 1) * HEAD_SIZE)
+                turned[:, at] = rotate(
+                    held_kv[b, :, at] + adapter_scale * update[:, at], kcos_ref[...], ksin_ref[...]
                 )
-                a.start()
-                b.start()
-                a.wait()
-                b.wait()
-
-        member = member_ref[...].astype(BF16)
-        low_block = low_ref[...]
-        update = jnp.dot(
-            spread(low_block[:, :rank], member), upq_ref[...], preferred_element_type=F32
-        )
-        for h in range(query_width // HEAD_SIZE):
-            at = slice(h * HEAD_SIZE, (h + 1) * HEAD_SIZE)
-            query_ref[:, at] = rotate(
-                held_q[:, at] + adapter_scale * update[:, at], cos_ref[...], sin_ref[...]
-            ).astype(BF16)
-        update = jnp.dot(
-            spread(low_block[:, rank:], member), upkv_ref[...], preferred_element_type=F32
-        )
-        for h in range(keyval_width // HEAD_SIZE):
-            at = slice(h * HEAD_SIZE, (h + 1) * HEAD_SIZE)
-            held_kv[:, at] = rotate(
-                held_kv[:, at] + adapter_scale * update[:, at], kcos_ref[...], ksin_ref[...]
-            )
-        mine_ref[...] = held_kv[:, pl.ds(pl.multiple_of(info[1], HEAD_SIZE), used)].astype(BF16)
-        send_ref[...] = held_kv[:, pl.ds(pl.multiple_of(info[2], HEAD_SIZE), used)].astype(BF16)
+            for out, first in ((mine_ref, info[1]), (send_ref, info[2])):
+                out[...] = turned[:, pl.ds(pl.multiple_of(first, HEAD_SIZE), used)].astype(BF16)
+
+        there = functools.reduce(jnp.logical_or, [test(block, z) for _, _, _, test in sources])
+
+        @pl.when(there)
+        def _():
+            for load in loads(block, 0):
+                load.wait()
+            add_and_turn(block)
 
     def by_block(width):
         return pl.BlockSpec((rows, width), lambda b, info: (b, 0))
@@ -346,8 +422,7 @@
         grid_spec=pltpu.PrefetchScalarGridSpec(
             num_scalar_prefetch=1,
             grid=(blocks,),
-            in_specs=[ANY] * len(sums_in)
-            + [whole(p.shape) for p in packed]
+            in_specs=[ANY] * (len(sums_in) + holders)
             + [by_block(low.shape[1]), by_block(members.shape[1])]
             + [by_block(HEAD_SIZE)] * 4,
             out_specs=[
@@ -358,9 +433,11 @@
                 whole((holders * rank, keyval_width)),
             ],
             scratch_shapes=[
-                pltpu.VMEM((rows, query_width), F32),
+                pltpu.VMEM((blocks, rows, query_width), F32),
+                pltpu.VMEM((blocks, rows, keyval_width), F32),
                 pltpu.VMEM((rows, keyval_width), F32),
-                pltpu.SemaphoreType.DMA((2,)),
+                pltpu.SemaphoreType.DMA((blocks, 2)),
+                pltpu.SemaphoreType.DMA((holders * (1 + cut),)),
             ],
         ),
         out_shape=[
@@ -371,8 +448,7 @@
             jax.ShapeDtypeStruct((holders * rank, keyval_width), BF16),
         ],
         compiler_params=params(
-            4 * holders * packed[0].size
-            + (12 * rows + 4 * holders * rank) * (query_width + keyval_width)
+            (4 * total + 12 * rows + 4 * holders * rank) * (query_width + keyval_width)
         ),
         cost_estimate=pl.CostEstimate(
             flops=2 * total * holders * rank * (query_width + keyval_width),
@@ -382,34 +458,20 @@
     )(info, *sums_in, *packed, low, members, *tables)
 
 
-def finish_late(candidates, pick, chunk_id, weight, sums, low, member, up, cosine, sine, cuts=None):
-    rows = candidates[0][0].shape[0]
-    chunk = weight.shape[0] // CHUNKS
+def finish_late(piece, chunk_id, weight, sums, low, member, up, cosine, sine, cuts=None):
+    rows, chunk = piece.shape
     width = weight.shape[1]
-    step_width = min(512, width)
+    step_width = min(1024, width)
     steps = width // step_width
-    count = len(candidates)
-
-    def kernel(info, *refs):
-        sources = [(ref, c) for ref, (_, c) in zip(refs, candidates)]
-        weight_ref, sum_ref, low_ref, member_ref, up_ref, cos_ref, sin_ref = refs[count : count + 7]
-        rest = refs[count + 7 :]
-        outs, (held, sem) = rest[:-2], rest[-2:]
-
-        @pl.when(pl.program_id(0) == 0)
-        def _():
-            start_picked(sources, info[0], chunk, held, sem.at[0])
-            pltpu.make_async_copy(
-                sources[0][0].at[:, pl.ds(0, chunk)], held, sem.at[0]
-            ).wait()
-
+
+    def kernel(info, x_ref, weight_ref, sum_ref, low_ref, member_ref, up_ref, cos_ref, sin_ref, *outs):
         update = jnp.dot(
             spread(low_ref[...], member_ref[...].astype(BF16)),
             up_ref[...],
             preferred_element_type=F32,
         )
         raw = (
-            jnp.dot(held[...], weight_ref[...], preferred_element_type=F32)
+            jnp.dot(x_ref[...], weight_ref[...], preferred_element_type=F32)
             + sum_ref[...]
             + adapter_scale * update
         )
@@ -421,7 +483,7 @@
             for h, part in enumerate(parts):
                 outs[0][:, h * HEAD_SIZE : (h + 1) * HEAD_SIZE] = part.astype(BF16)
         else:
-            for out, first in ((outs[0], info[2]), (outs[1], info[3])):
+            for out, first in ((outs[0], info[1]), (outs[1], info[2])):
                 for u in range(cuts[2]):
                     chosen = parts[0]
                     for h in range(1, len(parts)):
@@ -434,20 +496,20 @@
     if cuts is None:
         outs = [jax.ShapeDtypeStruct((rows, width), BF16)]
         out_specs = [column(rows)]
-        info = [pick, chunk_id]
+        info = [chunk_id]
     else:
         used = cuts[2] * HEAD_SIZE
         outs = [jax.ShapeDtypeStruct((rows, used), BF16)] * 2
         out_specs = [whole((rows, used))] * 2
-        info = [pick, chunk_id, cuts[0], cuts[1]]
+        info = [chunk_id, cuts[0], cuts[1]]
     return pl.pallas_call(
         kernel,
         grid_spec=pltpu.PrefetchScalarGridSpec(
             num_scalar_prefetch=1,
             grid=(steps,),
-            in_specs=[ANY] * count
-            + [
-                pl.BlockSpec((chunk, step_width), lambda g, info: (info[1], g)),
+            in_specs=[
+                whole(piece.shape),
+                pl.BlockSpec((chunk, step_width), lambda g, info: (info[0], g)),
                 column(rows),
                 whole(low.shape),
                 whole(member.shape),
@@ -456,16 +518,15 @@
                 whole(sine.shape),
             ],
             out_specs=out_specs,
-            scratch_shapes=[pltpu.VMEM((rows, chunk), BF16), pltpu.SemaphoreType.DMA((1,))],
         ),
         out_shape=outs,
-        compiler_params=params(4 * (chunk + up.shape[0] + 4 * rows) * step_width + 2 * rows * chunk),
+        compiler_params=params(4 * (chunk + up.shape[0] + 4 * rows) * step_width + 4 * rows * chunk),
         cost_estimate=pl.CostEstimate(
             flops=2 * rows * width * (chunk + up.shape[0]),
             bytes_accessed=2 * width * chunk,
             transcendentals=0,
         ),
-    )(jnp.stack(info).astype(jnp.int32), *[x for x, _ in candidates], weight, sums, low, member, up, cosine, sine)
+    )(jnp.stack(info).astype(jnp.int32), piece, weight, sums, low, member, up, cosine, sine)
 
 
 def attend(query, query_late, mine, mine_late, recv, recv_late, ids_column, ids_row, info, blocks):
@@ -480,7 +541,10 @@
     tiles = total // TILE
     back = -(-(LONGEST_REQUEST - 1) // TILE)
 
-    def kernel(info, q_ref, ql_ref, m_ref, ml_ref, r_ref, rl_ref, idc_ref, idr_ref, out_ref, k_ref, v_ref):
+    longest = (back + 1) * TILE
+
+    def kernel(info, q_ref, ql_ref, m_ref, ml_ref, r_ref, rl_ref, idc_ref, idr_ref, out_ref, *held):
+        k_ref, v_ref, bias_ref, held_q = held
         step = pl.program_id(0)
 
         @pl.when(step == 0)
@@ -500,34 +564,44 @@
 
             pl.when(info[2] == 1)(lambda: put(True))
             pl.when(info[2] == 0)(lambda: put(False))
+            for tile in range(tiles):
+                first = max(0, tile - back) * TILE
+                size = (tile + 1) * TILE - first
+                key_index = lax.broadcasted_iota(jnp.int32, (size, TILE), 0) + first
+                row_index = lax.broadcasted_iota(jnp.int32, (size, TILE), 1) + tile * TILE
+                same = idc_ref[first : first + size, :] == idr_ref[:, tile * TILE : (tile + 1) * TILE]
+                bias_ref[tile, :size, :] = jnp.where(same & (row_index >= key_index), 0.0, -1e30)
+
+        held_q[...] = q_ref[...]
 
         @pl.when(info[0] >= 0)
         def _():
-            q_ref[pl.ds(pl.multiple_of(info[0], rows), rows), :] = ql_ref[...]
+            held_q[pl.ds(pl.multiple_of(info[0], rows), rows), :] = ql_ref[...]
 
         kv_at = pl.ds(pl.multiple_of((step * together // per_kv) * HEAD_SIZE, HEAD_SIZE), HEAD_SIZE)
         for tile in range(tiles):
-            low_tile = max(0, tile - back)
-            key_rows = (tile + 1 - low_tile) * TILE
+            first = max(0, tile - back) * TILE
+            size = (tile + 1) * TILE - first
             at = slice(tile * TILE, (tile + 1) * TILE)
-            keys = k_ref[low_tile * TILE : low_tile * TILE + key_rows, kv_at]
-            values = v_ref[low_tile * TILE : low_tile * TILE + key_rows, kv_at]
-            row_index = lax.broadcasted_iota(jnp.int32, (TILE, key_rows), 0) + tile * TILE
-            column_index = lax.broadcasted_iota(jnp.int32, (TILE, key_rows), 1) + low_tile * TILE
-            allowed = (idc_ref[at, :] == idr_ref[:, low_tile * TILE : low_tile * TILE + key_rows]) & (
-                row_index >= column_index
-            )
+            keys = k_ref[first : first + size, kv_at]
+            values = v_ref[first : first + size, kv_at]
+            values = jnp.concatenate([values, jnp.ones_like(values)], axis=1)
             for h in range(together):
-                query_part = q_ref[at, h * HEAD_SIZE : (h + 1) * HEAD_SIZE]
                 scores = lax.dot_general(
-                    query_part, keys, (((1,), (1,)), ((), ())), preferred_element_type=F32
+                    keys,
+                    held_q[at, h * HEAD_SIZE : (h + 1) * HEAD_SIZE],
+                    (((1,), (1,)), ((), ())),
+                    preferred_element_type=F32,
                 )
-                scores = jnp.where(allowed, scores * scale, -1e30)
-                top = jnp.max(scores, axis=1, keepdims=True)
-                weights = jnp.exp2(scores - top)
-                norm = jnp.sum(weights, axis=1, keepdims=True)
-                mixed = jnp.dot(weights.astype(BF16), values, preferred_element_type=F32)
-                out_ref[at, h * HEAD_SIZE : (h + 1) * HEAD_SIZE] = (mixed * (1.0 / norm)).astype(BF16)
+                scores = scores * scale + bias_ref[tile, :size, :]
+                top = jnp.max(scores, axis=0, keepdims=True)
+                weights = jnp.exp2(scores - top).astype(BF16)
+                mixed = lax.dot_general(
+                    weights, values, (((0,), (0,)), ((), ())), preferred_element_type=F32
+                )
+                out_ref[at, h * HEAD_SIZE : (h + 1) * HEAD_SIZE] = (
+                    mixed[:, :HEAD_SIZE] / mixed[:, HEAD_SIZE:]
+                ).astype(BF16)
 
     by_heads = pl.BlockSpec((total, span), lambda g, info: (0, g))
     return pl.pallas_call(
@@ -546,7 +620,12 @@
                 whole(ids_row.shape),
             ],
             out_specs=by_heads,
-            scratch_shapes=[pltpu.VMEM(mine.shape, BF16), pltpu.VMEM(mine.shape, BF16)],
+            scratch_shapes=[
+                pltpu.VMEM(mine.shape, BF16),
+                pltpu.VMEM(mine.shape, BF16),
+                pltpu.VMEM((tiles, longest, TILE), F32),
+                pltpu.VMEM((total, span), BF16),
+            ],
         ),
         out_shape=jax.ShapeDtypeStruct((total, width), BF16),
         compiler_params=params(8 * total * span + 12 * mine.size + 4 * MIB),
@@ -587,10 +666,11 @@
     query_width = query_weight.shape[1]
     keyval_width = key_value_weight.shape[1]
 
-    front, back = (0, 1), (1, chunks)
-    late_pieces = [front, (1, chunks - 1), (chunks - 1, chunks)]
-    turns = [(k, piece) for k in range(1, late) for piece in (front, back)]
-    turns += [(late, piece) for piece in late_pieces]
+    front, middle, rear = (0, 1), (1, chunks - 1), (chunks - 1, chunks)
+    turns = [(k, piece) for k in range(1, n) for piece in (front, middle, rear)]
+    at = turns.index((late, front))
+    turns[at - 1], turns[at] = turns[at], turns[at - 1]
+    place = {turn: i for i, turn in enumerate(turns)}
     down = {(0, (0, chunks)): tokens}
     up = dict(down)
 
@@ -636,9 +716,6 @@
         )
         came[i] = (down[k, piece], up[k, other_piece])
 
-    def turn_of(k):
-        return max(i for i, (j, _) in enumerate(turns) if j == k)
-
     hold = {}
     first_sends = []
     last_in, last_out = {}, {}
@@ -709,34 +786,42 @@
         return [piece_at(down, k, a), piece_at(up, k, chunks - 1 - a)]
 
     for k in range(1, half):
-        send_until(turn_of(k) + 2)
+        send_until(place[k, rear] + 2)
         ways = ([(down, 0)] if k == 1 else []) + [(down, k), (up, k)]
         q, kv = project(
             [[[piece_at(way, j, c)] for way, j in ways] for c in range(chunks)],
-            after(jnp.zeros((len(ways),), jnp.int32), *came[turn_of(k) + 1]),
+            jnp.zeros((len(ways),), jnp.int32),
             list(range(chunks)),
             chunk_width,
             weights,
         )
-        hold[turn_of(k) + 4] = kv
+        hold[place[k + 1, front] + 2] = kv
         first = 0
         if k == 1:
             sources.append((q, kv, 0, lambda b, zz: b == zz))
             first = rows
         sources.append((q, kv, first, lambda b, zz, k=k: b == zz + k))
         sources.append((q, kv, first + rows, lambda b, zz, k=k: b == zz - k))
-    for k in range(half, late):
-        send_until(turn_of(k) + 2)
-        q, kv = project(
-            [[sided(k, a)] for a in range(chunks)],
-            jnp.stack([side]),
-            jnp.stack(side_chunks),
+
+    def far_block(k, some, picks, starts=None):
+        return project(
+            [[sided(k, a)] for a in some],
+            picks,
+            jnp.stack([side_chunks[a] for a in some]),
             chunk_width,
             weights,
+            starts,
         )
-        hold[turn_of(k) + 3] = kv
+
+    for k in range(half, late - 1):
+        send_until(place[k, rear] + 2)
+        q, kv = far_block(k, range(chunks), jnp.stack([side]))
+        hold[place[k + 1, front] + 2] = kv
         sources.append((q, kv, 0, lambda b, zz, k=k: (b == zz + k) | (b == zz - k)))
-    send_until(len(turns))
+    send_until(place[late - 1, rear])
+    begun = far_block(late - 1, range(chunks - 1), jnp.stack([side]))
+    hold[place[late, middle]] = begun[1]
+    send_until(place[late, middle])
 
     def home(way, k, c):
         x, first = piece_at(way, k, c)
@@ -750,12 +835,19 @@
         from_both = [home(down, k, c) for c in range(chunks // 2)]
         from_both += [home(up, k, c) for c in range(chunks // 2, chunks)]
         slots.append((from_both, jnp.where(side == 0, z + k, z - k), (z + k < n) | (z >= k)))
-    front_in, middle_in, back_in = (last_in[piece] for piece in late_pieces)
-    slots.append(([(front_in, home_offset)], jnp.where(side == 0, late, 0), (z == 0) | (z == late)))
+    slots.append(([(last_in[front], home_offset)], jnp.where(side == 0, late, 0), (z == 0) | (z == late)))
     low_part = low_parts(
-        slots, after(home_chunk, last_out[late_pieces[1]]), width_share, packed, members
-    )
-    low = lax.psum(low_part, "tensor").astype(BF16)
+        slots, after(home_chunk, last_out[middle]), width_share, packed, members
+    )
+    hold[len(turns) - 1] = low_part
+    send_until(len(turns))
+    low = low_part.astype(F32)
+    for r in range(1, n):
+        low += lax.ppermute(low_part, "tensor", [(i, (i + r) % n) for i in range(n)]).astype(F32)
+    low = low.astype(BF16)
+    q, kv = far_block(late - 1, [chunks - 1], after(jnp.stack([side]), low_part), begun)
+    sources.append((q, kv, 0, lambda b, zz: (b == zz + late - 1) | (b == zz - late + 1)))
+    front_in, middle_in, back_in = (last_in[piece] for piece in (front, middle, rear))
 
     group_size = QUERY_HEADS // KEY_VALUE_HEADS
     head_local = query_width // HEAD_SIZE
@@ -788,7 +880,7 @@
 
     late_block = jnp.where(side == 0, n - 1, 0)
     late_args = dict(
-        candidates=[(back_in, 0)], pick=side, chunk_id=side_chunks[chunks - 1]
+        piece=back_in, chunk_id=side_chunks[chunks - 1]
     )
     late_low = block_of(low, late_block)
     late_member = block_of(members, late_block)

time: 337 us -> 209 us (0.62)
  Pallas kernels: 222 us -> 101 us
  blocking collectives: 33.2 us -> 0 us
  starting transfers between devices: 28.8 us -> 44.5 us
  waiting for transfers between devices: 27.3 us -> 38.9 us
    pallas_call x1, Pallas kernels: 105 us -> 3.99 us  [pack(): pl.pallas_call(kernel, grid_spec=pltpu.PrefetchScalarGridSpec(num_scalar_...]
    psum x1 -> x0, blocking collectives: 33.2 us -> none  [on_device(): low = lax.psum(low_part, 'tensor').astype(BF16)]
    ppermute x0 -> x3, waiting for transfers between devices: none -> 9.63 us  [on_device(): lax.ppermute(low_part, 'tensor', [(i, (i + r) % n) for i in range(n)])]
    pallas_call x3 -> x4, Pallas kernels: 66.3 us -> 58 us  [project(): pl.pallas_call(kernel, grid_spec=pltpu.PrefetchScalarGridSpec(num_scalar_...]
    ppermute x0 -> x3, starting transfers between devices: none -> 7.48 us  [on_device(): lax.ppermute(low_part, 'tensor', [(i, (i + r) % n) for i in range(n)])]
    ppermute x4 -> x6, starting transfers between devices: 12.1 us -> 19.4 us  [send_turn(): lax.ppermute(send_up, 'tensor', [(j, j + 1) for j in range(k - 1, n - 1)])]
    pallas_call x1, Pallas kernels: 17.8 us -> 13.1 us  [attend(): pl.pallas_call(kernel, grid_spec=pltpu.PrefetchScalarGridSpec(num_scalar_...]
    ppermute x4 -> x6, waiting for transfers between devices: 0.01 us -> 4.16 us  [send_turn(): lax.ppermute(send_up, 'tensor', [(j, j + 1) for j in range(k - 1, n - 1)])]
  transfers between devices with their start and end apart: 16 -> 23, of which waited for: 3 -> 6; matrix products, arithmetic and copies ran while one was open for 5% -> 7% of each run, Pallas kernels for 61% -> 42%
where the time goes in v4:
time: 209 us; the launch traced here: 208 us
  Pallas kernels  101 us (48%)
  starting transfers between devices  44.5 us (21%)
  waiting for transfers between devices  38.9 us (19%)
  local copies, waits for them, and re-layouts  11.9 us (6%)
  other arithmetic  10.7 us (5%)
    pallas_call x4, Pallas kernels, project(): pl.pallas_call(kernel, grid_spec=pltpu.PrefetchScalarGridSpec(num_scalar_...  58 us
    ppermute x6, waiting for transfers between devices, send_turn(): lax.ppermute(send_down, 'tensor', [(j, j - 1) for j in range(1, n - k + 1)])  25.1 us
    ppermute x6, starting transfers between devices, send_turn(): lax.ppermute(send_up, 'tensor', [(j, j + 1) for j in range(k - 1, n - 1)])  19.4 us
    pallas_call x1, Pallas kernels, attend(): pl.pallas_call(kernel, grid_spec=pltpu.PrefetchScalarGridSpec(num_scalar_...  13.1 us
    pallas_call x2, Pallas kernels, finish_late(): pl.pallas_call(kernel, grid_spec=pltpu.PrefetchScalarGridSpec(num_scalar_...  9.84 us
    ppermute x3, waiting for transfers between devices, on_device(): lax.ppermute(low_part, 'tensor', [(i, (i + r) % n) for i in range(n)])  9.63 us
    pallas_call x1, Pallas kernels, finish(): pl.pallas_call(kernel, grid_spec=pltpu.PrefetchScalarGridSpec(num_scalar_...  8.79 us
    ppermute x6, starting transfers between devices, send_turn(): lax.ppermute(send_down, 'tensor', [(j, j - 1) for j in range(1, n - k + 1)])  7.84 us
  transfers between devices with their start and end apart: 23, of which 6 were waited for; matrix products, arithmetic and copies ran while one was open for 7% of the time, Pallas kernels for 42%

profile of v4, /device:TPU:0, one launch (start us, length us, event | category | flops | bytes accessed | tf_op | source)
XLA Modules:
  0.0 208.0 jit_solution(6537800823606608179)
XLA Ops:
  0.0 1.4 fusion.8
  1.5 0.4 copy-done.2
  1.9 1.0 slice.20
  3.0 1.3 collective-permute-start.3
  4.2 6.6 %collective-permute-start.4 = (bf16[128,4096]{1,0:T(8,128)(2,1)}, bf16[128,4096]{1,0:T(8,128)(2,1)}, u32[]{:S(2)}, u32[]{:S(2)}) collective-permute-start(bf16[128,4096]{1,0:T(8,128)(2,1)} %slice.20), channel_id=1, source_target_pairs={{0,4},{4,8},{8,12},{1,5},{5,9},{9,13},{2,6},{6,10},{10,14},{3,7},{... | collective-permute-start | bytes 3145736 | tf_op jit(solution)/shard_map/ppermute | solution.py:714
  10.8 1.3 collective-permute-start
  12.1 5.4 %collective-permute-start.1 = (bf16[128,2048]{1,0:T(8,128)(2,1)S(1)}, bf16[128,2048]{1,0:T(8,128)(2,1)}, u32[]{:S(2)}, u32[]{:S(2)}) collective-permute-start(bf16[128,2048]{1,0:T(8,128)(2,1)S(1)} %get-tuple-element.51), channel_id=1, source_target_pairs={{0,4},{4,8},{8,12},{1,5},{5,9},{9,13},{2,6},{6,10},{10,14},{3,7},{... | collective-permute-start | bytes 1572872 | tf_op jit(solution)/shard_map/ppermute | solution.py:714
  17.9 0.6 dynamic_slice.25.rows
  18.5 4.0 %shard_map.102 = (bf16[208,2048]{1,0:T(8,128)(2,1)}, bf16[208,2048]{1,0:T(8,128)(2,1)}, bf16[208,2048]{1,0:T(8,128)(2,1)}, bf16[208,2048]{1,0:T(8,128)(2,1)}) custom-call(s32[4]{0:T(128)} %dynamic_slice.25.rows, bf16[8,128,2048]{2,1,0:T(8,128)(2,1)} %down_ref.1, bf16[8,64,2048]{2,1,0:T(8,128)(2,1)} %upq_ref.1, bf16[8,64,512]{2,1,0:T(8,128)(2,1)} %upkv_ref.1), custom_call_target="tpu_custom_call" | custom-call | tf_op jit(solution)/shard_map/pallas_call | solution.py:106
  22.8 0.2 select_reduce_fusion
  23.3 1.0 fusion
  24.3 0.6 pad_add_fusion.1.info
  24.9 0.6 pad_add_fusion.6.info
  25.5 1.0 broadcast_select_fusion.3
  26.5 0.7 pad_add_fusion.info
  27.3 0.9 copy.12.idc_ref
  28.1 0.6 constant_dynamic-slice_fusion.cos_ref
  28.8 0.6 constant_dynamic-slice_fusion.4.sin_ref
  29.4 13.2 %collective-permute-done.refs_1_ = bf16[128,2048]{1,0:T(8,128)(2,1)} collective-permute-done((bf16[128,2048]{1,0:T(8,128)(2,1)S(1)}, bf16[128,2048]{1,0:T(8,128)(2,1)}, u32[]{:S(2)}, u32[]{:S(2)}) %collective-permute-start) | collective-permute-done | bytes 524320 | tf_op jit(solution)/shard_map/ppermute | solution.py:711
  42.6 1.1 collective-permute-done.1.refs_6_
  43.7 4.5 %collective-permute-start.2 = (bf16[128,2048]{1,0:T(8,128)(2,1)S(1)}, bf16[128,2048]{1,0:T(8,128)(2,1)S(1)}, u32[]{:S(2)}, u32[]{:S(2)}) collective-permute-start(bf16[128,2048]{1,0:T(8,128)(2,1)S(1)} %get-tuple-element.48), channel_id=1, source_target_pairs={{0,4},{4,8},{8,12},{1,5},{5,9},{9,13},{2,6},{6,10},{10,14},{3,7},{... | collective-permute-start | bytes 1572872 | tf_op jit(solution)/shard_map/ppermute | solution.py:714
  48.2 1.3 collective-permute-start.5
  49.5 0.6 pad_add_fusion.2.info
  50.2 0.7 constant_dynamic-slice_fusion.2.member_ref
  50.9 0.8 fusion.1
  51.7 1.6 collective-permute-start.12
  53.4 1.3 collective-permute-start.8
  54.7 0.7 collective-permute-start.9
  55.4 3.1 %collective-permute-done.2.refs_2_.refs_4_ = bf16[128,2048]{1,0:T(8,128)(2,1)S(1)} collective-permute-done((bf16[128,2048]{1,0:T(8,128)(2,1)S(1)}, bf16[128,2048]{1,0:T(8,128)(2,1)S(1)}, u32[]{:S(2)}, u32[]{:S(2)}) %collective-permute-start.2) | collective-permute-done | bytes 524320 | tf_op jit(solution)/shard_map/ppermute | solution.py:714
  58.4 0.8 copy-done.15
  59.3 5.8 %collective-permute-done.5.refs_5_.refs_3_ = bf16[128,2048]{1,0:T(8,128)(2,1)} collective-permute-done((bf16[128,2048]{1,0:T(8,128)(2,1)S(1)}, bf16[128,2048]{1,0:T(8,128)(2,1)}, u32[]{:S(2)}, u32[]{:S(2)}) %collective-permute-start.5) | collective-permute-done | bytes 524320 | tf_op jit(solution)/shard_map/ppermute | solution.py:711
  65.0 1.4 collective-permute-start.6
  66.5 0.7 collective-permute-start.7
  67.2 23.6 %shard_map.100 = (f32[384,2048]{1,0:T(8,128)}, f32[384,512]{1,0:T(8,128)}) custom-call(s32[7]{0:T(128)} %constant.150.info, bf16[128,8192]{1,0:T(8,128)(2,1)} %refs_0_.3, bf16[128,2048]{1,0:T(8,128)(2,1)} %collective-permute-done.refs_1_, bf16[128,2048]{1,0:T(8,128)(2,1)} %copy-done.15, bf16[128,4096]{1,0:T(8,128)(2,1)} %collective-permute-done.3.refs_3_.refs_2_, ...), custom_call_target="tpu_custom_call" | custom-call | flops 16106127360 | bytes 48234496 | tf_op jit(solution)/shard_map/pallas_call | solution.py:198
  90.9 1.3 collective-permute-start.10
  92.3 6.2 %collective-permute-done.6.refs_2_.refs_8_ = bf16[128,4096]{1,0:T(8,128)(2,1)S(1)} collective-permute-done((bf16[128,4096]{1,0:T(8,128)(2,1)}, bf16[128,4096]{1,0:T(8,128)(2,1)S(1)}, u32[]{:S(2)}, u32[]{:S(2)}) %collective-permute-start.6) | collective-permute-done | bytes 1048608 | tf_op jit(solution)/shard_map/ppermute | solution.py:711
  98.5 1.3 collective-permute-start.14
  99.8 1.5 collective-permute-start.15
  101.2 1.1 broadcast_select_fusion
  102.4 13.2 %shard_map.101 = (f32[128,2048]{1,0:T(8,128)}, f32[128,512]{1,0:T(8,128)}) custom-call(s32[4]{0:T(128)} %pad_add_fusion.2.info, bf16[128,2048]{1,0:T(8,128)(2,1)} %copy-done.3, bf16[128,2048]{1,0:T(8,128)(2,1)} %copy-done.4, bf16[128,4096]{1,0:T(8,128)(2,1)} %copy-done, bf16[128,4096]{1,0:T(8,128)(2,1)} %copy-done.1, bf16[8192,2048]{1,0:T(8,128)(2,1)} %weight_ref.2, ...), custom_call_target="tpu_custom_call" | custom-call | flops 4026531840 | bytes 33030144 | tf_op jit(solution)/shard_map/pallas_call | solution.py:198
  115.6 0.8 copy-done.9
  116.4 1.3 collective-permute-start.20
  117.7 0.7 concatenate.26.info
  118.4 7.7 %shard_map.103 = bf16[512,128]{1,0:T(8,128)(2,1)} custom-call(s32[25]{0:T(128)} %concatenate.26.info, bf16[128,8192]{1,0:T(8,128)(2,1)} %refs_0_.3, bf16[128,2048]{1,0:T(8,128)(2,1)} %collective-permute-done.refs_1_, bf16[128,4096]{1,0:T(8,128)(2,1)} %collective-permute-done.3.refs_3_.refs_2_, bf16[128,2048]{1,0:T(8,128)(2,1)} %collective-permute-done.5.refs_5_.refs_3_, ...), custom_call_target="tpu_custom_call" | custom-call | flops 1073741824 | bytes 4194304 | tf_op jit(solution)/shard_map/pallas_call | solution.py:286
  126.0 5.0 %collective-permute-start.16 = (bf16[512,128]{1,0:T(8,128)(2,1)}, bf16[512,128]{1,0:T(8,128)(2,1)S(1)}, u32[]{:S(2)}, u32[]{:S(2)}) collective-permute-start(bf16[512,128]{1,0:T(8,128)(2,1)} %shard_map.103), channel_id=1, source_target_pairs={{0,4},{4,8},{8,12},{12,0},{1,5},{5,9},{9,13},{13,1},{2,6},{6,10},{... | collective-permute-start | bytes 393224 | tf_op jit(solution)/shard_map/ppermute | solution.py:846
  131.1 0.6 pad_add_fusion.4.info
  131.7 0.6 pad_add_fusion.5.info
  132.3 2.4 %collective-permute-start.18 = (bf16[512,128]{1,0:T(8,128)(2,1)}, bf16[512,128]{1,0:T(8,128)(2,1)S(1)}, u32[]{:S(2)}, u32[]{:S(2)}) collective-permute-start(bf16[512,128]{1,0:T(8,128)(2,1)} %shard_map.103), channel_id=1, source_target_pairs={{0,12},{4,0},{8,4},{12,8},{1,13},{5,1},{9,5},{13,9},{2,14},{6,2},{... | collective-permute-start | bytes 393224 | tf_op jit(solution)/shard_map/ppermute | solution.py:846
  134.8 1.1 broadcast_select_fusion.1
  135.9 1.5 collective-permute-start.19
  137.3 8.0 %shard_map.104 = (f32[128,2048]{1,0:T(8,128)}, f32[128,512]{1,0:T(8,128)}) custom-call(s32[2]{0:T(128)} %pad_add_fusion.4.info, bf16[128,2048]{1,0:T(8,128)(2,1)} %collective-permute-done.14.refs_0_, bf16[128,2048]{1,0:T(8,128)(2,1)} %collective-permute-done.15.refs_1_, bf16[8192,2048]{1,0:T(8,128)(2,1)} %weight_ref.2, bf16[8192,512]{1,0:T(8,128)(2,1)} %weight_ref.3, ...), custom_call_target="tpu_custom_call" | custom-call | flops 1342177280 | bytes 11010048 | tf_op jit(solution)/shard_map/pallas_call | solution.py:198
  145.4 9.6 %collective-permute-done.18 = bf16[512,128]{1,0:T(8,128)(2,1)S(1)} collective-permute-done((bf16[512,128]{1,0:T(8,128)(2,1)}, bf16[512,128]{1,0:T(8,128)(2,1)S(1)}, u32[]{:S(2)}, u32[]{:S(2)}) %collective-permute-start.18) | collective-permute-done | bytes 131104 | tf_op jit(solution)/shard_map/ppermute | solution.py:846
  155.0 0.7 add_convert_fusion.refs_8_
  155.8 8.8 %shard_map.105 = (bf16[512,2048]{1,0:T(8,128)(2,1)}, bf16[512,256]{1,0:T(8,128)(2,1)}, bf16[512,256]{1,0:T(8,128)(2,1)}, bf16[256,2048]{1,0:T(8,128)(2,1)}, bf16[256,512]{1,0:T(8,128)(2,1)}) custom-call(s32[3]{0:T(128)} %pad_add_fusion.1.info, f32[384,2048]{1,0:T(8,128)} %get-tuple-element.52.refs_0_, f32[384,512]{1,0:T(8,128)} %get-tuple-element.53.refs_1_, ...), custom_call_target="tpu_custom_call" | custom-call | flops 671088640 | bytes 10485760 | tf_op jit(solution)/shard_map/pallas_call | solution.py:420
  164.6 0.6 collective-permute-start.21
  165.2 0.7 fusion.9
  165.9 1.0 copy-done.12
  166.8 13.2 %shard_map.106 = (f32[128,2048]{1,0:T(8,128)}, f32[128,512]{1,0:T(8,128)}) custom-call(s32[4]{0:T(128)} %pad_add_fusion.5.info, bf16[128,2048]{1,0:T(8,128)(2,1)} %copy-done.9, bf16[128,4096]{1,0:T(8,128)(2,1)} %copy-done.12, bf16[8192,2048]{1,0:T(8,128)(2,1)} %weight_ref.2, bf16[8192,512]{1,0:T(8,128)(2,1)} %weight_ref.3), custom_call_target="tpu_custom_call" | custom-call | flops 4026531840 | bytes 33030144 | tf_op jit(solution)/shard_map/pallas_call | solution.py:198
  180.1 0.8 copy-done.8
  180.9 3.9 %shard_map.108 = (bf16[128,256]{1,0:T(8,128)(2,1)}, bf16[128,256]{1,0:T(8,128)(2,1)}) custom-call(s32[3]{0:T(128)} %pad_add_fusion.6.info, bf16[128,2048]{1,0:T(8,128)(2,1)} %copy-done.8, bf16[8192,512]{1,0:T(8,128)(2,1)} %weight_ref.3, f32[128,512]{1,0:T(8,128)} %get-tuple-element.82.sum_ref, bf16[128,64]{1,0:T(8,128)(2,1)} %get-tuple-element.93.low_ref, ...), custom_call_target="tpu_custom_call" | custom-call | flops 301989888 | bytes 2097152 | tf_op jit(solution)/shard_map/pallas_call | solution.py:505
  184.7 3.4 %collective-permute-start.22 = (bf16[128,256]{1,0:T(8,128)(2,1)}, bf16[128,256]{1,0:T(8,128)(2,1)S(1)}, u32[]{:S(2)}, u32[]{:S(2)}) collective-permute-start(bf16[128,256]{1,0:T(8,128)(2,1)} %get-tuple-element.86), channel_id=1, source_target_pairs={{0,4},{12,8},{1,5},{13,9},{2,6},{14,10},{3,7},{15,11},{16,20},{28,... | collective-permute-start | bytes 196616 | tf_op jit(solution)/shard_map/ppermute | solution.py:898
  188.1 6.0 %shard_map.107.ql_ref = bf16[128,2048]{1,0:T(8,128)(2,1)} custom-call(s32[1]{0:T(128)} %bitcast.14.info, bf16[128,2048]{1,0:T(8,128)(2,1)} %copy-done.8, bf16[8192,2048]{1,0:T(8,128)(2,1)} %weight_ref.2, f32[128,2048]{1,0:T(8,128)} %get-tuple-element.79.sum_ref, bf16[128,64]{1,0:T(8,128)(2,1)} %get-tuple-element.94.low_ref, ...), custom_call_target="tpu_custom_call" | custom-call | flops 1207959552 | bytes 8388608 | tf_op jit(solution)/shard_map/pallas_call | solution.py:505
  194.1 0.7 copy-done.20
  194.9 13.1 %shard_map.109 = bf16[512,2048]{1,0:T(8,128)(2,1)} custom-call(s32[3]{0:T(128)} %pad_add_fusion.info, bf16[512,2048]{1,0:T(8,128)(2,1)} %get-tuple-element.76.q_ref, bf16[128,2048]{1,0:T(8,128)(2,1)} %shard_map.107.ql_ref, bf16[512,256]{1,0:T(8,128)(2,1)} %get-tuple-element.81.m_ref, bf16[128,256]{1,0:T(8,128)(2,1)} %get-tuple-element.84.ml_ref, ...), custom_call_target="tpu_custom_call" | custom-call | flops 2147483648 | bytes 4194304 | tf_op jit(solution)/shard_map/pallas_call | solution.py:607
  (69 shorter events, 1.3 us)
Async XLA Ops:
  0.0 1.9 copy-start.2
  0.0 17.5 %copy-start.19 = (s32[32]{0:T(128)S(1)}, s32[32]{0:T(128)}, u32[]{:S(2)}) copy-start(s32[32]{0:T(128)} %param.16) | copy-start | bytes 388
  0.0 17.5 %copy-start.18 = (s32[4,4]{1,0:T(4,128)S(1)}, s32[4,4]{1,0:T(4,128)}, u32[]{:S(2)}) copy-start(s32[4,4]{1,0:T(4,128)} %param.17) | copy-start | bytes 196
  3.0 50.4 %collective-permute-start.3 = (bf16[128,4096]{1,0:T(8,128)(2,1)}, bf16[128,4096]{1,0:T(8,128)(2,1)}, u32[]{:S(2)}, u32[]{:S(2)}) collective-permute-start(bf16[128,4096]{1,0:T(8,128)(2,1)} %slice.20), channel_id=1, source_target_pairs={{4,0},{8,4},{12,8},{5,1},{9,5},{13,9},{6,2},{10,6},{14,10},{7,3},{... | collective-permute-start | bytes 3145736 | tf_op jit(solution)/shard_map/ppermute | solution.py:711
  4.2 49.1 %collective-permute-start.4 = (bf16[128,4096]{1,0:T(8,128)(2,1)}, bf16[128,4096]{1,0:T(8,128)(2,1)}, u32[]{:S(2)}, u32[]{:S(2)}) collective-permute-start(bf16[128,4096]{1,0:T(8,128)(2,1)} %slice.20), channel_id=1, source_target_pairs={{0,4},{4,8},{8,12},{1,5},{5,9},{9,13},{2,6},{6,10},{10,14},{3,7},{... | collective-permute-start | bytes 3145736 | tf_op jit(solution)/shard_map/ppermute | solution.py:714
  10.8 31.8 %collective-permute-start = (bf16[128,2048]{1,0:T(8,128)(2,1)S(1)}, bf16[128,2048]{1,0:T(8,128)(2,1)}, u32[]{:S(2)}, u32[]{:S(2)}) collective-permute-start(bf16[128,2048]{1,0:T(8,128)(2,1)S(1)} %get-tuple-element.48), channel_id=1, source_target_pairs={{4,0},{8,4},{12,8},{5,1},{9,5},{13,9},{6,2},{10,6},{14,10},{7,3},{... | collective-permute-start | bytes 1572872 | tf_op jit(solution)/shard_map/ppermute | solution.py:711
  12.1 31.5 %collective-permute-start.1 = (bf16[128,2048]{1,0:T(8,128)(2,1)S(1)}, bf16[128,2048]{1,0:T(8,128)(2,1)}, u32[]{:S(2)}, u32[]{:S(2)}) collective-permute-start(bf16[128,2048]{1,0:T(8,128)(2,1)S(1)} %get-tuple-element.51), channel_id=1, source_target_pairs={{0,4},{4,8},{8,12},{1,5},{5,9},{9,13},{2,6},{6,10},{10,14},{3,7},{... | collective-permute-start | bytes 1572872 | tf_op jit(solution)/shard_map/ppermute | solution.py:714
  18.5 4.2 %copy-start.17 = (s32[1,512]{1,0:T(1,128)S(1)}, s32[1,512]{1,0:T(1,128)}, u32[]{:S(2)}) copy-start(s32[1,512]{1,0:T(1,128)} %idr_ref.1) | copy-start | bytes 6148
  22.5 29.2 %collective-permute-start.11 = (bf16[208,2048]{1,0:T(8,128)(2,1)}, bf16[208,2048]{1,0:T(8,128)(2,1)S(1)}, u32[]{:S(2)}, u32[]{:S(2)}) collective-permute-start(bf16[208,2048]{1,0:T(8,128)(2,1)} %get-tuple-element.65), channel_id=1, source_target_pairs={{0,1},{1,2},{2,3},{3,0},{4,5},{5,6},{6,7},{7,4},{8,9},{9,10},{10,1... | collective-permute-start | bytes 2555912 | tf_op jit(solution)/shard_map/ppermute | solution.py:751
  26.5 26.8 %copy-start.11 = (f32[512,128]{1,0:T(8,128)}, f32[512,128]{1,0:T(8,128)S(1)}, u32[]{:S(2)}) copy-start(f32[512,128]{1,0:T(8,128)S(1)} %get-tuple-element.99.refs_12_) | copy-start | bytes 786436
  26.5 38.5 %copy-start.10 = (f32[512,128]{1,0:T(8,128)}, f32[512,128]{1,0:T(8,128)S(1)}, u32[]{:S(2)}) copy-start(f32[512,128]{1,0:T(8,128)S(1)} %get-tuple-element.87.refs_13_) | copy-start | bytes 786436
  43.7 14.8 %collective-permute-start.2 = (bf16[128,2048]{1,0:T(8,128)(2,1)S(1)}, bf16[128,2048]{1,0:T(8,128)(2,1)S(1)}, u32[]{:S(2)}, u32[]{:S(2)}) collective-permute-start(bf16[128,2048]{1,0:T(8,128)(2,1)S(1)} %get-tuple-element.48), channel_id=1, source_target_pairs={{0,4},{4,8},{8,12},{1,5},{5,9},{9,13},{2,6},{6,10},{10,14},{3,7},{... | collective-permute-start | bytes 1572872 | tf_op jit(solution)/shard_map/ppermute | solution.py:714
  48.2 16.9 %collective-permute-start.5 = (bf16[128,2048]{1,0:T(8,128)(2,1)S(1)}, bf16[128,2048]{1,0:T(8,128)(2,1)}, u32[]{:S(2)}, u32[]{:S(2)}) collective-permute-start(bf16[128,2048]{1,0:T(8,128)(2,1)S(1)} %get-tuple-element.51), channel_id=1, source_target_pairs={{4,0},{8,4},{12,8},{5,1},{9,5},{13,9},{6,2},{10,6},{14,10},{7,3},{... | collective-permute-start | bytes 1572872 | tf_op jit(solution)/shard_map/ppermute | solution.py:711
  50.2 40.6 %copy-start.7 = (f32[512,4]{1,0:T(8,128)}, f32[512,4]{1,0:T(8,128)S(1)}, u32[]{:S(2)}) copy-start(f32[512,4]{1,0:T(8,128)S(1)} %compare_convert_fusion.refs_16_.refs_9_) | copy-start | bytes 24580
  51.7 6.7 %copy-start.5 = (bf16[208,2048]{1,0:T(8,128)(2,1)}, bf16[208,2048]{1,0:T(8,128)(2,1)S(1)}, u32[]{:S(2)}) copy-start(bf16[208,2048]{1,0:T(8,128)(2,1)S(1)} %collective-permute-done.11.refs_13_.refs_5_) | copy-start | bytes 2555908
  51.7 40.5 %collective-permute-start.12 = (bf16[208,2048]{1,0:T(8,128)(2,1)}, bf16[208,2048]{1,0:T(8,128)(2,1)S(1)}, u32[]{:S(2)}, u32[]{:S(2)}) collective-permute-start(bf16[208,2048]{1,0:T(8,128)(2,1)} %get-tuple-element.67), channel_id=1, source_target_pairs={{0,2},{1,3},{2,0},{3,1},{4,6},{5,7},{6,4},{7,5},{8,10},{9,11},{10,... | collective-permute-start | bytes 2555912 | tf_op jit(solution)/shard_map/ppermute | solution.py:751
  53.4 37.5 %collective-permute-start.8 = (bf16[128,2048]{1,0:T(8,128)(2,1)}, bf16[128,2048]{1,0:T(8,128)(2,1)S(1)}, u32[]{:S(2)}, u32[]{:S(2)}) collective-permute-start(bf16[128,2048]{1,0:T(8,128)(2,1)} %collective-permute-done.refs_1_), channel_id=1, source_target_pairs={{4,0},{8,4},{5,1},{9,5},{6,2},{10,6},{7,3},{11,7},{20,16},{24,20},... | collective-permute-start | bytes 1572872 | tf_op jit(solution)/shard_map/ppermute | solution.py:711
  54.7 36.2 %collective-permute-start.9 = (bf16[128,2048]{1,0:T(8,128)(2,1)}, bf16[128,2048]{1,0:T(8,128)(2,1)S(1)}, u32[]{:S(2)}, u32[]{:S(2)}) collective-permute-start(bf16[128,2048]{1,0:T(8,128)(2,1)} %collective-permute-done.1.refs_6_), channel_id=1, source_target_pairs={{4,8},{8,12},{5,9},{9,13},{6,10},{10,14},{7,11},{11,15},{20,24},{2... | collective-permute-start | bytes 1572872 | tf_op jit(solution)/shard_map/ppermute | solution.py:714
  58.4 0.8 copy-start.15
  65.0 34.7 %copy-start.16 = (bf16[128,2048]{1,0:T(8,128)(2,1)S(1)}, bf16[128,2048]{1,0:T(8,128)(2,1)}, u32[]{:S(2)}) copy-start(bf16[128,2048]{1,0:T(8,128)(2,1)} %copy-done.15) | copy-start | bytes 1572868
  65.0 33.4 %collective-permute-start.6 = (bf16[128,4096]{1,0:T(8,128)(2,1)}, bf16[128,4096]{1,0:T(8,128)(2,1)S(1)}, u32[]{:S(2)}, u32[]{:S(2)}) collective-permute-start(bf16[128,4096]{1,0:T(8,128)(2,1)} %collective-permute-done.3.refs_3_.refs_2_), channel_id=1, source_target_pairs={{4,0},{8,4},{5,1},{9,5},{6,2},{10,6},{7,3},{11,7},{20,16},{24,20},... | collective-permute-start | bytes 3145736 | tf_op jit(solution)/shard_map/ppermute | solution.py:711
  66.5 32.0 %collective-permute-start.7 = (bf16[128,4096]{1,0:T(8,128)(2,1)}, bf16[128,4096]{1,0:T(8,128)(2,1)S(1)}, u32[]{:S(2)}, u32[]{:S(2)}) collective-permute-start(bf16[128,4096]{1,0:T(8,128)(2,1)} %collective-permute-done.4.refs_4_.refs_5_), channel_id=1, source_target_pairs={{4,8},{8,12},{5,9},{9,13},{6,10},{10,14},{7,11},{11,15},{20,24},{2... | collective-permute-start | bytes 3145736 | tf_op jit(solution)/shard_map/ppermute | solution.py:714
  90.8 11.5 %copy-start.3 = (bf16[128,2048]{1,0:T(8,128)(2,1)}, bf16[128,2048]{1,0:T(8,128)(2,1)S(1)}, u32[]{:S(2)}) copy-start(bf16[128,2048]{1,0:T(8,128)(2,1)S(1)} %collective-permute-done.8.refs_0_.refs_7_) | copy-start | bytes 1572868
  90.9 11.5 %copy-start.4 = (bf16[128,2048]{1,0:T(8,128)(2,1)}, bf16[128,2048]{1,0:T(8,128)(2,1)S(1)}, u32[]{:S(2)}) copy-start(bf16[128,2048]{1,0:T(8,128)(2,1)S(1)} %collective-permute-done.9.refs_1_.refs_10_) | copy-start | bytes 1572868
  90.9 24.6 %collective-permute-start.10 = (bf16[128,2048]{1,0:T(8,128)(2,1)S(1)}, bf16[128,2048]{1,0:T(8,128)(2,1)S(1)}, u32[]{:S(2)}, u32[]{:S(2)}) collective-permute-start(bf16[128,2048]{1,0:T(8,128)(2,1)S(1)} %broadcast_select_fusion.2), channel_id=1, source_target_pairs={{4,0},{8,12},{5,1},{9,13},{6,2},{10,14},{7,3},{11,15},{20,16},{24,... | collective-permute-start | bytes 1572872 | tf_op jit(solution)/shard_map/ppermute | solution.py:701
  92.2 23.3 %copy-start.6 = (bf16[208,2048]{1,0:T(8,128)(2,1)}, bf16[208,2048]{1,0:T(8,128)(2,1)S(1)}, u32[]{:S(2)}) copy-start(bf16[208,2048]{1,0:T(8,128)(2,1)S(1)} %collective-permute-done.12.refs_14_.refs_6_) | copy-start | bytes 2555908
  92.3 26.1 %collective-permute-start.13 = (bf16[208,2048]{1,0:T(8,128)(2,1)}, bf16[208,2048]{1,0:T(8,128)(2,1)}, u32[]{:S(2)}, u32[]{:S(2)}) collective-permute-start(bf16[208,2048]{1,0:T(8,128)(2,1)} %get-tuple-element.69), channel_id=1, source_target_pairs={{0,3},{1,0},{2,1},{3,2},{4,7},{5,4},{6,5},{7,6},{8,11},{9,8},{10,9... | collective-permute-start | bytes 2555912 | tf_op jit(solution)/shard_map/ppermute | solution.py:751
  98.5 3.9 %copy-start = (bf16[128,4096]{1,0:T(8,128)(2,1)}, bf16[128,4096]{1,0:T(8,128)(2,1)S(1)}, u32[]{:S(2)}) copy-start(bf16[128,4096]{1,0:T(8,128)(2,1)S(1)} %collective-permute-done.6.refs_2_.refs_8_) | copy-start | bytes 3145732
  98.5 3.9 %copy-start.1 = (bf16[128,4096]{1,0:T(8,128)(2,1)}, bf16[128,4096]{1,0:T(8,128)(2,1)S(1)}, u32[]{:S(2)}) copy-start(bf16[128,4096]{1,0:T(8,128)(2,1)S(1)} %collective-permute-done.7.refs_3_.refs_9_) | copy-start | bytes 3145732
  98.5 33.8 %collective-permute-start.14 = (bf16[128,2048]{1,0:T(8,128)(2,1)}, bf16[128,2048]{1,0:T(8,128)(2,1)}, u32[]{:S(2)}, u32[]{:S(2)}) collective-permute-start(bf16[128,2048]{1,0:T(8,128)(2,1)} %collective-permute-done.5.refs_5_.refs_3_), channel_id=1, source_target_pairs={{4,0},{8,4},{5,1},{9,5},{6,2},{10,6},{7,3},{11,7},{20,16},{24,20},... | collective-permute-start | bytes 1572872 | tf_op jit(solution)/shard_map/ppermute | solution.py:711
  99.8 35.0 %collective-permute-start.15 = (bf16[128,2048]{1,0:T(8,128)(2,1)S(1)}, bf16[128,2048]{1,0:T(8,128)(2,1)}, u32[]{:S(2)}, u32[]{:S(2)}) collective-permute-start(bf16[128,2048]{1,0:T(8,128)(2,1)S(1)} %copy-done.16), channel_id=1, source_target_pairs={{4,8},{8,12},{5,9},{9,13},{6,10},{10,14},{7,11},{11,15},{20,24},{2... | collective-permute-start | bytes 1572872 | tf_op jit(solution)/shard_map/ppermute | solution.py:714
  115.6 0.8 copy-start.9
  116.4 49.5 %collective-permute-start.20 = (bf16[128,4096]{1,0:T(8,128)(2,1)}, bf16[128,4096]{1,0:T(8,128)(2,1)S(1)}, u32[]{:S(2)}, u32[]{:S(2)}) collective-permute-start(bf16[128,4096]{1,0:T(8,128)(2,1)} %broadcast_select_fusion), channel_id=1, source_target_pairs={{4,0},{8,12},{5,1},{9,13},{6,2},{10,14},{7,3},{11,15},{20,16},{24,... | collective-permute-start | bytes 3145736 | tf_op jit(solution)/shard_map/ppermute | solution.py:701
  126.0 19.4 %collective-permute-start.16 = (bf16[512,128]{1,0:T(8,128)(2,1)}, bf16[512,128]{1,0:T(8,128)(2,1)S(1)}, u32[]{:S(2)}, u32[]{:S(2)}) collective-permute-start(bf16[512,128]{1,0:T(8,128)(2,1)} %shard_map.103), channel_id=1, source_target_pairs={{0,4},{4,8},{8,12},{12,0},{1,5},{5,9},{9,13},{13,1},{2,6},{6,10},{... | collective-permute-start | bytes 393224 | tf_op jit(solution)/shard_map/ppermute | solution.py:846
  131.1 14.3 %collective-permute-start.17 = (bf16[512,128]{1,0:T(8,128)(2,1)}, bf16[512,128]{1,0:T(8,128)(2,1)S(1)}, u32[]{:S(2)}, u32[]{:S(2)}) collective-permute-start(bf16[512,128]{1,0:T(8,128)(2,1)} %shard_map.103), channel_id=1, source_target_pairs={{0,8},{4,12},{8,0},{12,4},{1,9},{5,13},{9,1},{13,5},{2,10},{6,14},... | collective-permute-start | bytes 393224 | tf_op jit(solution)/shard_map/ppermute | solution.py:846
  132.3 22.7 %collective-permute-start.18 = (bf16[512,128]{1,0:T(8,128)(2,1)}, bf16[512,128]{1,0:T(8,128)(2,1)S(1)}, u32[]{:S(2)}, u32[]{:S(2)}) collective-permute-start(bf16[512,128]{1,0:T(8,128)(2,1)} %shard_map.103), channel_id=1, source_target_pairs={{0,12},{4,0},{8,4},{12,8},{1,13},{5,1},{9,5},{13,9},{2,14},{6,2},{... | collective-permute-start | bytes 393224 | tf_op jit(solution)/shard_map/ppermute | solution.py:846
  135.9 44.2 %collective-permute-start.19 = (bf16[128,2048]{1,0:T(8,128)(2,1)S(1)}, bf16[128,2048]{1,0:T(8,128)(2,1)S(1)}, u32[]{:S(2)}, u32[]{:S(2)}) collective-permute-start(bf16[128,2048]{1,0:T(8,128)(2,1)S(1)} %broadcast_select_fusion.1), channel_id=1, source_target_pairs={{4,0},{8,12},{5,1},{9,13},{6,2},{10,14},{7,3},{11,15},{20,16},{24,... | collective-permute-start | bytes 1572872 | tf_op jit(solution)/shard_map/ppermute | solution.py:701
  137.3 17.7 %copy-start.14 = (bf16[512,128]{1,0:T(8,128)(2,1)S(1)}, bf16[512,128]{1,0:T(8,128)(2,1)}, u32[]{:S(2)}) copy-start(bf16[512,128]{1,0:T(8,128)(2,1)} %shard_map.103) | copy-start | bytes 393220
  155.8 9.4 %copy-start.13 = (bf16[512,128]{1,0:T(8,128)(2,1)S(1)}, bf16[512,128]{1,0:T(8,128)(2,1)}, u32[]{:S(2)}) copy-start(bf16[512,128]{1,0:T(8,128)(2,1)} %add_convert_fusion.refs_8_) | copy-start | bytes 393220
  164.6 29.5 %collective-permute-start.21 = (bf16[512,256]{1,0:T(8,128)(2,1)}, bf16[512,256]{1,0:T(8,128)(2,1)S(1)}, u32[]{:S(2)}, u32[]{:S(2)}) collective-permute-start(bf16[512,256]{1,0:T(8,128)(2,1)} %get-tuple-element.85), channel_id=1, source_target_pairs={{0,4},{4,0},{8,12},{12,8},{1,5},{5,1},{9,13},{13,9},{2,6},{6,2},{1... | collective-permute-start | bytes 786440 | tf_op jit(solution)/shard_map/ppermute | solution.py:872
  165.9 1.0 copy-start.12
  180.1 0.8 copy-start.8
  184.7 9.4 %collective-permute-start.22 = (bf16[128,256]{1,0:T(8,128)(2,1)}, bf16[128,256]{1,0:T(8,128)(2,1)S(1)}, u32[]{:S(2)}, u32[]{:S(2)}) collective-permute-start(bf16[128,256]{1,0:T(8,128)(2,1)} %get-tuple-element.86), channel_id=1, source_target_pairs={{0,4},{12,8},{1,5},{13,9},{2,6},{14,10},{3,7},{15,11},{16,20},{28,... | collective-permute-start | bytes 196616 | tf_op jit(solution)/shard_map/ppermute | solution.py:898
  194.1 0.7 copy-start.20
  194.1 0.7 copy-start.21

commit v5 on v4

--- a/solution.py
+++ b/solution.py
@@ -121,9 +121,9 @@
     )(local, down_maps, up_query, up_keyval)
 
 
-def project(candidates, picks, chunk_ids, chunk, weights, starts=None):
+def project(candidates, picks, chunk_ids, chunk, weights, starts=None, start_group=0):
     steps, groups = len(candidates), len(candidates[0])
-    rows = candidates[0][0][0][0].shape[0]
+    rows = next(x.shape[0] for group in candidates[0] for x, _ in group)
     block = min(1024, chunk)
     sub = chunk // block
     blocks = steps * sub
@@ -156,7 +156,10 @@
         for a in range(steps):
             for r in range(groups):
                 target = held.at[a, pl.ds(r * rows, rows), :]
-                start_picked(sources[a][r], info[r], chunk, target, sems.at[a, r])
+                if sources[a][r]:
+                    start_picked(sources[a][r], info[r], chunk, target, sems.at[a, r])
+                else:
+                    target[...] = jnp.zeros(target.shape, BF16)
             if a == 0:
                 for i in range(ahead):
                     for load in loads(i, i):
@@ -168,11 +171,16 @@
             slot = lax.rem(i, ahead)
             at, part_at = i // sub, lax.rem(i, sub)
 
-            @pl.when(part_at == 0)
-            def _():
-                for r in range(groups):
+            for r in range(groups):
+                here = [a for a in range(steps) if sources[a][r]]
+                first_piece = part_at == 0
+                if len(here) < steps:
+                    first_piece &= functools.reduce(jnp.logical_or, [at == a for a in here])
+
+                @pl.when(first_piece)
+                def _(r=r, source=sources[here[0]][r][0][0]):
                     pltpu.make_async_copy(
-                        sources[0][r][0][0].at[:, pl.ds(0, chunk)],
+                        source.at[:, pl.ds(0, chunk)],
                         held.at[at, pl.ds(r * rows, rows), :],
                         sems.at[at, r],
                     ).wait()
@@ -201,7 +209,11 @@
             num_scalar_prefetch=1,
             grid=(1,),
             in_specs=[ANY] * (len(arrays) + count)
-            + ([whole((height, w)) for w in widths] if starts is not None else []),
+            + (
+                [pl.BlockSpec((height, w), lambda g, info: (start_group, 0)) for w in widths]
+                if starts is not None
+                else []
+            ),
             out_specs=[whole((height, w)) for w in widths],
             scratch_shapes=[pltpu.VMEM((ahead, block, w), BF16) for w in widths]
             + [
@@ -535,7 +547,7 @@
     heads = width // HEAD_SIZE
     used = mine.shape[1] // HEAD_SIZE
     per_kv = heads // used
-    together = min(4, per_kv)
+    together = min(8, per_kv)
     span = together * HEAD_SIZE
     scale = math.log2(math.e) / math.sqrt(HEAD_SIZE)
     tiles = total // TILE
@@ -567,10 +579,10 @@
             for tile in range(tiles):
                 first = max(0, tile - back) * TILE
                 size = (tile + 1) * TILE - first
-                key_index = lax.broadcasted_iota(jnp.int32, (size, TILE), 0) + first
-                row_index = lax.broadcasted_iota(jnp.int32, (size, TILE), 1) + tile * TILE
-                same = idc_ref[first : first + size, :] == idr_ref[:, tile * TILE : (tile + 1) * TILE]
-                bias_ref[tile, :size, :] = jnp.where(same & (row_index >= key_index), 0.0, -1e30)
+                row_index = lax.broadcasted_iota(jnp.int32, (TILE, size), 0) + tile * TILE
+                key_index = lax.broadcasted_iota(jnp.int32, (TILE, size), 1) + first
+                same = idc_ref[tile * TILE : (tile + 1) * TILE, :] == idr_ref[:, first : first + size]
+                bias_ref[tile, :, :size] = jnp.where(same & (row_index >= key_index), 0.0, -1e30)
 
         held_q[...] = q_ref[...]
 
@@ -586,22 +598,19 @@
             keys = k_ref[first : first + size, kv_at]
             values = v_ref[first : first + size, kv_at]
             values = jnp.concatenate([values, jnp.ones_like(values)], axis=1)
+            queries = jnp.concatenate(
+                [held_q[at, h * HEAD_SIZE : (h + 1) * HEAD_SIZE] for h in range(together)], axis=0
+            )
+            scores = lax.dot_general(
+                queries, keys, (((1,), (1,)), ((), ())), preferred_element_type=F32
+            ).reshape(together, TILE, size)
+            scores = scores * scale + bias_ref[tile, :, :size][None]
+            top = jnp.max(scores, axis=2, keepdims=True)
+            weights = jnp.exp2(scores - top).astype(BF16).reshape(together * TILE, size)
+            mixed = jnp.dot(weights, values, preferred_element_type=F32)
+            mixed = (mixed[:, :HEAD_SIZE] / mixed[:, HEAD_SIZE:]).astype(BF16)
             for h in range(together):
-                scores = lax.dot_general(
-                    keys,
-                    held_q[at, h * HEAD_SIZE : (h + 1) * HEAD_SIZE],
-                    (((1,), (1,)), ((), ())),
-                    preferred_element_type=F32,
-                )
-                scores = scores * scale + bias_ref[tile, :size, :]
-                top = jnp.max(scores, axis=0, keepdims=True)
-                weights = jnp.exp2(scores - top).astype(BF16)
-                mixed = lax.dot_general(
-                    weights, values, (((0,), (0,)), ((), ())), preferred_element_type=F32
-                )
-                out_ref[at, h * HEAD_SIZE : (h + 1) * HEAD_SIZE] = (
-                    mixed[:, :HEAD_SIZE] / mixed[:, HEAD_SIZE:]
-                ).astype(BF16)
+                out_ref[at, h * HEAD_SIZE : (h + 1) * HEAD_SIZE] = mixed[h * TILE : (h + 1) * TILE]
 
     by_heads = pl.BlockSpec((total, span), lambda g, info: (0, g))
     return pl.pallas_call(
@@ -623,7 +632,7 @@
             scratch_shapes=[
                 pltpu.VMEM(mine.shape, BF16),
                 pltpu.VMEM(mine.shape, BF16),
-                pltpu.VMEM((tiles, longest, TILE), F32),
+                pltpu.VMEM((tiles, TILE, longest), F32),
                 pltpu.VMEM((total, span), BF16),
             ],
         ),
@@ -803,24 +812,17 @@
         sources.append((q, kv, first, lambda b, zz, k=k: b == zz + k))
         sources.append((q, kv, first + rows, lambda b, zz, k=k: b == zz - k))
 
-    def far_block(k, some, picks, starts=None):
-        return project(
-            [[sided(k, a)] for a in some],
-            picks,
-            jnp.stack([side_chunks[a] for a in some]),
+    for k in range(half, late - 1):
+        send_until(place[k, rear] + 2)
+        q, kv = project(
+            [[sided(k, a)] for a in range(chunks)],
+            jnp.stack([side]),
+            jnp.stack(side_chunks),
             chunk_width,
             weights,
-            starts,
         )
-
-    for k in range(half, late - 1):
-        send_until(place[k, rear] + 2)
-        q, kv = far_block(k, range(chunks), jnp.stack([side]))
         hold[place[k + 1, front] + 2] = kv
         sources.append((q, kv, 0, lambda b, zz, k=k: (b == zz + k) | (b == zz - k)))
-    send_until(place[late - 1, rear])
-    begun = far_block(late - 1, range(chunks - 1), jnp.stack([side]))
-    hold[place[late, middle]] = begun[1]
     send_until(place[late, middle])
 
     def home(way, k, c):
@@ -845,9 +847,16 @@
     for r in range(1, n):
         low += lax.ppermute(low_part, "tensor", [(i, (i + r) % n) for i in range(n)]).astype(F32)
     low = low.astype(BF16)
-    q, kv = far_block(late - 1, [chunks - 1], after(jnp.stack([side]), low_part), begun)
+    front_in, middle_in, back_in = (last_in[piece] for piece in (front, middle, rear))
+    q, kv = project(
+        [[sided(late - 1, a), [(front_in, 0)] if a == 0 else []] for a in range(chunks)],
+        after(jnp.stack([side, side]), low_part),
+        jnp.stack(side_chunks),
+        chunk_width,
+        weights,
+    )
+    late_begun = [q, kv]
     sources.append((q, kv, 0, lambda b, zz: (b == zz + late - 1) | (b == zz - late + 1)))
-    front_in, middle_in, back_in = (last_in[piece] for piece in (front, middle, rear))
 
     group_size = QUERY_HEADS // KEY_VALUE_HEADS
     head_local = query_width // HEAD_SIZE
@@ -871,11 +880,13 @@
     )
     recv = lax.ppermute(send, "tensor", [(i, i ^ 1) for i in range(n)])
     late_q, late_kv = project(
-        [[[(front_in, 0)]]] + [[[(middle_in, a * chunk_width)]] for a in range(chunks - 2)],
-        after(jnp.zeros((1,), jnp.int32), low_part),
-        jnp.stack([side_chunks[0]] + list(range(1, chunks - 1))),
+        [[[(middle_in, a * chunk_width)]] for a in range(chunks - 2)],
+        after(jnp.zeros((1,), jnp.int32), mine),
+        jnp.arange(1, chunks - 1, dtype=jnp.int32),
         chunk_width,
         weights,
+        late_begun,
+        1,
     )
 
     late_block = jnp.where(side == 0, n - 1, 0)

time: 209 us -> 199 us (0.952)
  Pallas kernels: 101 us -> 90.8 us
  waiting for transfers between devices: 38.9 us -> 42.4 us
    ppermute x6, waiting for transfers between devices: 25.1 us -> 10.5 us  [send_turn(): lax.ppermute(send_down, 'tensor', [(j, j - 1) for j in range(1, n - k + 1)])]
    ppermute x6, waiting for transfers between devices: 4.16 us -> 16.2 us  [send_turn(): lax.ppermute(send_up, 'tensor', [(j, j + 1) for j in range(k - 1, n - 1)])]
    ppermute x3, waiting for transfers between devices: 0.01 us -> 11.9 us  [send_turn(): came[i] = (lax.ppermute(send, 'tensor', [(1, 0), (n - 2, n - 1)]),)]
    ppermute x3, waiting for transfers between devices: 9.63 us -> 3.83 us  [on_device(): lax.ppermute(low_part, 'tensor', [(i, (i + r) % n) for i in range(n)])]
    pallas_call x4 -> x3, Pallas kernels: 58 us -> 52.6 us  [project(): pl.pallas_call(kernel, grid_spec=pltpu.PrefetchScalarGridSpec(num_scalar_...]
    pallas_call x1, Pallas kernels: 13.1 us -> 7.97 us  [attend(): pl.pallas_call(kernel, grid_spec=pltpu.PrefetchScalarGridSpec(num_scalar_...]
  transfers between devices with their start and end apart: 23 -> 23, of which waited for: 6 -> 4; matrix products, arithmetic and copies ran while one was open for 7% -> 8% of each run, Pallas kernels for 42% -> 42%
where the time goes in v5:
time: 199 us; the launch traced here: 198 us
  Pallas kernels  90.8 us (46%)
  starting transfers between devices  43.8 us (22%)
  waiting for transfers between devices  42.4 us (21%)
  local copies, waits for them, and re-layouts  11.3 us (6%)
  other arithmetic  9.49 us (5%)
    pallas_call x3, Pallas kernels, project(): pl.pallas_call(kernel, grid_spec=pltpu.PrefetchScalarGridSpec(num_scalar_...  52.6 us
    ppermute x6, starting transfers between devices, send_turn(): lax.ppermute(send_up, 'tensor', [(j, j + 1) for j in range(k - 1, n - 1)])  17.8 us
    ppermute x6, waiting for transfers between devices, send_turn(): lax.ppermute(send_up, 'tensor', [(j, j + 1) for j in range(k - 1, n - 1)])  16.2 us
    ppermute x3, waiting for transfers between devices, send_turn(): came[i] = (lax.ppermute(send, 'tensor', [(1, 0), (n - 2, n - 1)]),)  11.9 us
    ppermute x6, waiting for transfers between devices, send_turn(): lax.ppermute(send_down, 'tensor', [(j, j - 1) for j in range(1, n - k + 1)])  10.5 us
    pallas_call x2, Pallas kernels, finish_late(): pl.pallas_call(kernel, grid_spec=pltpu.PrefetchScalarGridSpec(num_scalar_...  9.81 us
    pallas_call x1, Pallas kernels, finish(): pl.pallas_call(kernel, grid_spec=pltpu.PrefetchScalarGridSpec(num_scalar_...  8.8 us
    pallas_call x1, Pallas kernels, attend(): pl.pallas_call(kernel, grid_spec=pltpu.PrefetchScalarGridSpec(num_scalar_...  7.97 us
  transfers between devices with their start and end apart: 23, of which 4 were waited for; matrix products, arithmetic and copies ran while one was open for 8% of the time, Pallas kernels for 42%

profile of v5, /device:TPU:0, one launch (start us, length us, event | category | flops | bytes accessed | tf_op | source)
XLA Modules:
  0.0 198.2 jit_solution(4963036047468786782)
XLA Ops:
  0.0 2.2 %fusion.8 = (bf16[128,2048]{1,0:T(8,128)(2,1)S(1)}, bf16[128,2048]{1,0:T(8,128)(2,1)}) fusion(bf16[128,8192]{1,0:T(8,128)(2,1)} %refs_0_.3), kind=kLoop, calls=%fused_computation.57 | loop fusion | bytes 2097152 | tf_op jit(solution)/shard_map/slice | solution.py:697
  2.2 1.3 collective-permute-start
  3.5 6.4 %collective-permute-start.1 = (bf16[128,2048]{1,0:T(8,128)(2,1)S(1)}, bf16[128,2048]{1,0:T(8,128)(2,1)}, u32[]{:S(2)}, u32[]{:S(2)}) collective-permute-start(bf16[128,2048]{1,0:T(8,128)(2,1)S(1)} %get-tuple-element.49), channel_id=1, source_target_pairs={{0,4},{4,8},{8,12},{1,5},{5,9},{9,13},{2,6},{6,10},{10,14},{3,7},{... | collective-permute-start | bytes 1572872 | tf_op jit(solution)/shard_map/ppermute | solution.py:723
  9.9 1.0 slice.20
  10.9 1.3 collective-permute-start.3
  12.2 5.6 %collective-permute-start.4 = (bf16[128,4096]{1,0:T(8,128)(2,1)}, bf16[128,4096]{1,0:T(8,128)(2,1)}, u32[]{:S(2)}, u32[]{:S(2)}) collective-permute-start(bf16[128,4096]{1,0:T(8,128)(2,1)} %slice.20), channel_id=1, source_target_pairs={{0,4},{4,8},{8,12},{1,5},{5,9},{9,13},{2,6},{6,10},{10,14},{3,7},{... | collective-permute-start | bytes 3145736 | tf_op jit(solution)/shard_map/ppermute | solution.py:723
  17.8 0.2 select_reduce_fusion.1
  18.0 0.1 select_reduce_fusion.3
  18.1 0.1 pad_add_fusion.3
  18.2 0.7 dynamic_slice.25.rows
  18.9 4.0 %shard_map.101 = (bf16[208,2048]{1,0:T(8,128)(2,1)}, bf16[208,2048]{1,0:T(8,128)(2,1)}, bf16[208,2048]{1,0:T(8,128)(2,1)}, bf16[208,2048]{1,0:T(8,128)(2,1)}) custom-call(s32[4]{0:T(128)} %dynamic_slice.25.rows, bf16[8,128,2048]{2,1,0:T(8,128)(2,1)} %down_ref.1, bf16[8,64,2048]{2,1,0:T(8,128)(2,1)} %upq_ref.1, bf16[8,64,512]{2,1,0:T(8,128)(2,1)} %upkv_ref.1), custom_call_target="tpu_custom_call" | custom-call | tf_op jit(solution)/shard_map/pallas_call | solution.py:106
  23.0 0.1 convert_reduce_fusion
  23.2 0.2 select_reduce_fusion.2
  23.4 0.1 compare_convert_fusion.refs_16_.refs_9_
  23.5 0.2 select_reduce_fusion
  23.8 0.6 constant_dynamic-slice_fusion.2.member_ref
  24.5 0.6 pad_add_fusion.info
  25.1 0.6 pad_add_fusion.1.info
  25.7 1.0 fusion
  26.7 3.0 %collective-permute-start.2 = (bf16[128,2048]{1,0:T(8,128)(2,1)}, bf16[128,2048]{1,0:T(8,128)(2,1)}, u32[]{:S(2)}, u32[]{:S(2)}) collective-permute-start(bf16[128,2048]{1,0:T(8,128)(2,1)} %get-tuple-element.46), channel_id=1, source_target_pairs={{0,4},{4,8},{8,12},{1,5},{5,9},{9,13},{2,6},{6,10},{10,14},{3,7},{... | collective-permute-start | bytes 1572872 | tf_op jit(solution)/shard_map/ppermute | solution.py:723
  29.7 1.3 collective-permute-start.5
  31.0 0.6 pad_add_fusion.5.info
  31.6 0.9 copy.12.idc_ref
  32.5 1.0 broadcast_select_fusion.3
  33.5 0.7 constant_dynamic-slice_fusion.cos_ref
  34.1 0.6 constant_dynamic-slice_fusion.4.sin_ref
  34.8 0.8 fusion.1
  35.5 2.3 %collective-permute-start.12 = (bf16[208,2048]{1,0:T(8,128)(2,1)}, bf16[208,2048]{1,0:T(8,128)(2,1)S(1)}, u32[]{:S(2)}, u32[]{:S(2)}) collective-permute-start(bf16[208,2048]{1,0:T(8,128)(2,1)} %get-tuple-element.64), channel_id=1, source_target_pairs={{0,2},{1,3},{2,0},{3,1},{4,6},{5,7},{6,4},{7,5},{8,10},{9,11},{10,... | collective-permute-start | bytes 2555912 | tf_op jit(solution)/shard_map/ppermute | solution.py:760
  37.9 16.2 %collective-permute-done.2.refs_2_.refs_4_ = bf16[128,2048]{1,0:T(8,128)(2,1)} collective-permute-done((bf16[128,2048]{1,0:T(8,128)(2,1)}, bf16[128,2048]{1,0:T(8,128)(2,1)}, u32[]{:S(2)}, u32[]{:S(2)}) %collective-permute-start.2) | collective-permute-done | bytes 524320 | tf_op jit(solution)/shard_map/ppermute | solution.py:723
  54.1 1.3 collective-permute-start.6
  55.4 0.7 collective-permute-start.7
  56.2 1.3 collective-permute-start.8
  57.5 0.7 collective-permute-start.9
  58.2 23.6 %shard_map.100 = (f32[384,2048]{1,0:T(8,128)}, f32[384,512]{1,0:T(8,128)}) custom-call(s32[7]{0:T(128)} %constant.147.info, bf16[128,8192]{1,0:T(8,128)(2,1)} %refs_0_.3, bf16[128,2048]{1,0:T(8,128)(2,1)} %copy-done.15, bf16[128,2048]{1,0:T(8,128)(2,1)} %collective-permute-done.2.refs_2_.refs_4_, bf16[128,4096]{1,0:T(8,128)(2,1)} %collective-permute-done.3.refs_3_.refs_2_, ...), custom_call_target="tpu_custom_call" | custom-call | flops 16106127360 | bytes 48234496 | tf_op jit(solution)/shard_map/pallas_call | solution.py:206
  81.8 10.4 %collective-permute-done.8.refs_7_.refs_0_ = bf16[128,2048]{1,0:T(8,128)(2,1)S(1)} collective-permute-done((bf16[128,2048]{1,0:T(8,128)(2,1)S(1)}, bf16[128,2048]{1,0:T(8,128)(2,1)S(1)}, u32[]{:S(2)}, u32[]{:S(2)}) %collective-permute-start.8) | collective-permute-done | bytes 524320 | tf_op jit(solution)/shard_map/ppermute | solution.py:720
  92.3 1.3 collective-permute-start.10
  93.7 1.3 collective-permute-start.14
  95.0 1.5 collective-permute-start.15
  96.5 1.1 broadcast_select_fusion
  97.6 11.9 %collective-permute-done.10.refs_11_.refs_2_ = bf16[128,2048]{1,0:T(8,128)(2,1)S(1)} collective-permute-done((bf16[128,2048]{1,0:T(8,128)(2,1)S(1)}, bf16[128,2048]{1,0:T(8,128)(2,1)S(1)}, u32[]{:S(2)}, u32[]{:S(2)}) %collective-permute-start.10) | collective-permute-done | bytes 524320 | tf_op jit(solution)/shard_map/ppermute | solution.py:710
  109.5 1.3 collective-permute-start.20
  110.8 0.6 concatenate.22.info
  111.4 7.7 %shard_map.102 = bf16[512,128]{1,0:T(8,128)(2,1)} custom-call(s32[25]{0:T(128)} %concatenate.22.info, bf16[128,8192]{1,0:T(8,128)(2,1)} %refs_0_.3, bf16[128,2048]{1,0:T(8,128)(2,1)} %copy-done.15, bf16[128,4096]{1,0:T(8,128)(2,1)} %collective-permute-done.3.refs_3_.refs_2_, bf16[128,2048]{1,0:T(8,128)(2,1)} %collective-permute-done.5.refs_5_.refs_3_, ...), custom_call_target="tpu_custom_call" | custom-call | flops 1073741824 | bytes 4194304 | tf_op jit(solution)/shard_map/pallas_call | solution.py:298
  119.1 4.2 %collective-permute-start.18 = (bf16[512,128]{1,0:T(8,128)(2,1)}, bf16[512,128]{1,0:T(8,128)(2,1)S(1)}, u32[]{:S(2)}, u32[]{:S(2)}) collective-permute-start(bf16[512,128]{1,0:T(8,128)(2,1)} %shard_map.102), channel_id=1, source_target_pairs={{0,12},{4,0},{8,4},{12,8},{1,13},{5,1},{9,5},{13,9},{2,14},{6,2},{... | collective-permute-start | bytes 393224 | tf_op jit(solution)/shard_map/ppermute | solution.py:848
  123.4 1.5 collective-permute-start.17
  124.8 0.7 concatenate.24.info
  125.5 1.9 collective-permute-start.16
  127.4 1.1 broadcast_select_fusion.1
  128.6 1.6 collective-permute-start.19
  130.2 17.6 %shard_map.103 = (f32[256,2048]{1,0:T(8,128)}, f32[256,512]{1,0:T(8,128)}) custom-call(s32[6]{0:T(128)} %concatenate.24.info, bf16[128,2048]{1,0:T(8,128)(2,1)} %copy-done.3, bf16[128,2048]{1,0:T(8,128)(2,1)} %copy-done.4, bf16[128,2048]{1,0:T(8,128)(2,1)} %copy-done.9, bf16[128,4096]{1,0:T(8,128)(2,1)} %copy-done, bf16[128,4096]{1,0:T(8,128)(2,1)} %copy-done.1, ...), custom_call_target="tpu_custom_call" | custom-call | flops 10737418240 | bytes 46137344 | tf_op jit(solution)/shard_map/pallas_call | solution.py:206
  147.8 3.8 %collective-permute-done.18 = bf16[512,128]{1,0:T(8,128)(2,1)S(1)} collective-permute-done((bf16[512,128]{1,0:T(8,128)(2,1)}, bf16[512,128]{1,0:T(8,128)(2,1)S(1)}, u32[]{:S(2)}, u32[]{:S(2)}) %collective-permute-start.18) | collective-permute-done | bytes 131104 | tf_op jit(solution)/shard_map/ppermute | solution.py:848
  151.6 0.7 add_convert_fusion.refs_8_
  152.4 8.8 %shard_map.104 = (bf16[512,2048]{1,0:T(8,128)(2,1)}, bf16[512,256]{1,0:T(8,128)(2,1)}, bf16[512,256]{1,0:T(8,128)(2,1)}, bf16[256,2048]{1,0:T(8,128)(2,1)}, bf16[256,512]{1,0:T(8,128)(2,1)}) custom-call(s32[3]{0:T(128)} %pad_add_fusion.1.info, f32[384,2048]{1,0:T(8,128)} %get-tuple-element.50.refs_0_, f32[384,512]{1,0:T(8,128)} %get-tuple-element.51.refs_1_, ...), custom_call_target="tpu_custom_call" | custom-call | flops 671088640 | bytes 10485760 | tf_op jit(solution)/shard_map/pallas_call | solution.py:432
  161.2 0.5 collective-permute-start.21
  161.7 0.7 pad_add_fusion.4.info
  162.4 0.7 fusion.9
  163.1 1.0 copy-done.12
  164.1 11.3 %shard_map.105 = (f32[128,2048]{1,0:T(8,128)}, f32[128,512]{1,0:T(8,128)}) custom-call(s32[3]{0:T(128)} %pad_add_fusion.4.info, bf16[128,4096]{1,0:T(8,128)(2,1)} %copy-done.12, bf16[8192,2048]{1,0:T(8,128)(2,1)} %weight_ref.2, bf16[8192,512]{1,0:T(8,128)(2,1)} %weight_ref.3, f32[256,2048]{1,0:T(8,128)} %get-tuple-element.70.refs_2_.refs_3_, ...), custom_call_target="tpu_custom_call" | custom-call | flops 2684354560 | bytes 22020096 | tf_op jit(solution)/shard_map/pallas_call | solution.py:206
  175.4 0.8 copy-done.8
  176.2 3.9 %shard_map.107 = (bf16[128,256]{1,0:T(8,128)(2,1)}, bf16[128,256]{1,0:T(8,128)(2,1)}) custom-call(s32[3]{0:T(128)} %pad_add_fusion.5.info, bf16[128,2048]{1,0:T(8,128)(2,1)} %copy-done.8, bf16[8192,512]{1,0:T(8,128)(2,1)} %weight_ref.3, f32[128,512]{1,0:T(8,128)} %get-tuple-element.78.sum_ref, bf16[128,64]{1,0:T(8,128)(2,1)} %get-tuple-element.89.low_ref, ...), custom_call_target="tpu_custom_call" | custom-call | flops 301989888 | bytes 2097152 | tf_op jit(solution)/shard_map/pallas_call | solution.py:517
  180.1 3.4 %collective-permute-start.22 = (bf16[128,256]{1,0:T(8,128)(2,1)}, bf16[128,256]{1,0:T(8,128)(2,1)S(1)}, u32[]{:S(2)}, u32[]{:S(2)}) collective-permute-start(bf16[128,256]{1,0:T(8,128)(2,1)} %get-tuple-element.82), channel_id=1, source_target_pairs={{0,4},{12,8},{1,5},{13,9},{2,6},{14,10},{3,7},{15,11},{16,20},{28,... | collective-permute-start | bytes 196616 | tf_op jit(solution)/shard_map/ppermute | solution.py:909
  183.5 6.0 %shard_map.106.ql_ref = bf16[128,2048]{1,0:T(8,128)(2,1)} custom-call(s32[1]{0:T(128)} %bitcast.11.info, bf16[128,2048]{1,0:T(8,128)(2,1)} %copy-done.8, bf16[8192,2048]{1,0:T(8,128)(2,1)} %weight_ref.2, f32[128,2048]{1,0:T(8,128)} %get-tuple-element.76.sum_ref, bf16[128,64]{1,0:T(8,128)(2,1)} %get-tuple-element.90.low_ref, ...), custom_call_target="tpu_custom_call" | custom-call | flops 1207959552 | bytes 8388608 | tf_op jit(solution)/shard_map/pallas_call | solution.py:517
  189.5 0.7 copy-done.20
  190.2 8.0 %shard_map.108 = bf16[512,2048]{1,0:T(8,128)(2,1)} custom-call(s32[3]{0:T(128)} %pad_add_fusion.info, bf16[512,2048]{1,0:T(8,128)(2,1)} %get-tuple-element.72.q_ref, bf16[128,2048]{1,0:T(8,128)(2,1)} %shard_map.106.ql_ref, bf16[512,256]{1,0:T(8,128)(2,1)} %get-tuple-element.74.m_ref, bf16[128,256]{1,0:T(8,128)(2,1)} %get-tuple-element.80.ml_ref, ...), custom_call_target="tpu_custom_call" | custom-call | flops 2147483648 | bytes 4194304 | tf_op jit(solution)/shard_map/pallas_call | solution.py:616
  (69 shorter events, 0.5 us)
Async XLA Ops:
  0.0 9.9 %copy-start.2 = (bf16[128,8192]{1,0:T(8,128)(2,1)S(1)}, bf16[128,8192]{1,0:T(8,128)(2,1)}, u32[]{:S(2)}) copy-start(bf16[128,8192]{1,0:T(8,128)(2,1)} %refs_0_.3) | copy-start | bytes 6291460
  0.0 17.8 %copy-start.19 = (s32[32]{0:T(128)S(1)}, s32[32]{0:T(128)}, u32[]{:S(2)}) copy-start(s32[32]{0:T(128)} %param.16) | copy-start | bytes 388
  0.0 17.8 %copy-start.18 = (s32[4,4]{1,0:T(4,128)S(1)}, s32[4,4]{1,0:T(4,128)}, u32[]{:S(2)}) copy-start(s32[4,4]{1,0:T(4,128)} %param.17) | copy-start | bytes 196
  2.2 24.4 %collective-permute-start = (bf16[128,2048]{1,0:T(8,128)(2,1)}, bf16[128,2048]{1,0:T(8,128)(2,1)S(1)}, u32[]{:S(2)}, u32[]{:S(2)}) collective-permute-start(bf16[128,2048]{1,0:T(8,128)(2,1)} %get-tuple-element.46), channel_id=1, source_target_pairs={{4,0},{8,4},{12,8},{5,1},{9,5},{13,9},{6,2},{10,6},{14,10},{7,3},{... | collective-permute-start | bytes 1572872 | tf_op jit(solution)/shard_map/ppermute | solution.py:720
  3.5 23.2 %collective-permute-start.1 = (bf16[128,2048]{1,0:T(8,128)(2,1)S(1)}, bf16[128,2048]{1,0:T(8,128)(2,1)}, u32[]{:S(2)}, u32[]{:S(2)}) collective-permute-start(bf16[128,2048]{1,0:T(8,128)(2,1)S(1)} %get-tuple-element.49), channel_id=1, source_target_pairs={{0,4},{4,8},{8,12},{1,5},{5,9},{9,13},{2,6},{6,10},{10,14},{3,7},{... | collective-permute-start | bytes 1572872 | tf_op jit(solution)/shard_map/ppermute | solution.py:723
  10.9 43.1 %collective-permute-start.3 = (bf16[128,4096]{1,0:T(8,128)(2,1)}, bf16[128,4096]{1,0:T(8,128)(2,1)}, u32[]{:S(2)}, u32[]{:S(2)}) collective-permute-start(bf16[128,4096]{1,0:T(8,128)(2,1)} %slice.20), channel_id=1, source_target_pairs={{4,0},{8,4},{12,8},{5,1},{9,5},{13,9},{6,2},{10,6},{14,10},{7,3},{... | collective-permute-start | bytes 3145736 | tf_op jit(solution)/shard_map/ppermute | solution.py:720
  12.2 41.9 %collective-permute-start.4 = (bf16[128,4096]{1,0:T(8,128)(2,1)}, bf16[128,4096]{1,0:T(8,128)(2,1)}, u32[]{:S(2)}, u32[]{:S(2)}) collective-permute-start(bf16[128,4096]{1,0:T(8,128)(2,1)} %slice.20), channel_id=1, source_target_pairs={{0,4},{4,8},{8,12},{1,5},{5,9},{9,13},{2,6},{6,10},{10,14},{3,7},{... | collective-permute-start | bytes 3145736 | tf_op jit(solution)/shard_map/ppermute | solution.py:723
  18.9 4.1 %copy-start.17 = (s32[1,512]{1,0:T(1,128)S(1)}, s32[1,512]{1,0:T(1,128)}, u32[]{:S(2)}) copy-start(s32[1,512]{1,0:T(1,128)} %idr_ref.1) | copy-start | bytes 6148
  22.9 12.6 %collective-permute-start.11 = (bf16[208,2048]{1,0:T(8,128)(2,1)}, bf16[208,2048]{1,0:T(8,128)(2,1)S(1)}, u32[]{:S(2)}, u32[]{:S(2)}) collective-permute-start(bf16[208,2048]{1,0:T(8,128)(2,1)} %get-tuple-element.62), channel_id=1, source_target_pairs={{0,1},{1,2},{2,3},{3,0},{4,5},{5,6},{6,7},{7,4},{8,9},{9,10},{10,1... | collective-permute-start | bytes 2555912 | tf_op jit(solution)/shard_map/ppermute | solution.py:760
  23.5 12.0 %copy-start.7 = (f32[512,4]{1,0:T(8,128)}, f32[512,4]{1,0:T(8,128)S(1)}, u32[]{:S(2)}) copy-start(f32[512,4]{1,0:T(8,128)S(1)} %compare_convert_fusion.refs_16_.refs_9_) | copy-start | bytes 24580
  26.7 5.8 %copy-start.15 = (bf16[128,2048]{1,0:T(8,128)(2,1)}, bf16[128,2048]{1,0:T(8,128)(2,1)S(1)}, u32[]{:S(2)}) copy-start(bf16[128,2048]{1,0:T(8,128)(2,1)S(1)} %collective-permute-done.refs_1_) | copy-start | bytes 1572868
  26.7 27.4 %collective-permute-start.2 = (bf16[128,2048]{1,0:T(8,128)(2,1)}, bf16[128,2048]{1,0:T(8,128)(2,1)}, u32[]{:S(2)}, u32[]{:S(2)}) collective-permute-start(bf16[128,2048]{1,0:T(8,128)(2,1)} %get-tuple-element.46), channel_id=1, source_target_pairs={{0,4},{4,8},{8,12},{1,5},{5,9},{9,13},{2,6},{6,10},{10,14},{3,7},{... | collective-permute-start | bytes 1572872 | tf_op jit(solution)/shard_map/ppermute | solution.py:723
  29.7 24.4 %collective-permute-start.5 = (bf16[128,2048]{1,0:T(8,128)(2,1)S(1)}, bf16[128,2048]{1,0:T(8,128)(2,1)}, u32[]{:S(2)}, u32[]{:S(2)}) collective-permute-start(bf16[128,2048]{1,0:T(8,128)(2,1)S(1)} %get-tuple-element.49), channel_id=1, source_target_pairs={{4,0},{8,4},{12,8},{5,1},{9,5},{13,9},{6,2},{10,6},{14,10},{7,3},{... | collective-permute-start | bytes 1572872 | tf_op jit(solution)/shard_map/ppermute | solution.py:720
  32.5 23.7 %copy-start.16 = (bf16[128,2048]{1,0:T(8,128)(2,1)S(1)}, bf16[128,2048]{1,0:T(8,128)(2,1)}, u32[]{:S(2)}) copy-start(bf16[128,2048]{1,0:T(8,128)(2,1)} %copy-done.15) | copy-start | bytes 1572868
  33.5 20.6 %copy-start.10 = (f32[512,128]{1,0:T(8,128)}, f32[512,128]{1,0:T(8,128)S(1)}, u32[]{:S(2)}) copy-start(f32[512,128]{1,0:T(8,128)S(1)} %get-tuple-element.83.refs_13_) | copy-start | bytes 786436
  33.5 20.6 %copy-start.11 = (f32[512,128]{1,0:T(8,128)}, f32[512,128]{1,0:T(8,128)S(1)}, u32[]{:S(2)}) copy-start(f32[512,128]{1,0:T(8,128)S(1)} %get-tuple-element.95.refs_12_) | copy-start | bytes 786436
  35.5 18.6 %copy-start.5 = (bf16[208,2048]{1,0:T(8,128)(2,1)}, bf16[208,2048]{1,0:T(8,128)(2,1)S(1)}, u32[]{:S(2)}) copy-start(bf16[208,2048]{1,0:T(8,128)(2,1)S(1)} %collective-permute-done.11.refs_13_.refs_5_) | copy-start | bytes 2555908
  35.5 58.1 %collective-permute-start.12 = (bf16[208,2048]{1,0:T(8,128)(2,1)}, bf16[208,2048]{1,0:T(8,128)(2,1)S(1)}, u32[]{:S(2)}, u32[]{:S(2)}) collective-permute-start(bf16[208,2048]{1,0:T(8,128)(2,1)} %get-tuple-element.64), channel_id=1, source_target_pairs={{0,2},{1,3},{2,0},{3,1},{4,6},{5,7},{6,4},{7,5},{8,10},{9,11},{10,... | collective-permute-start | bytes 2555912 | tf_op jit(solution)/shard_map/ppermute | solution.py:760
  54.1 39.6 %collective-permute-start.6 = (bf16[128,4096]{1,0:T(8,128)(2,1)}, bf16[128,4096]{1,0:T(8,128)(2,1)S(1)}, u32[]{:S(2)}, u32[]{:S(2)}) collective-permute-start(bf16[128,4096]{1,0:T(8,128)(2,1)} %collective-permute-done.3.refs_3_.refs_2_), channel_id=1, source_target_pairs={{4,0},{8,4},{5,1},{9,5},{6,2},{10,6},{7,3},{11,7},{20,16},{24,20},... | collective-permute-start | bytes 3145736 | tf_op jit(solution)/shard_map/ppermute | solution.py:720
  55.4 38.3 %collective-permute-start.7 = (bf16[128,4096]{1,0:T(8,128)(2,1)}, bf16[128,4096]{1,0:T(8,128)(2,1)S(1)}, u32[]{:S(2)}, u32[]{:S(2)}) collective-permute-start(bf16[128,4096]{1,0:T(8,128)(2,1)} %collective-permute-done.4.refs_4_.refs_5_), channel_id=1, source_target_pairs={{4,8},{8,12},{5,9},{9,13},{6,10},{10,14},{7,11},{11,15},{20,24},{2... | collective-permute-start | bytes 3145736 | tf_op jit(solution)/shard_map/ppermute | solution.py:723
  56.2 36.1 %collective-permute-start.8 = (bf16[128,2048]{1,0:T(8,128)(2,1)S(1)}, bf16[128,2048]{1,0:T(8,128)(2,1)S(1)}, u32[]{:S(2)}, u32[]{:S(2)}) collective-permute-start(bf16[128,2048]{1,0:T(8,128)(2,1)S(1)} %copy-done.16), channel_id=1, source_target_pairs={{4,0},{8,4},{5,1},{9,5},{6,2},{10,6},{7,3},{11,7},{20,16},{24,20},... | collective-permute-start | bytes 1572872 | tf_op jit(solution)/shard_map/ppermute | solution.py:720
  57.5 34.8 %collective-permute-start.9 = (bf16[128,2048]{1,0:T(8,128)(2,1)}, bf16[128,2048]{1,0:T(8,128)(2,1)S(1)}, u32[]{:S(2)}, u32[]{:S(2)}) collective-permute-start(bf16[128,2048]{1,0:T(8,128)(2,1)} %collective-permute-done.1.refs_6_), channel_id=1, source_target_pairs={{4,8},{8,12},{5,9},{9,13},{6,10},{10,14},{7,11},{11,15},{20,24},{2... | collective-permute-start | bytes 1572872 | tf_op jit(solution)/shard_map/ppermute | solution.py:723
  92.2 5.4 %copy-start.3 = (bf16[128,2048]{1,0:T(8,128)(2,1)}, bf16[128,2048]{1,0:T(8,128)(2,1)S(1)}, u32[]{:S(2)}) copy-start(bf16[128,2048]{1,0:T(8,128)(2,1)S(1)} %collective-permute-done.8.refs_7_.refs_0_) | copy-start | bytes 1572868
  92.2 5.4 %copy-start.4 = (bf16[128,2048]{1,0:T(8,128)(2,1)}, bf16[128,2048]{1,0:T(8,128)(2,1)S(1)}, u32[]{:S(2)}) copy-start(bf16[128,2048]{1,0:T(8,128)(2,1)S(1)} %collective-permute-done.9.refs_10_.refs_1_) | copy-start | bytes 1572868
  92.3 17.2 %collective-permute-start.10 = (bf16[128,2048]{1,0:T(8,128)(2,1)S(1)}, bf16[128,2048]{1,0:T(8,128)(2,1)S(1)}, u32[]{:S(2)}, u32[]{:S(2)}) collective-permute-start(bf16[128,2048]{1,0:T(8,128)(2,1)S(1)} %broadcast_select_fusion.2), channel_id=1, source_target_pairs={{4,0},{8,12},{5,1},{9,13},{6,2},{10,14},{7,3},{11,15},{20,16},{24,... | collective-permute-start | bytes 1572872 | tf_op jit(solution)/shard_map/ppermute | solution.py:710
  93.6 15.9 %copy-start.6 = (bf16[208,2048]{1,0:T(8,128)(2,1)}, bf16[208,2048]{1,0:T(8,128)(2,1)S(1)}, u32[]{:S(2)}) copy-start(bf16[208,2048]{1,0:T(8,128)(2,1)S(1)} %collective-permute-done.12.refs_14_.refs_6_) | copy-start | bytes 2555908
  93.6 17.8 %collective-permute-start.13 = (bf16[208,2048]{1,0:T(8,128)(2,1)}, bf16[208,2048]{1,0:T(8,128)(2,1)}, u32[]{:S(2)}, u32[]{:S(2)}) collective-permute-start(bf16[208,2048]{1,0:T(8,128)(2,1)} %get-tuple-element.66), channel_id=1, source_target_pairs={{0,3},{1,0},{2,1},{3,2},{4,7},{5,4},{6,5},{7,6},{8,11},{9,8},{10,9... | collective-permute-start | bytes 2555912 | tf_op jit(solution)/shard_map/ppermute | solution.py:760
  93.7 17.7 %copy-start = (bf16[128,4096]{1,0:T(8,128)(2,1)}, bf16[128,4096]{1,0:T(8,128)(2,1)S(1)}, u32[]{:S(2)}) copy-start(bf16[128,4096]{1,0:T(8,128)(2,1)S(1)} %collective-permute-done.6.refs_8_.refs_3_) | copy-start | bytes 3145732
  93.7 17.7 %copy-start.1 = (bf16[128,4096]{1,0:T(8,128)(2,1)}, bf16[128,4096]{1,0:T(8,128)(2,1)S(1)}, u32[]{:S(2)}) copy-start(bf16[128,4096]{1,0:T(8,128)(2,1)S(1)} %collective-permute-done.7.refs_9_.refs_4_) | copy-start | bytes 3145732
  93.7 31.8 %collective-permute-start.14 = (bf16[128,2048]{1,0:T(8,128)(2,1)}, bf16[128,2048]{1,0:T(8,128)(2,1)}, u32[]{:S(2)}, u32[]{:S(2)}) collective-permute-start(bf16[128,2048]{1,0:T(8,128)(2,1)} %collective-permute-done.5.refs_5_.refs_3_), channel_id=1, source_target_pairs={{4,0},{8,4},{5,1},{9,5},{6,2},{10,6},{7,3},{11,7},{20,16},{24,20},... | collective-permute-start | bytes 1572872 | tf_op jit(solution)/shard_map/ppermute | solution.py:720
  95.0 32.4 %collective-permute-start.15 = (bf16[128,2048]{1,0:T(8,128)(2,1)}, bf16[128,2048]{1,0:T(8,128)(2,1)}, u32[]{:S(2)}, u32[]{:S(2)}) collective-permute-start(bf16[128,2048]{1,0:T(8,128)(2,1)} %collective-permute-done.2.refs_2_.refs_4_), channel_id=1, source_target_pairs={{4,8},{8,12},{5,9},{9,13},{6,10},{10,14},{7,11},{11,15},{20,24},{2... | collective-permute-start | bytes 1572872 | tf_op jit(solution)/shard_map/ppermute | solution.py:723
  109.5 1.3 copy-start.9
  109.5 53.6 %collective-permute-start.20 = (bf16[128,4096]{1,0:T(8,128)(2,1)}, bf16[128,4096]{1,0:T(8,128)(2,1)S(1)}, u32[]{:S(2)}, u32[]{:S(2)}) collective-permute-start(bf16[128,4096]{1,0:T(8,128)(2,1)} %broadcast_select_fusion), channel_id=1, source_target_pairs={{4,0},{8,12},{5,1},{9,13},{6,2},{10,14},{7,3},{11,15},{20,16},{24,... | collective-permute-start | bytes 3145736 | tf_op jit(solution)/shard_map/ppermute | solution.py:710
  119.1 32.5 %collective-permute-start.18 = (bf16[512,128]{1,0:T(8,128)(2,1)}, bf16[512,128]{1,0:T(8,128)(2,1)S(1)}, u32[]{:S(2)}, u32[]{:S(2)}) collective-permute-start(bf16[512,128]{1,0:T(8,128)(2,1)} %shard_map.102), channel_id=1, source_target_pairs={{0,12},{4,0},{8,4},{12,8},{1,13},{5,1},{9,5},{13,9},{2,14},{6,2},{... | collective-permute-start | bytes 393224 | tf_op jit(solution)/shard_map/ppermute | solution.py:848
  123.4 28.3 %collective-permute-start.17 = (bf16[512,128]{1,0:T(8,128)(2,1)}, bf16[512,128]{1,0:T(8,128)(2,1)S(1)}, u32[]{:S(2)}, u32[]{:S(2)}) collective-permute-start(bf16[512,128]{1,0:T(8,128)(2,1)} %shard_map.102), channel_id=1, source_target_pairs={{0,8},{4,12},{8,0},{12,4},{1,9},{5,13},{9,1},{13,5},{2,10},{6,14},... | collective-permute-start | bytes 393224 | tf_op jit(solution)/shard_map/ppermute | solution.py:848
  125.5 26.1 %collective-permute-start.16 = (bf16[512,128]{1,0:T(8,128)(2,1)}, bf16[512,128]{1,0:T(8,128)(2,1)S(1)}, u32[]{:S(2)}, u32[]{:S(2)}) collective-permute-start(bf16[512,128]{1,0:T(8,128)(2,1)} %shard_map.102), channel_id=1, source_target_pairs={{0,4},{4,8},{8,12},{12,0},{1,5},{5,9},{9,13},{13,1},{2,6},{6,10},{... | collective-permute-start | bytes 393224 | tf_op jit(solution)/shard_map/ppermute | solution.py:848
  128.5 23.1 %copy-start.14 = (bf16[512,128]{1,0:T(8,128)(2,1)S(1)}, bf16[512,128]{1,0:T(8,128)(2,1)}, u32[]{:S(2)}) copy-start(bf16[512,128]{1,0:T(8,128)(2,1)} %shard_map.102) | copy-start | bytes 393220
  128.6 46.9 %collective-permute-start.19 = (bf16[128,2048]{1,0:T(8,128)(2,1)S(1)}, bf16[128,2048]{1,0:T(8,128)(2,1)S(1)}, u32[]{:S(2)}, u32[]{:S(2)}) collective-permute-start(bf16[128,2048]{1,0:T(8,128)(2,1)S(1)} %broadcast_select_fusion.1), channel_id=1, source_target_pairs={{4,0},{8,12},{5,1},{9,13},{6,2},{10,14},{7,3},{11,15},{20,16},{24,... | collective-permute-start | bytes 1572872 | tf_op jit(solution)/shard_map/ppermute | solution.py:710
  152.4 10.0 %copy-start.13 = (bf16[512,128]{1,0:T(8,128)(2,1)S(1)}, bf16[512,128]{1,0:T(8,128)(2,1)}, u32[]{:S(2)}) copy-start(bf16[512,128]{1,0:T(8,128)(2,1)} %add_convert_fusion.refs_8_) | copy-start | bytes 393220
  161.2 28.3 %collective-permute-start.21 = (bf16[512,256]{1,0:T(8,128)(2,1)}, bf16[512,256]{1,0:T(8,128)(2,1)S(1)}, u32[]{:S(2)}, u32[]{:S(2)}) collective-permute-start(bf16[512,256]{1,0:T(8,128)(2,1)} %get-tuple-element.81), channel_id=1, source_target_pairs={{0,4},{4,0},{8,12},{12,8},{1,5},{5,1},{9,13},{13,9},{2,6},{6,2},{1... | collective-permute-start | bytes 786440 | tf_op jit(solution)/shard_map/ppermute | solution.py:881
  163.1 1.0 copy-start.12
  175.4 0.8 copy-start.8
  180.1 9.4 %collective-permute-start.22 = (bf16[128,256]{1,0:T(8,128)(2,1)}, bf16[128,256]{1,0:T(8,128)(2,1)S(1)}, u32[]{:S(2)}, u32[]{:S(2)}) collective-permute-start(bf16[128,256]{1,0:T(8,128)(2,1)} %get-tuple-element.82), channel_id=1, source_target_pairs={{0,4},{12,8},{1,5},{13,9},{2,6},{14,10},{3,7},{15,11},{16,20},{28,... | collective-permute-start | bytes 196616 | tf_op jit(solution)/shard_map/ppermute | solution.py:909
  189.5 0.7 copy-start.20
  189.5 0.7 copy-start.21
